TPU v7x, 32 devices: a whole 2x2x4 slice. The times are simulated.
32 devices in a mesh: fsdp: 16 (over z, y, core), tp: 2 (over x).
Axes of the slice: x: 2, y: 2, z: 4, core: 2. Of those that a mesh axis runs over, the one named last changes fastest.
Arguments:
- entering_states: bfloat16 [35328, 1024], P(('fsdp', 'tp')), may hold values from -6 to 6
- bypass_states: bfloat16 [35328, 1024], P(('fsdp', 'tp')), may hold values from -6 to 6
- mentor_states: bfloat16 [35328, 1024], P(('fsdp', 'tp')), may hold values from -18 to 18
- occupancy_mask: int32 [32], P('fsdp'), may hold values from 0 to 1, as said below
- bypass_merge_matrix: bfloat16 [2048, 1024], P(('fsdp', 'tp')), may hold values from -0.125 to 0.125
- bypass_merge_offset: bfloat16 [1024], P(('fsdp', 'tp')), may hold values from -1.5 to 1.5
- mixer_layernorm_scale: bfloat16 [1024], P(('fsdp', 'tp')), may hold values from 0.25 to 1.75
- mixer_layernorm_offset: bfloat16 [1024], P(('fsdp', 'tp')), may hold values from -1.5 to 1.5
- asking_map_matrix: bfloat16 [1024, 1024], P('fsdp', 'tp'), may hold values from -0.3125 to 0.3125
- lookup_map_matrix: bfloat16 [1024, 1024], P('fsdp', 'tp'), may hold values from -0.3125 to 0.3125
- content_map_matrix: bfloat16 [1024, 1024], P('fsdp', 'tp'), may hold values from -0.1875 to 0.1875
- mixer_result_matrix: bfloat16 [1024, 1024], P('tp', 'fsdp'), may hold values from -0.25 to 0.25
- mixer_result_offset: bfloat16 [1024], P(('fsdp', 'tp')), may hold values from -1.5 to 1.5
- perceptron_layernorm_scale: bfloat16 [1024], P(('fsdp', 'tp')), may hold values from 0.25 to 1.75
- perceptron_layernorm_offset: bfloat16 [1024], P(('fsdp', 'tp')), may hold values from -1.5 to 1.5
- expand_layer_matrix: bfloat16 [1024, 4096], P('fsdp', 'tp'), may hold values from -0.1875 to 0.1875
- expand_layer_offset: bfloat16 [4096], P(('fsdp', 'tp')), may hold values from -1.5 to 1.5
- contract_layer_matrix: bfloat16 [4096, 1024], P('tp', 'fsdp'), may hold values from -0.09375 to 0.09375
- contract_layer_offset: bfloat16 [1024], P(('fsdp', 'tp')), may hold values from -1.5 to 1.5
Outputs:
- block_out: bfloat16 [35328, 1024], P(('fsdp', 'tp'))
- loss_value: float32 [], replicated
- grad_tokens: float32 [35328, 1024], P(('fsdp', 'tp'))
- grad_shortcut: float32 [35328, 1024], P(('fsdp', 'tp'))
- grad_merge_weight: float32 [2048, 1024], P(('fsdp', 'tp'))
- grad_merge_bias: float32 [1024], P(('fsdp', 'tp'))
- grad_first_gain: float32 [1024], P(('fsdp', 'tp'))
- grad_first_shift: float32 [1024], P(('fsdp', 'tp'))
- grad_query_weight: float32 [1024, 1024], P('fsdp', 'tp')
- grad_key_weight: float32 [1024, 1024], P('fsdp', 'tp')
- grad_value_weight: float32 [1024, 1024], P('fsdp', 'tp')
- grad_output_weight: float32 [1024, 1024], P('tp', 'fsdp')
- grad_output_bias: float32 [1024], P(('fsdp', 'tp'))
- grad_second_gain: float32 [1024], P(('fsdp', 'tp'))
- grad_second_shift: float32 [1024], P(('fsdp', 'tp'))
- grad_hidden_weight: float32 [1024, 4096], P('fsdp', 'tp')
- grad_hidden_bias: float32 [4096], P(('fsdp', 'tp'))
- grad_down_weight: float32 [4096, 1024], P('tp', 'fsdp')
- grad_down_bias: float32 [1024], P(('fsdp', 'tp'))
Inputs may be any that keep to these rules, and one draw needn't show every extreme that they name: `occupancy_mask`: in each group of 2 slots (the slots of one index of fsdp) the live slots come first and at least one is live; in every draw some group has all 2 slots live.
All inputs are finite; a program needn't handle non-finite values.
Results may differ from a plain program's by a relative error of at most 0.015.
Values may be sent and summed in bfloat16 or wider, within the bound.
No kernel may reach another device: no remote copies, remote signals or barrier semaphores. Data moves between devices by JAX's collectives and lax.ppermute only.
A program may use at most 320 MiB of HBM per device.

v0:
```python
import functools
import math

import jax
import jax.numpy as jnp
from jax import lax
from jax.experimental import pallas as pl
from jax.experimental.pallas import tpu as pltpu
from jax.sharding import PartitionSpec as P

D = 1024
HEADS = 16
SEQ_LEN = 1104


EPSILON = 1e-05


def layer_norm(value, gain, shift):
    centred = value - jnp.mean(value, axis=-1, keepdims=True)
    spread = jnp.mean(centred * centred, axis=-1, keepdims=True)
    return centred * lax.rsqrt(spread + EPSILON) * gain + shift


def contract_rows(left, right):
    return lax.dot_general(
        left, right, (((0,), (0,)), ((), ())), preferred_element_type=jnp.float32
    )


def contract_cols(left, right):
    return lax.dot_general(
        left, right, (((1,), (1,)), ((), ())), preferred_element_type=jnp.float32
    )


def attend_forward(queries, keys_all, values):
    scale = float(queries.shape[-1]) ** (-0.5)
    scores = (
        jnp.einsum("qhd,khd->hqk", queries, keys_all, preferred_element_type=jnp.float32) * scale
    )
    peak_score = jnp.max(scores, axis=-1, keepdims=True)
    raised = jnp.exp(scores - peak_score)
    row_total = jnp.sum(raised, axis=-1, keepdims=True)
    weights_low = (raised / row_total).astype(jnp.bfloat16)
    output = jnp.einsum("hqk,khd->qhd", weights_low, values, preferred_element_type=jnp.float32)
    return (output.astype(jnp.bfloat16), peak_score + jnp.log(row_total))


def attend_backward(queries, keys_all, values, summary, upstream):
    scale = float(queries.shape[-1]) ** (-0.5)
    scores = (
        jnp.einsum("qhd,khd->hqk", queries, keys_all, preferred_element_type=jnp.float32) * scale
    )
    probs_full = jnp.exp(scores - summary)
    grad_probs = jnp.einsum("qhd,khd->hqk", upstream, values, preferred_element_type=jnp.float32)
    grad_values = jnp.einsum(
        "hqk,qhd->khd",
        probs_full.astype(jnp.bfloat16),
        upstream,
        preferred_element_type=jnp.float32,
    )
    centre = jnp.sum(probs_full * grad_probs, axis=-1, keepdims=True)
    grad_scores = (probs_full * (grad_probs - centre)).astype(jnp.bfloat16)
    grad_queries = (
        jnp.einsum("hqk,khd->qhd", grad_scores, keys_all, preferred_element_type=jnp.float32)
        * scale
    )
    grad_keys = (
        jnp.einsum("hqk,qhd->khd", grad_scores, queries, preferred_element_type=jnp.float32) * scale
    )
    return (
        grad_queries.astype(jnp.bfloat16),
        grad_keys.astype(jnp.bfloat16),
        grad_values.astype(jnp.bfloat16),
    )


def gelu_exact(value):
    return jax.nn.gelu(value, approximate=False)


def per_device_split(
    entering_states,
    bypass_states,
    mentor_states,
    occupancy_mask,
    bypass_merge_matrix,
    bypass_merge_offset,
    mixer_layernorm_scale,
    mixer_layernorm_offset,
    asking_map_matrix,
    lookup_map_matrix,
    content_map_matrix,
    mixer_result_matrix,
    mixer_result_offset,
    perceptron_layernorm_scale,
    perceptron_layernorm_offset,
    expand_layer_matrix,
    expand_layer_offset,
    contract_layer_matrix,
    contract_layer_offset,
):
    rows = entering_states.shape[0]
    width = D // HEADS
    position = lax.axis_index("tp")
    (
        merge_full,
        merge_add,
        gain_one,
        shift_one,
        output_add,
        gain_two,
        shift_two,
        hidden_add,
        down_add,
    ) = (
        lax.all_gather(bypass_merge_matrix, ("fsdp", "tp"), axis=0, tiled=True),
        lax.all_gather(bypass_merge_offset, ("fsdp", "tp"), axis=0, tiled=True),
        lax.all_gather(mixer_layernorm_scale, ("fsdp", "tp"), axis=0, tiled=True),
        lax.all_gather(mixer_layernorm_offset, ("fsdp", "tp"), axis=0, tiled=True),
        lax.all_gather(mixer_result_offset, ("fsdp", "tp"), axis=0, tiled=True),
        lax.all_gather(perceptron_layernorm_scale, ("fsdp", "tp"), axis=0, tiled=True),
        lax.all_gather(perceptron_layernorm_offset, ("fsdp", "tp"), axis=0, tiled=True),
        lax.all_gather(expand_layer_offset, ("fsdp", "tp"), axis=0, tiled=True),
        lax.all_gather(contract_layer_offset, ("fsdp", "tp"), axis=0, tiled=True),
    )
    query_full, key_full, value_full, output_full, hidden_full, down_full = (
        lax.all_gather(asking_map_matrix, "fsdp", axis=0, tiled=True),
        lax.all_gather(lookup_map_matrix, "fsdp", axis=0, tiled=True),
        lax.all_gather(content_map_matrix, "fsdp", axis=0, tiled=True),
        lax.all_gather(mixer_result_matrix, "fsdp", axis=1, tiled=True),
        lax.all_gather(expand_layer_matrix, "fsdp", axis=0, tiled=True),
        lax.all_gather(contract_layer_matrix, "fsdp", axis=1, tiled=True),
    )
    gain_one = gain_one.astype(jnp.float32)
    shift_one = shift_one.astype(jnp.float32)
    gain_two = gain_two.astype(jnp.float32)
    shift_two = shift_two.astype(jnp.float32)
    project = jnp.concatenate([query_full, key_full, value_full], axis=1)
    local_width = query_full.shape[1]
    local_heads = local_width // width
    local_hidden = hidden_full.shape[1]
    row_index = position * rows + jnp.arange(rows, dtype=jnp.int32)
    slot_of_row = row_index // SEQ_LEN
    series_place_total = occupancy_mask.shape[0]
    agreeing_lines = (
        slot_of_row[:, None] == jnp.arange(series_place_total, dtype=jnp.int32)[None, :]
    ).astype(jnp.float32)
    alive_tokens = jnp.sum(
        agreeing_lines * occupancy_mask.astype(jnp.float32)[None, :], axis=1, keepdims=True
    )
    joined = jnp.concatenate([entering_states, bypass_states], axis=1)
    merged = jnp.dot(joined, merge_full, preferred_element_type=jnp.float32) + merge_add.astype(
        jnp.float32
    )
    first = layer_norm(merged, gain_one, shift_one).astype(jnp.bfloat16)
    first_all = lax.all_gather(first, "tp", axis=0, tiled=True)
    group_rows = first_all.shape[0]
    slots = group_rows // SEQ_LEN
    projected = jnp.dot(first_all, project, preferred_element_type=jnp.float32).astype(jnp.bfloat16)
    shaped = projected.reshape(slots, SEQ_LEN, 3, local_heads, width)
    queries = shaped[:, :, 0]
    keys_all = shaped[:, :, 1]
    values = shaped[:, :, 2]
    attended, summary = lax.map(
        lambda item: attend_forward(item[0], item[1], item[2]), (queries, keys_all, values)
    )
    attended_flat = attended.reshape(group_rows, local_width)
    attention_term = jnp.dot(attended_flat, output_full, preferred_element_type=jnp.float32)
    after_attn = (
        merged
        + lax.psum_scatter(
            attention_term.astype(jnp.bfloat16), "tp", scatter_dimension=0, tiled=True
        ).astype(jnp.float32)
        + output_add.astype(jnp.float32)
    )
    second = layer_norm(after_attn, gain_two, shift_two).astype(jnp.bfloat16)
    second_all = lax.all_gather(second, "tp", axis=0, tiled=True)
    hidden_slice = lax.dynamic_slice_in_dim(
        hidden_add.astype(jnp.float32), position * local_hidden, local_hidden, 0
    )
    hidden = jnp.dot(second_all, hidden_full, preferred_element_type=jnp.float32) + hidden_slice
    active = gelu_exact(hidden).astype(jnp.bfloat16)
    feed_term = jnp.dot(active, down_full, preferred_element_type=jnp.float32)
    final = (
        after_attn
        + lax.psum_scatter(
            feed_term.astype(jnp.bfloat16), "tp", scatter_dimension=0, tiled=True
        ).astype(jnp.float32)
        + down_add.astype(jnp.float32)
    )
    missing = final - mentor_states.astype(jnp.float32)
    grad_final = alive_tokens * missing
    block_out = (final * alive_tokens).astype(jnp.bfloat16)
    energy, counted = lax.psum(
        (0.5 * jnp.sum(grad_final * missing), jnp.sum(alive_tokens)), ("fsdp", "tp")
    )
    loss_value = energy / (counted * D)
    grad_down_bias = jnp.sum(grad_final, axis=0)
    upstream = grad_final.astype(jnp.bfloat16)
    upstream_all = lax.all_gather(upstream, "tp", axis=0, tiled=True)
    grad_down = contract_rows(active, upstream_all)
    grad_active = contract_cols(upstream_all, down_full)
    gelu_value, gelu_pull = jax.vjp(gelu_exact, hidden)
    grad_hidden = gelu_pull(grad_active)[0].astype(jnp.bfloat16)
    grad_hidden_local = jnp.sum(grad_hidden.astype(jnp.float32), axis=0)
    grad_hidden_weight = contract_rows(second_all, grad_hidden)
    feed_back_term = contract_cols(grad_hidden, hidden_full)
    grad_second = lax.psum_scatter(
        feed_back_term.astype(jnp.bfloat16), "tp", scatter_dimension=0, tiled=True
    ).astype(jnp.float32)
    hidden_bias_term = lax.dynamic_update_slice_in_dim(
        jnp.zeros((hidden_add.shape[0],), jnp.float32),
        grad_hidden_local,
        position * local_hidden,
        0,
    )
    norm_value, second_pull = jax.vjp(layer_norm, after_attn, gain_two, shift_two)
    back_after, grad_gain_two, grad_shift_two = second_pull(grad_second)
    grad_after = grad_final + back_after
    grad_output_bias = jnp.sum(grad_after, axis=0)
    branch_all = lax.all_gather(grad_after.astype(jnp.bfloat16), "tp", axis=0, tiled=True)
    grad_output_weight = contract_rows(attended_flat, branch_all)
    grad_attended = contract_cols(branch_all, output_full).astype(jnp.bfloat16)
    upstream_heads = grad_attended.reshape(slots, SEQ_LEN, local_heads, width)
    grad_q_heads, grad_k_heads, grad_v_heads = lax.map(
        lambda item: attend_backward(item[0], item[1], item[2], item[3], item[4]),
        (queries, keys_all, values, summary, upstream_heads),
    )
    grad_projected = jnp.stack([grad_q_heads, grad_k_heads, grad_v_heads], axis=2).reshape(
        group_rows, 3 * local_width
    )
    grad_project = contract_rows(first_all, grad_projected)
    attention_back_term = contract_cols(grad_projected, project)
    grad_first = lax.psum_scatter(
        attention_back_term.astype(jnp.bfloat16), "tp", scatter_dimension=0, tiled=True
    ).astype(jnp.float32)
    first_value, first_pull = jax.vjp(layer_norm, merged, gain_one, shift_one)
    back_merged, grad_gain_one, grad_shift_one = first_pull(grad_first)
    grad_merged = grad_after + back_merged
    grad_merge_bias = jnp.sum(grad_merged, axis=0)
    merge_grad = grad_merged.astype(jnp.bfloat16)
    grad_merge_weight = contract_rows(joined, merge_grad)
    grad_joined = contract_cols(merge_grad, merge_full)
    model_width = entering_states.shape[1]
    grad_tokens = grad_joined[:, :model_width]
    grad_shortcut = grad_joined[:, model_width:]
    grad_query, grad_key, grad_value, grad_output, grad_hidden_full, grad_down_full = (
        lax.psum_scatter(
            grad_project[:, :local_width].astype(jnp.bfloat16),
            "fsdp",
            scatter_dimension=0,
            tiled=True,
        ).astype(jnp.float32),
        lax.psum_scatter(
            grad_project[:, local_width : 2 * local_width].astype(jnp.bfloat16),
            "fsdp",
            scatter_dimension=0,
            tiled=True,
        ).astype(jnp.float32),
        lax.psum_scatter(
            grad_project[:, 2 * local_width :].astype(jnp.bfloat16),
            "fsdp",
            scatter_dimension=0,
            tiled=True,
        ).astype(jnp.float32),
        lax.psum_scatter(
            grad_output_weight.astype(jnp.bfloat16), "fsdp", scatter_dimension=1, tiled=True
        ).astype(jnp.float32),
        lax.psum_scatter(
            grad_hidden_weight.astype(jnp.bfloat16), "fsdp", scatter_dimension=0, tiled=True
        ).astype(jnp.float32),
        lax.psum_scatter(
            grad_down.astype(jnp.bfloat16), "fsdp", scatter_dimension=1, tiled=True
        ).astype(jnp.float32),
    )
    (
        merge_weight_sum,
        merge_bias_sum,
        gain_one_sum,
        shift_one_sum,
        output_bias_sum,
        gain_two_sum,
        shift_two_sum,
        hidden_bias_sum,
        down_bias_sum,
    ) = (
        lax.psum_scatter(grad_merge_weight, ("fsdp", "tp"), scatter_dimension=0, tiled=True),
        lax.psum_scatter(grad_merge_bias, ("fsdp", "tp"), scatter_dimension=0, tiled=True),
        lax.psum_scatter(grad_gain_one, ("fsdp", "tp"), scatter_dimension=0, tiled=True),
        lax.psum_scatter(grad_shift_one, ("fsdp", "tp"), scatter_dimension=0, tiled=True),
        lax.psum_scatter(grad_output_bias, ("fsdp", "tp"), scatter_dimension=0, tiled=True),
        lax.psum_scatter(grad_gain_two, ("fsdp", "tp"), scatter_dimension=0, tiled=True),
        lax.psum_scatter(grad_shift_two, ("fsdp", "tp"), scatter_dimension=0, tiled=True),
        lax.psum_scatter(hidden_bias_term, ("fsdp", "tp"), scatter_dimension=0, tiled=True),
        lax.psum_scatter(grad_down_bias, ("fsdp", "tp"), scatter_dimension=0, tiled=True),
    )
    return (
        block_out,
        loss_value,
        grad_tokens,
        grad_shortcut,
        merge_weight_sum,
        merge_bias_sum,
        gain_one_sum,
        shift_one_sum,
        grad_query,
        grad_key,
        grad_value,
        grad_output,
        output_bias_sum,
        gain_two_sum,
        shift_two_sum,
        grad_hidden_full,
        hidden_bias_sum,
        grad_down_full,
        down_bias_sum,
    )


LOG2E = math.log2(math.e)
PAIR = 128
CHUNK = 368


def nn(a, b):
    return lax.dot_general(a, b, (((1,), (0,)), ((), ())), preferred_element_type=jnp.float32)


def nt(a, b):
    return lax.dot_general(a, b, (((1,), (1,)), ((), ())), preferred_element_type=jnp.float32)


def tn(a, b):
    return lax.dot_general(a, b, (((0,), (0,)), ((), ())), preferred_element_type=jnp.float32)


def vmem():
    return pltpu.CompilerParams(vmem_limit_bytes=60 * 2**20)


def cuts(count, size):
    edges = [i * size for i in range(count // size)] + [count]
    return [slice(a, b) for a, b in zip(edges, edges[1:])]


def attention_forward_kernel(q_ref, k_ref, v_ref, o_ref, l_ref):
    count = q_ref.shape[0]
    scale = (PAIR // 2) ** -0.5 * LOG2E
    low = lax.broadcasted_iota(jnp.int32, (1, PAIR), 1) < PAIR // 2
    keys, values = k_ref[...], v_ref[...]
    zero = jnp.zeros_like(keys)
    heads = (jnp.where(low, keys, zero), jnp.where(low, zero, keys))
    wide = jnp.concatenate([values, jnp.ones_like(values)], axis=1)
    for part in cuts(count, 512):
        queries = q_ref[part, :]
        outs, sums = [], []
        for scores in [nt(queries, head) for head in heads]:
            peak = jnp.max(scores, axis=1, keepdims=True) * scale
            raised = jnp.exp2(scores * scale - peak).astype(jnp.bfloat16)
            both = nn(raised, wide)
            total = both[:, PAIR:]
            outs.append(both[:, :PAIR] / total)
            sums.append(peak + jnp.log2(total))
        o_ref[part, :] = jnp.where(low, outs[0], outs[1]).astype(jnp.bfloat16)
        l_ref[part, :] = jnp.where(low, sums[0], sums[1])


def attention_backward_kernel(q_ref, k_ref, v_ref, o_ref, l_ref, u_ref, out_ref, total_ref):
    count = q_ref.shape[0]
    plain = (PAIR // 2) ** -0.5
    scale = plain * LOG2E
    low = lax.broadcasted_iota(jnp.int32, (1, PAIR), 1) < PAIR // 2
    queries, upstream = q_ref[...], u_ref[...]
    product = upstream.astype(jnp.float32) * o_ref[...].astype(jnp.float32)
    left = jnp.sum(jnp.where(low, product, 0.0), axis=1, keepdims=True)
    right = jnp.sum(jnp.where(low, 0.0, product), axis=1, keepdims=True)
    centres = jnp.transpose(jnp.where(low, left, right))
    logs = jnp.transpose(l_ref[...])
    for head in range(2):

        def own(value):
            zero = jnp.zeros_like(value)
            return jnp.where(low, value, zero) if head == 0 else jnp.where(low, zero, value)

        row = head * (PAIR // 2)
        own_queries, own_upstream = own(queries), own(upstream)
        log_row, centre = logs[row : row + 1, :], centres[row : row + 1, :]
        for part in cuts(count, 256):
            keys, values = k_ref[part, :], v_ref[part, :]
            probs = jnp.exp2(nt(keys, own_queries) * scale - log_row)
            slopes = (probs * (nt(values, own_upstream) - centre)).astype(jnp.bfloat16)
            grad_v = nn(probs.astype(jnp.bfloat16), own_upstream).astype(jnp.bfloat16)
            grad_k = (nn(slopes, own_queries) * plain).astype(jnp.bfloat16)
            grad_q = tn(slopes, own(keys))
            if head == 0:
                out_ref[1, part, :] = grad_k
                out_ref[2, part, :] = grad_v
            else:
                out_ref[1, part, :] = jnp.where(low, out_ref[1, part, :], grad_k)
                out_ref[2, part, :] = jnp.where(low, out_ref[2, part, :], grad_v)
            if head == 0 and part.start == 0:
                total_ref[...] = grad_q
            else:
                total_ref[...] += grad_q
    out_ref[0] = (total_ref[...] * plain).astype(jnp.bfloat16)


def gelu_both(value):
    t = 1.0 / (1.0 + 0.3275911 * math.sqrt(0.5) * jnp.abs(value))
    bell = jnp.exp2(value * value * (-0.5 * LOG2E))
    poly = 0.5 * 1.061405429 * t - 0.5 * 1.453152027
    poly = poly * t + 0.5 * 1.421413741
    poly = poly * t - 0.5 * 0.284496736
    poly = poly * t + 0.5 * 0.254829592
    rest = poly * t * bell
    below = jnp.where(value >= 0, 1.0 - rest, rest)
    return value * below, below + value * bell * (1.0 / math.sqrt(2.0 * math.pi))


def normalized(value):
    centred = value - jnp.mean(value, axis=-1, keepdims=True)
    spread = jnp.mean(centred * centred, axis=-1, keepdims=True)
    inverse = lax.rsqrt(spread + EPSILON)
    return centred * inverse, inverse


def place_at(where_ref, hi, lo, y_rel, c_rel, rows):
    y = jnp.bitwise_xor(where_ref[0], y_rel)
    c = jnp.bitwise_xor(where_ref[1], c_rel)
    return pl.multiple_of(((hi * 2 + lo) * 4 + y * 2 + c) * rows, rows)


BITS = (0, 1)


def once(block, index):
    return pl.BlockSpec(block, index, pipeline_mode=pl.Buffered(1))


def call(kernel, grid, where, ins, outs, scratch, name, after=(), aliases=(), flops=0):
    first, count = len(ins), len(after)

    def ordered_kernel(where_ref, *refs):
        kernel(where_ref, *refs[:first], *refs[first + count :])

    anywhere = pl.BlockSpec(memory_space=pl.ANY)
    return pl.pallas_call(
        ordered_kernel,
        grid_spec=pltpu.PrefetchScalarGridSpec(
            num_scalar_prefetch=1,
            grid=grid,
            in_specs=[spec for _, spec in ins] + [anywhere] * count,
            out_specs=[spec for _, _, spec in outs],
            scratch_shapes=scratch,
        ),
        out_shape=[jax.ShapeDtypeStruct(s, t) for s, t, _ in outs],
        input_output_aliases={1 + i: o for i, o in aliases},
        compiler_params=vmem(),
        cost_estimate=pl.CostEstimate(flops=flops, bytes_accessed=0, transcendentals=0),
        name=name,
    )(where, *(x for x, _ in ins), *after)


def resident(shape):
    return once(shape, lambda *_: (0,) * len(shape))


def attention_forward(where, projected):
    rows, columns = projected.shape
    pairs = columns // 3 // PAIR

    def block(offset):
        return pl.BlockSpec((rows, PAIR), lambda j, s: (0, offset + j))

    return call(
        lambda where_ref, *refs: attention_forward_kernel(*refs),
        (pairs,),
        where,
        [(projected, block(0)), (projected, block(pairs)), (projected, block(2 * pairs))],
        [
            ((rows, pairs * PAIR), jnp.bfloat16, block(0)),
            ((rows, pairs * PAIR), jnp.float32, block(0)),
        ],
        [],
        "attention_forward",
    )


def attention_backward(where, projected, attended, logs, upstream, index, of, grads):
    rows, columns = projected.shape
    pairs = columns // 3 // PAIR
    here = index * (pairs // of)

    def block(offset):
        return pl.BlockSpec((rows, PAIR), lambda j, s: (0, offset + here + j))

    ins = [
        (projected, block(0)),
        (projected, block(pairs)),
        (projected, block(2 * pairs)),
        (attended, block(0)),
        (logs, block(0)),
        (upstream, block(0)),
    ]
    aliases = ()
    if grads is not None:
        ins.append((grads, pl.BlockSpec(memory_space=pl.ANY)))
        aliases = ((6, 0),)

    def kernel(where_ref, *refs):
        attention_backward_kernel(*refs[:6], *refs[-2:])

    return call(
        kernel,
        (pairs // of,),
        where,
        ins,
        [((3, rows, pairs * PAIR), jnp.bfloat16, pl.BlockSpec((3, rows, PAIR), lambda j, s: (0, 0, here + j)))],
        [pltpu.VMEM((rows, PAIR), jnp.float32)],
        "attention_backward",
        (),
        aliases,
    )[0]


def gate(where, values, after):
    anywhere = pl.BlockSpec(memory_space=pl.ANY)
    return call(
        lambda *refs: None,
        (1,),
        where,
        [(v, anywhere) for v in values],
        [(v.shape, v.dtype, anywhere) for v in values],
        [],
        "gate",
        after,
        tuple((i, i) for i in range(len(values))),
    )


def fold_kernel(jobs, carried, waited, where, *refs):
    sources = iter(refs)
    total = sum(len(parts) for pieces, _ in jobs for parts in pieces)
    targets = iter(refs[total + carried + waited :])
    for pieces, results in jobs:
        held = [[next(sources) for _ in parts] for parts in pieces]
        for kind, select in results:
            out, begin = next(targets), 0
            at = tuple(slice(None) if t is None else jnp.bitwise_xor(where[t[0]], t[1]) for t in select)
            for parts in held:
                value = parts[0][at + (Ellipsis,)].astype(jnp.float32)
                for part in parts[1:]:
                    value = value + part[at + (Ellipsis,)].astype(jnp.float32)
                end = begin + value.shape[-1]
                out[..., begin:end] = value.astype(out.dtype)
                begin = end


def fold(where, jobs, carry=(), after=(), flops=0):
    ins, outs, plan = [], [], []
    for pieces, results in jobs:
        columns = 0
        for parts in pieces:
            for array, lead in parts:
                fixed = lead + (None, None)
                block = tuple(n if t is None else pl.squeezed for n, t in zip(array.shape, fixed))
                index = tuple(0 if t is None else t for t in fixed)
                ins.append((array, once(block, lambda i, s, index=index: index)))
            columns += array.shape[-1]
        shape = tuple(n for n, t in zip(array.shape, fixed) if t is None)[:-1] + (columns,)
        for kind, select in results:
            made = tuple(n for n, t in zip(shape, select) if t is None) + shape[len(select) :]
            outs.append((made, kind, resident(made)))
        plan.append((pieces, results))
    anywhere = pl.BlockSpec(memory_space=pl.ANY)
    count, made = len(ins), len(outs)
    ins += [(c, anywhere) for c in carry]
    outs += [(c.shape, c.dtype, anywhere) for c in carry]
    return call(
        functools.partial(fold_kernel, plan, len(carry), 0),
        (1,),
        where,
        ins,
        outs,
        [],
        "fold",
        after,
        tuple((count + i, made + i) for i in range(len(carry))),
        flops,
    )


def pile_kernel(slot, axis, where, mine, other, *outs):
    here = 0 if slot is None else where[slot]
    there = 1 - here
    lead = outs[0].shape[:axis]
    rows = outs[0].shape[-2]
    for number, out in enumerate(outs):
        part = slice(number * rows, (number + 1) * rows)
        for i in range(math.prod(lead)):
            at = ()
            for size in reversed(lead):
                at = (i % size,) + at
                i //= size
            out[at + (here,)] = mine[at + (Ellipsis, part, slice(None))]
            out[at + (there,)] = other[at + (Ellipsis, part, slice(None))]


def pile(where, slot, mine, other, axis, parts=1):
    shape = mine.shape[:axis] + (2,) + mine.shape[axis:-2] + (mine.shape[-2] // parts, mine.shape[-1])
    made = call(
        functools.partial(pile_kernel, slot, axis),
        (1,),
        where,
        [(mine, resident(mine.shape)), (other, resident(mine.shape))],
        [(shape, mine.dtype, resident(shape))] * parts,
        [],
        "pile",
    )
    return made if parts > 1 else made[0]


def merge_kernel(where, ent, byp, full, out):
    half = ent.shape[1]
    weight = full[...].reshape(2 * half, half)
    out[...] = nn(ent[...], weight[:half, :]) + nn(byp[...], weight[half:, :])


def merge_forward(where, ent, byp, gathered, r):
    rows, d = ent.shape
    part = pl.BlockSpec((CHUNK, d), lambda i, w: (i, 0))
    return call(
        merge_kernel,
        (rows // CHUNK,),
        where,
        [(ent, part), (byp, part), (gathered, resident((2, 2, 2, 2, 2, r, d)))],
        [((rows, d), jnp.float32, part)],
        [],
        "merge_forward",
    )[0]


def weight_block(r, col, number):
    def index(*args):
        which, x_rel = number(*args[:-1])
        return 0, 0, 0, 0, jnp.bitwise_xor(x_rel, args[-1][2]), 1 + which // 2, which % 2

    return pl.BlockSpec((2, 2, 2, 2, pl.squeezed, r, col), index)


def project_kernel(where, raw, vec, weight, merged, first, out):
    @pl.when((pl.program_id(0) == 0) & (pl.program_id(1) == 0))
    def _():
        for start in range(0, raw.shape[0], CHUNK):
            part = slice(start, start + CHUNK)
            total = raw[part, :] + vec[0:1, :]
            merged[part, :] = total
            norm, _ = normalized(total)
            first[part, :] = (norm * vec[1:2, :] + vec[2:3, :]).astype(jnp.bfloat16)

    out[...] = nn(first[...], weight[...].reshape(first.shape[1], -1)).astype(jnp.bfloat16)


def project_forward(where, raw, vec, gathered, r, col):
    rows, d = raw.shape
    f32, bf16 = jnp.float32, jnp.bfloat16
    return call(
        project_kernel,
        (3, 2),
        where,
        [
            (raw, resident((rows, d))),
            (vec, resident(vec.shape)),
            (gathered, weight_block(r, col, lambda w, x: (w, x))),
        ],
        [
            ((rows, d), f32, resident((rows, d))),
            ((rows, d), bf16, resident((rows, d))),
            ((rows, 6 * col), bf16, pl.BlockSpec((rows, col), lambda w, x, s: (0, w * 2 + x))),
        ],
        [],
        "project_forward",
    )


def result_kernel(where, attended, merged, vec, weight, after, second, total):
    step = pl.program_id(0)
    natural = weight[...].reshape(after.shape[1], -1)

    @pl.when(step == 0)
    def _():
        total[...] = nt(attended[...], natural)

    @pl.when(step == 1)
    def _():
        for start in range(0, after.shape[0], CHUNK):
            here = slice(start, start + CHUNK)
            part = nt(attended[here, :], natural)
            value = merged[here, :] + vec[3:4, :] + (total[here, :] + part)
            after[here, :] = value
            norm, _ = normalized(value)
            second[here, :] = (norm * vec[4:5, :] + vec[5:6, :]).astype(jnp.bfloat16)


def result_forward(where, attended, merged, vec, gathered, r, col):
    rows, d = merged.shape
    return call(
        result_kernel,
        (2,),
        where,
        [
            (attended, pl.BlockSpec((rows, col), lambda x, s: (0, x))),
            (merged, resident((rows, d))),
            (vec, resident(vec.shape)),
            (gathered, weight_block(r, col, lambda x: (3, x))),
        ],
        [
            ((rows, d), jnp.float32, resident((rows, d))),
            ((rows, d), jnp.bfloat16, resident((rows, d))),
        ],
        [pltpu.VMEM((rows, d), jnp.float32)],
        "result_forward",
    )


def fill_by_core(where, full, refs, rows):
    for c_rel, ref in enumerate(refs):
        for y_rel in BITS:
            for hi in BITS:
                for lo in BITS:
                    at = place_at(where, hi, lo, y_rel, c_rel, rows)
                    full[pl.ds(at, rows), :] = ref[y_rel, hi, lo]


def spill_by_core(where, full, refs, rows):
    for c_rel, ref in enumerate(refs):
        for y_rel in BITS:
            for hi in BITS:
                for lo in BITS:
                    at = place_at(where, hi, lo, y_rel, c_rel, rows)
                    ref[y_rel, hi, lo] = full[pl.ds(at, rows), :]


def expand_kernel(rows, where, second, bias, w0, w1, w2, w3, active, slope, full):
    @pl.when(pl.program_id(0) == 0)
    def _():
        fill_by_core(where, full, (w0, w1), rows)

    @pl.when(pl.program_id(0) == 1)
    def _():
        fill_by_core(where, full, (w2, w3), rows)

    for start in range(0, second.shape[0], CHUNK):
        part = slice(start, start + CHUNK)
        hidden = nn(second[part, :], full[...]) + bias[...]
        value, rate = gelu_both(hidden)
        active[part, :] = value.astype(jnp.bfloat16)
        slope[part, :] = rate.astype(jnp.bfloat16)


def expand_forward(where, second, bias, pieces, block=512):
    rows, d = second.shape
    *_, r, half = pieces[0][0].shape
    steps = half // block
    near = pl.BlockSpec((2, 2, 2, r, block), lambda x, j, s: (0, 0, 0, 0, jnp.where(x == 0, j, steps - 1)))
    far = pl.BlockSpec((2, 2, 2, r, block), lambda x, j, s: (0, 0, 0, 0, jnp.where(x == 0, 0, j)))
    out = pl.BlockSpec((pl.squeezed, rows, block), lambda x, j, s: (x, 0, j))
    return call(
        functools.partial(expand_kernel, r),
        (2, steps),
        where,
        [
            (second, resident((rows, d))),
            (bias, pl.BlockSpec((pl.squeezed, 1, block), lambda x, j, s: (jnp.bitwise_xor(x, s[2]), 0, j))),
        ]
        + [(p, near) for p in pieces[0]]
        + [(p, far) for p in pieces[1]],
        [((2, rows, half), jnp.bfloat16, out)] * 2,
        [pltpu.VMEM((d, block), jnp.bfloat16)],
        "expand_forward",
    )


def contract_kernel(steps, where, alive, active, after, mentor, vec, weight, out, upstream, sums, energy, total):
    step = pl.program_id(0)
    count, d = after.shape
    full = weight[...].reshape(d, -1)

    @pl.when(step == 0)
    def _():
        total[...] = nt(active[...], full)

    @pl.when((step > 0) & (step < 2 * steps - 1))
    def _():
        total[...] += nt(active[...], full)

    @pl.when(step == 2 * steps - 1)
    def _():
        live = alive[0]
        column, squares = 0.0, 0.0
        for start in range(0, count, CHUNK):
            part = slice(start, start + CHUNK)
            final = after[part, :] + (total[part, :] + nt(active[part, :], full)) + vec[6:7, :]
            missing = final - mentor[part, :].astype(jnp.float32)
            slope = live * missing
            out[part, :] = (live * final).astype(jnp.bfloat16)
            upstream[part, :] = slope.astype(jnp.bfloat16)
            column += jnp.sum(slope, axis=0, keepdims=True)
            squares += jnp.sum(slope * missing, axis=0, keepdims=True)
        sums[...] = jnp.broadcast_to(column, sums.shape)
        energy[...] = jnp.broadcast_to(0.5 * jnp.sum(squares, axis=1, keepdims=True), energy.shape)


def contract_forward(where, alive, active, after, mentor, vec, weights, block=1024):
    rows, d = after.shape
    *_, r, half = weights.shape
    steps = half // block
    weight = pl.BlockSpec(
        (2, 2, 2, 2, pl.squeezed, r, block),
        lambda j, s: (0, 0, 0, 0, jnp.bitwise_xor(j // steps, s[2]), 0, j % steps),
    )
    f32, bf16 = jnp.float32, jnp.bfloat16
    whole = resident((rows, d))
    return call(
        functools.partial(contract_kernel, steps),
        (2 * steps,),
        where,
        [
            (alive, pl.BlockSpec(memory_space=pltpu.SMEM)),
            (active, pl.BlockSpec((pl.squeezed, rows, block), lambda j, s: (j // steps, 0, j % steps))),
            (after, whole),
            (mentor, whole),
            (vec, resident(vec.shape)),
            (weights, weight),
        ],
        [
            ((rows, d), bf16, whole),
            ((rows, d), bf16, whole),
            ((8, d), f32, resident((8, d))),
            ((8, 128), f32, resident((8, 128))),
        ],
        [pltpu.VMEM((rows, d), f32)],
        "contract_forward",
    )


def feed_backward_kernel(rows, where, upstream, second, active, slope, weight, w0, w1,
                         grad_second, e0, e1, d0, d1, bias, up, result, total):
    step, last = pl.program_id(0), pl.num_programs(0) - 1
    fill_by_core(where, up, (w0, w1), rows)
    grad_active = nn(upstream[...], weight[...].reshape(up.shape))
    grad_hidden = grad_active * slope[...].astype(jnp.float32)
    bias[...] = jnp.broadcast_to(jnp.sum(grad_hidden, axis=0, keepdims=True), bias.shape)
    grad_hidden = grad_hidden.astype(jnp.bfloat16)
    result[...] = tn(upstream[...], active[...]).astype(jnp.bfloat16)
    spill_by_core(where, result, (d0, d1), rows)
    back = nt(grad_hidden, up[...])

    @pl.when(step == 0)
    def _():
        total[...] = back

    @pl.when((step > 0) & (step < last))
    def _():
        total[...] += back

    @pl.when(step == last)
    def _():
        grad_second[...] = (total[...] + back).astype(jnp.bfloat16)

    result[...] = tn(second[...], grad_hidden).astype(jnp.bfloat16)
    spill_by_core(where, result, (e0, e1), rows)


def feed_backward(where, upstream, second, active, slope, down, up, x_rel, block=512):
    rows, d = upstream.shape
    *_, r, half = up[0].shape
    f32, bf16 = jnp.float32, jnp.bfloat16
    whole = resident((rows, d))
    part = pl.BlockSpec((pl.squeezed, rows, block), lambda j, s: (x_rel, 0, j))
    piece = pl.BlockSpec((2, 2, 2, r, block), lambda j, s: (0, 0, 0, 0, j))
    weight = pl.BlockSpec(
        (2, 2, 2, 2, pl.squeezed, r, block),
        lambda j, s: (0, 0, 0, 0, jnp.bitwise_xor(x_rel, s[2]), 0, j),
    )
    return call(
        functools.partial(feed_backward_kernel, r),
        (half // block,),
        where,
        [(upstream, whole), (second, whole), (active, part), (slope, part), (down, weight)]
        + [(p, piece) for p in up],
        [((rows, d), bf16, whole)]
        + [((2, 2, 2, r, half), bf16, piece)] * 4
        + [((8, half), f32, pl.BlockSpec((8, block), lambda j, s: (0, j)))],
        [pltpu.VMEM((d, block), bf16)] * 2 + [pltpu.VMEM((rows, d), f32)],
        "feed_backward",
    )


def norm_backward_kernel(count, gain_row, last, where, value, base, vec, *refs):
    outs = 2 if last else 3
    grads, extra, (*total, low, sums) = refs[:count], refs[count:-outs], refs[-outs:]

    @pl.when(pl.program_id(0) == 0)
    def _():
        sums[...] = jnp.zeros_like(sums)
        if extra:
            column, energy, alive, own, other = extra
            d = sums.shape[1]
            sums[3:4, :] = column[0:1, :]
            sums[4:5, :] = jnp.broadcast_to(energy[0:1, 0:1], (1, d))
            sums[5:6, :] = jnp.full((1, d), alive[0] * (value.shape[0] * pl.num_programs(0)), jnp.float32)
            here = where[2] == 0
            for i in BITS:
                part = slice(i * d, (i + 1) * d)
                sums[8 + i : 9 + i, :] = jnp.where(here, own[0:1, part], other[0:1, part])
                sums[10 + i : 11 + i, :] = jnp.where(here, other[0:1, part], own[0:1, part])

    upstream = grads[0][...].astype(jnp.float32)
    for ref in grads[1:]:
        upstream = upstream + ref[...].astype(jnp.float32)
    norm, inverse = normalized(value[...])
    e = upstream * vec[gain_row : gain_row + 1, :]
    mean_e = jnp.mean(e, axis=-1, keepdims=True)
    mean_en = jnp.mean(e * norm, axis=-1, keepdims=True)
    result = base[...].astype(jnp.float32) + inverse * (e - mean_e - norm * mean_en)
    for ref in total:
        ref[...] = result
    low[...] = result.astype(jnp.bfloat16)
    for row, item in enumerate((upstream * norm, upstream, result)):
        sums[row : row + 1, :] += jnp.sum(item, axis=0, keepdims=True)


def norm_backward(where, value, base, vec, gain_row, grads, extra=(), last=False):
    rows, d = value.shape
    part = pl.BlockSpec((CHUNK, d), lambda i, s: (i, 0))
    height = 16 if extra else 8
    carried = [
        (x, pl.BlockSpec(memory_space=pltpu.SMEM) if x.ndim == 1 else resident(x.shape)) for x in extra
    ]
    return call(
        functools.partial(norm_backward_kernel, len(grads), gain_row, last),
        (rows // CHUNK,),
        where,
        [(value, part), (base, part), (vec, resident(vec.shape))] + [(g, part) for g in grads] + carried,
        [((rows, d), jnp.float32, part)] * (0 if last else 1)
        + [
            ((rows, d), jnp.bfloat16, part),
            ((height, d), jnp.float32, resident((height, d))),
        ],
        [],
        "norm_backward",
    )


def result_backward_kernel(rows, where, branch, attended, weight, grad, o0, o1, full):
    grad[...] = nn(branch[...], weight[...].reshape(branch.shape[1], -1)).astype(jnp.bfloat16)
    full[...] = tn(branch[...], attended[...]).astype(jnp.bfloat16)
    spill_by_core(where, full, (o0, o1), rows)


def result_backward(where, branch, attended, gathered, r, col):
    rows, d = branch.shape
    bf16 = jnp.bfloat16
    part = pl.BlockSpec((rows, col), lambda x, s: (0, x))
    piece = pl.BlockSpec((pl.squeezed, pl.squeezed, 2, 2, 2, r, col), lambda x, s: (1, x, 0, 0, 0, 0, 0))
    return call(
        functools.partial(result_backward_kernel, r),
        (2,),
        where,
        [
            (branch, resident((rows, d))),
            (attended, part),
            (gathered, weight_block(r, col, lambda x: (3, x))),
        ],
        [((rows, d), bf16, part)] + [((2, 2, 2, 2, 2, r, col), bf16, piece)] * 2,
        [pltpu.VMEM((d, col), bf16)],
        "result_backward",
    )


def project_weight_kernel(rows, where, first, grad, _, __, a0, a1, b0, b1, full):
    full[...] = tn(first[...], grad[...]).astype(jnp.bfloat16)

    @pl.when(pl.program_id(0) < 2)
    def _():
        spill_by_core(where, full, (a0, a1), rows)

    @pl.when(pl.program_id(0) == 2)
    def _():
        spill_by_core(where, full, (b0, b1), rows)


def project_weight(where, first, grads, with_result, r, col):
    rows, d = first.shape
    bf16 = jnp.bfloat16
    part = pl.BlockSpec((pl.squeezed, rows, col), lambda w, x, s: (w, 0, x))
    block = (pl.squeezed, pl.squeezed, 2, 2, 2, r, col)
    front = pl.BlockSpec(
        block, lambda w, x, s: (jnp.minimum(w, 1), jnp.where(w < 2, x, 1), 0, 0, 0, 0, 0)
    )
    back = pl.BlockSpec(block, lambda w, x, s: (0, jnp.where(w < 2, 0, x), 0, 0, 0, 0, 0))
    anywhere = pl.BlockSpec(memory_space=pl.ANY)
    return call(
        functools.partial(project_weight_kernel, r),
        (3, 2),
        where,
        [(first, resident((rows, d))), (grads, part)] + [(p, anywhere) for p in with_result],
        [((2, 2, 2, 2, 2, r, col), bf16, front)] * 2 + [((2, 2, 2, 2, 2, r, col), bf16, back)] * 2,
        [pltpu.VMEM((d, col), bf16)],
        "project_weight",
        (),
        ((2, 2), (3, 3)),
    )


def project_backward_kernel(where, grad, weight, out, total):
    part = nt(grad[...], weight[...].reshape(out.shape[1], -1))
    step = pl.program_id(0) * pl.num_programs(1) + pl.program_id(1)
    last = pl.num_programs(0) * pl.num_programs(1) - 1

    @pl.when(step == 0)
    def _():
        total[...] = part

    @pl.when((step > 0) & (step < last))
    def _():
        total[...] += part

    @pl.when(step == last)
    def _():
        out[...] = (total[...] + part).astype(jnp.bfloat16)


def project_backward(where, grads, gathered, r, col):
    _, rows, d = grads.shape
    return call(
        project_backward_kernel,
        (3, 2),
        where,
        [
            (grads, pl.BlockSpec((pl.squeezed, rows, col), lambda w, x, s: (w, 0, x))),
            (gathered, weight_block(r, col, lambda w, x: (w, x))),
        ],
        [((rows, d), jnp.bfloat16, resident((rows, d)))],
        [pltpu.VMEM((rows, d), jnp.float32)],
        "project_backward",
    )[0]


def merge_weight_kernel(where, ent, byp, grad, o0, o1, full):
    half = ent.shape[1]
    full[:half, :] = tn(ent[...], grad[...]).astype(jnp.bfloat16)
    full[half:, :] = tn(byp[...], grad[...]).astype(jnp.bfloat16)
    for c_rel, ref in enumerate((o0, o1)):
        for x_rel in BITS:
            x = jnp.bitwise_xor(where[2], x_rel)
            for y_rel in BITS:
                for hi in BITS:
                    for lo in BITS:
                        at = place_at(where, hi, lo, y_rel, c_rel, 128) + x * 64
                        ref[x_rel, y_rel, hi, lo] = full[pl.ds(pl.multiple_of(at, 64), 64), :]


def merge_weight(where, ent, byp, grad, r):
    rows, d = ent.shape
    half = d // 2
    bf16 = jnp.bfloat16
    whole = resident((rows, d))
    piece = pl.BlockSpec((pl.squeezed, 2, 2, 2, 2, r, half), lambda j, s: (j, 0, 0, 0, 0, 0, 0))
    return call(
        merge_weight_kernel,
        (2,),
        where,
        [(ent, whole), (byp, whole), (grad, pl.BlockSpec((rows, half), lambda j, s: (0, j)))],
        [((2, 2, 2, 2, 2, r, half), bf16, piece)] * 2,
        [pltpu.VMEM((2 * d, half), bf16)],
        "merge_weight",
    )


def merge_backward_kernel(where, grad, full, left, right):
    half = left.shape[1]
    weight = full[...].reshape(2 * half, half)
    left[...] = nt(grad[...], weight[:half, :])
    right[...] = nt(grad[...], weight[half:, :])


def merge_backward(where, grad, gathered, r, after):
    rows, d = grad.shape
    part = pl.BlockSpec((CHUNK, d), lambda i, w: (i, 0))
    return call(
        merge_backward_kernel,
        (rows // CHUNK,),
        where,
        [(grad, part), (gathered, resident((2, 2, 2, 2, 2, r, d)))],
        [((rows, d), jnp.float32, part)] * 2,
        [],
        "merge_backward",
        after,
    )


def swap(value, axis):
    return lax.ppermute(value, axis, [(0, 1), (1, 0)])


def swap_line(value, bit):
    return lax.ppermute(value, "z", [(i, i ^ bit) for i in range(4)])


def plus(*parts):
    total = parts[0].astype(jnp.float32)
    for part in parts[1:]:
        total = total + part.astype(jnp.float32)
    return total


def send(value, axis):
    return swap(value.astype(jnp.bfloat16), axis)


def line_parts(total, index, dim):
    mine = lax.dynamic_index_in_dim(total, index, dim, keepdims=False)
    other = lax.dynamic_index_in_dim(total, 1 - index, dim, keepdims=False)
    return mine, other.astype(jnp.bfloat16)


def one_sequence_plan(
    entering_states,
    bypass_states,
    mentor_states,
    occupancy_mask,
    bypass_merge_matrix,
    bypass_merge_offset,
    mixer_layernorm_scale,
    mixer_layernorm_offset,
    asking_map_matrix,
    lookup_map_matrix,
    content_map_matrix,
    mixer_result_matrix,
    mixer_result_offset,
    perceptron_layernorm_scale,
    perceptron_layernorm_offset,
    expand_layer_matrix,
    expand_layer_offset,
    contract_layer_matrix,
    contract_layer_offset,
):
    f32, bf16 = jnp.float32, jnp.bfloat16
    rows, d = entering_states.shape
    r, col = asking_map_matrix.shape
    half = expand_layer_matrix.shape[1]
    everyone = ("z", "y", "c", "x")
    z, y, c, x = (lax.axis_index(axis) for axis in everyone)
    hi, lo = z // 2, z % 2
    device = ((z * 2 + y) * 2 + c) * 2 + x
    where = jnp.stack([y, c, x, hi, lo]).astype(jnp.int32)
    small = (
        bypass_merge_offset,
        mixer_layernorm_scale,
        mixer_layernorm_offset,
        mixer_result_offset,
        perceptron_layernorm_scale,
        perceptron_layernorm_offset,
        contract_layer_offset,
        expand_layer_offset,
    )
    flat = jnp.concatenate(small)
    flat = jnp.pad(flat, (0, 8 * d - flat.shape[0])).reshape(8, d)
    pack = jnp.concatenate(
        [
            bypass_merge_matrix,
            jnp.concatenate([asking_map_matrix, lookup_map_matrix], axis=1),
            jnp.concatenate([content_map_matrix, mixer_result_matrix.T], axis=1),
            flat,
        ]
    )
    pack = lax.all_gather(pack, everyone, axis=0, tiled=False)
    gathered = pack.reshape((2,) * 5 + pack.shape[1:])

    down = lax.all_gather(contract_layer_matrix.T, everyone, axis=0, tiled=False)
    down = down.reshape((2,) * 5 + down.shape[1:])

    up = expand_layer_matrix
    up = pile(where, 3, up, swap_line(up, 2), 0)
    up = pile(where, 4, up, swap_line(up, 1), 1)
    up_block = pile(where, None, up, swap(up, "y"), 0)
    (gathered,) = gate(where, [gathered], (up_block,))
    raw = merge_forward(where, entering_states, bypass_states, gathered, r)

    rest = pack[:, 3 * r].astype(f32)
    count = pack.shape[0]
    vec = rest[:, : 7 * d // count].reshape(count, 7, d // count).transpose(1, 0, 2).reshape(7, d)
    vec = jnp.pad(vec, ((0, 1), (0, 0)))
    hidden_add = rest[:, 7 * d // count : 7 * d // count + 2 * half // count].reshape(2, 1, half)
    alive = lax.dynamic_index_in_dim(occupancy_mask, x, keepdims=True).astype(f32)

    merged, first, projected = project_forward(where, raw, vec, gathered, r, col)
    up_other, projected = gate(where, [swap(up_block, "x"), projected], ())
    up_away = [swap(up_block, "c"), swap(up_other, "c")]
    attended, logs = attention_forward(where, projected)
    *up_away, attended, logs = gate(where, up_away + [attended, logs], ())
    expand_pieces = ((up_block, up_away[0]), (up_other, up_away[1]))
    after_attn, second = result_forward(where, attended, merged, vec, gathered, r, col)
    active, slope = expand_forward(where, second, hidden_add, expand_pieces)
    block_out, upstream, down_bias, energy = contract_forward(
        where, alive, active, after_attn, mentor_states, vec, down
    )

    def feed(x_rel):
        return feed_backward(
            where, upstream, second, active, slope, down, expand_pieces[x_rel], x_rel
        )

    none2, none3 = (None,) * 2, (None,) * 3
    by_lo = [(f32, (None, (4, 0))), (bf16, (None, (4, 1)))]
    by_hi = [(f32, ((3, 0),)), (bf16, ((3, 1),))]

    gs1, e1, e1s, d1, d1s, hb1 = feed(1)
    e1c, d1c = swap(e1s, "c"), swap(d1s, "c")
    gs0, e0, e0s, d0, d0s, hb0 = feed(0)
    e1x, d1y, gs0, e0s, d0s = fold(
        where,
        [
            ([[(e1, none3), (e1c, none3)]], [(bf16, ())]),
            ([[(d1, (1,) + none2), (d1c, (1,) + none2)]], [(bf16, ())]),
        ],
        (gs0, e0s, d0s),
    )
    e1x, d1y, e0c, d0c = swap(e1x, "x"), swap(d1y, "y"), swap(e0s, "c"), swap(d0s, "c")
    grad_after, branch, sums_two = norm_backward(
        where, after_attn, upstream, vec, 4, [gs0, gs1], (down_bias, energy, alive, hb0, hb1)
    )
    parcel = lax.all_gather(sums_two, everyone, axis=0, tiled=False)
    d0y, branch = fold(
        where, [([[(d0, (1,) + none2), (d0c, (1,) + none2)]], [(bf16, ())])], (branch,), (e0c,)
    )
    d0y = swap(d0y, "y")
    grad_attended, o0, o1 = result_backward(where, branch, attended, gathered, r, col)

    def attend(part, grads):
        return attention_backward(where, projected, attended, logs, grad_attended, part, 2, grads)

    grads = attend(0, None)
    e_far, d_far, grads = fold(
        where,
        [
            ([[(a, (1,) + none2) for a in (e0, e0c, e1x)]], [(bf16, ())]),
            ([[(d1, (0,) + none2), (d1c, (0,) + none2), (d1y, none2)]], [(bf16, ())]),
        ],
        (grads,),
        (d0y,),
    )
    e_far, d_far = swap(e_far, "y"), swap(d_far, "x")
    grads = attend(1, grads)
    front = (0,) + none2
    ends, ends_z, grads = fold(
        where,
        [
            (
                [
                    [(e0, front), (e0c, front), (e1x, front), (e_far, none2)],
                    [(d0, front), (d0c, front), (d0y, none2), (d_far, none2)],
                ],
                by_lo,
            )
        ],
        (grads,),
        (parcel,),
    )
    ends_z = swap_line(ends_z, 1)
    p0, p1, vo0, vo1 = project_weight(where, first, grads, (o0, o1), r, col)
    qk_c, vo_c = swap(p1, "c"), swap(vo1, "c")
    grad_first = project_backward(where, grads, gathered, r, col)
    ends, ends_z, grad_first = fold(
        where, [([[(a, (None,)) for a in (ends, ends_z)]], by_hi)], (grad_first,), flops=4 * 10**10
    )
    qk_x, vo_y, grad_first = fold(
        where,
        [
            ([[(a, (None, 1) + none3) for a in (p0, qk_c)]], [(bf16, ())]),
            ([[(a, (None, None, 1) + none2) for a in (vo0, vo_c)]], [(bf16, ())]),
        ],
        (grad_first,),
    )
    qk_x, vo_y, ends_z = swap(qk_x, "x"), swap(vo_y, "y"), swap_line(ends_z, 2)
    merge_grad, three = norm_backward(where, merged, grad_after, vec, 1, [grad_first], last=True)
    m0, m1 = merge_weight(where, entering_states, bypass_states, merge_grad, r)
    three_c = swap(three, "c")
    ends, qk_y, vo_x, three, merge_grad, m1 = fold(
        where,
        [
            ([[(a, ()) for a in (ends, ends_z)]], [(f32, ())]),
            ([[(a, (None, 0, 1) + none2) for a in (p0, qk_c)] + [(qk_x, (None, 1) + none2)]], [(bf16, ())]),
            ([[(a, (None, 1, 0) + none2) for a in (vo0, vo_c)] + [(vo_y, (None, 1) + none2)]], [(bf16, ())]),
            ([[(three, ()), (three_c, ())]], [(f32, ())]),
        ],
        (merge_grad, m1),
    )
    qk_y, vo_x, m_c, three_x = swap(qk_y, "y"), swap(vo_x, "x"), swap(m1, "c"), swap_line(three, 1)
    grad_tokens, grad_shortcut = merge_backward(where, merge_grad, gathered, r, ())
    four_pieces = [
        [(a, (i, 0, 0) + none2) for a in (p0, qk_c)] + [(qk_x, (i, 0) + none2), (qk_y, (i,) + none2)]
        for i in BITS
    ] + [
        [(a, (i, 0, 0) + none2) for a in (vo0, vo_c)] + [(vo_y, (i, 0) + none2), (vo_x, (i,) + none2)]
        for i in BITS
    ]
    four, four_z, l_x, r_y, three, grad_tokens = fold(
        where,
        [
            (four_pieces, by_lo),
            ([[(a, (0, 1) + none3) for a in (m0, m_c)]], [(bf16, ())]),
            ([[(a, (1, None, 1) + none2) for a in (m0, m_c)]], [(bf16, ())]),
            ([[(three, ()), (three_x, ())]], [(f32, ())]),
        ],
        (grad_tokens,),
    )
    l_x, r_y, three_y, four_z = swap(l_x, "x"), swap(r_y, "y"), swap_line(three, 2), swap_line(four_z, 1)
    l_y, r_x, three, four, four_z = fold(
        where,
        [
            ([[(a, (0, 0, 1) + none2) for a in (m0, m_c)] + [(l_x, (1,) + none2)]], [(bf16, ())]),
            ([[(a, (1, 1, 0) + none2) for a in (m0, m_c)] + [(r_y, (1,) + none2)]], [(bf16, ())]),
            ([[(three, ()), (three_y, ())]], [(f32, ())]),
            ([[(a, (None,)) for a in (four, four_z)]], by_hi),
        ],
    )
    l_y, r_x, three_z, four_z = swap(l_y, "y"), swap(r_x, "x"), swap(three, "x"), swap_line(four_z, 2)
    grad_merge, merge_z, three = fold(
        where,
        [
            (
                [
                    [(a, (0, 0, 0) + none2) for a in (m0, m_c)] + [(l_x, (0,) + none2), (l_y, none2)],
                    [(a, (1, 0, 0) + none2) for a in (m0, m_c)] + [(r_y, (0,) + none2), (r_x, none2)],
                ],
                by_lo,
            ),
            ([[(a, ()) for a in (three, three_z)]], [(f32, ())]),
        ],
    )
    merge_z, three_z = swap_line(merge_z, 1), swap(three, "y")
    grad_merge, merge_z, four, three = fold(
        where,
        [
            ([[(a, (None,)) for a in (grad_merge, merge_z)]], by_hi),
            ([[(a, ()) for a in (four, four_z)]], [(f32, ())]),
            ([[(a, ()) for a in (three, three_z)]], [(f32, ())]),
        ],
    )
    grad_merge = plus(grad_merge, swap_line(merge_z, 2))
    own = jnp.sum(parcel, axis=0)
    grad_expand, grad_contract = ends[:, :half], ends[:, half:]
    grad_query, grad_key, grad_value, grad_result = (four[:, i * col : (i + 1) * col] for i in range(4))

    share = d // count
    three = lax.dynamic_slice_in_dim(three, device * share, share, 1)
    four_rows = lax.dynamic_slice_in_dim(own[:4], device * share, share, 1)
    loss_value = own[4, 0] / (own[5, 0] * d)
    share = 2 * half // count
    hidden_row = lax.dynamic_slice_in_dim(own[8:12].reshape(-1), device * share, share, 0)
    sums = (three[2], three[0], three[1], four_rows[2], four_rows[0], four_rows[1], four_rows[3], hidden_row)
    return (
        block_out,
        loss_value,
        grad_tokens,
        grad_shortcut,
        grad_merge,
        sums[0],
        sums[1],
        sums[2],
        grad_query,
        grad_key,
        grad_value,
        grad_result.T,
        sums[3],
        sums[4],
        sums[5],
        grad_expand,
        sums[7],
        grad_contract.T,
        sums[6],
    )


ARGUMENTS = (
    ("ft", None),
    ("ft", None),
    ("ft", None),
    ("f",),
    ("ft", None),
    ("ft",),
    ("ft",),
    ("ft",),
    ("f", "t"),
    ("f", "t"),
    ("f", "t"),
    ("t", "f"),
    ("ft",),
    ("ft",),
    ("ft",),
    ("f", "t"),
    ("ft",),
    ("t", "f"),
    ("ft",),
)
RESULTS = (
    ("ft", None),
    (),
    ("ft", None),
    ("ft", None),
    ("ft", None),
    ("ft",),
    ("ft",),
    ("ft",),
    ("f", "t"),
    ("f", "t"),
    ("f", "t"),
    ("t", "f"),
    ("ft",),
    ("ft",),
    ("ft",),
    ("f", "t"),
    ("ft",),
    ("t", "f"),
    ("ft",),
)


def solution(mesh):
    def whole(*args):
        rows = args[0].shape[0] // mesh.size
        if rows == SEQ_LEN and dict(mesh.shape) == {"fsdp": 16, "tp": 2}:
            plan = one_sequence_plan
            use = jax.sharding.Mesh(mesh.devices.reshape(4, 2, 2, 2), ("z", "y", "c", "x"))
            names = {"f": ("z", "y", "c"), "t": ("x",), "ft": ("z", "y", "c", "x")}
        else:
            plan = per_device_split
            use = mesh
            names = {"f": ("fsdp",), "t": ("tp",), "ft": ("fsdp", "tp")}

        def place(entry):
            return P(*(None if e is None else names[e] for e in entry))

        return jax.shard_map(
            plan,
            mesh=use,
            in_specs=tuple(place(e) for e in ARGUMENTS),
            out_specs=tuple(place(e) for e in RESULTS),
            check_vma=False,
        )(*args)

    return whole
```

profile of v0, /device:TPU:0, one launch (start us, length us, event | category | flops | bytes accessed | tf_op | source)
XLA Modules:
  0.0 613.1 jit_solution(12536943673162750970)
XLA Ops:
  7.2 5.4 concatenate.14
  12.7 1.8 pad_maximum_fusion
  15.4 4.1 collective-permute-start
  20.1 16.3 %collective-permute-done.refs_1_ = bf16[64,2048]{1,0:T(8,128)(2,1)S(1)} collective-permute-done((bf16[64,2048]{1,0:T(8,128)(2,1)}, bf16[64,2048]{1,0:T(8,128)(2,1)S(1)}, u32[]{:S(2)}, u32[]{:S(2)}) %collective-permute-start) | collective-permute-done | bytes 262176 | tf_op jit(solution)/shard_map/ppermute | solution.py:1111
  37.0 2.5 pile.3.refs_0_
  39.6 3.4 collective-permute-start.1
  43.0 23.0 %collective-permute-done.1.refs_1_ = bf16[2,64,2048]{2,1,0:T(8,128)(2,1)S(1)} collective-permute-done((bf16[2,64,2048]{2,1,0:T(8,128)(2,1)}, bf16[2,64,2048]{2,1,0:T(8,128)(2,1)S(1)}, u32[]{:S(2)}, u32[]{:S(2)}) %collective-permute-start.1) | collective-permute-done | bytes 524320 | tf_op jit(solution)/shard_map/ppermute | solution.py:1111
  66.7 2.9 pile.4.refs_0_
  69.6 1.4 collective-permute-start.2
  71.0 31.6 %collective-permute-done.2.refs_1_ = bf16[2,2,64,2048]{3,2,1,0:T(8,128)(2,1)S(1)} collective-permute-done((bf16[2,2,64,2048]{3,2,1,0:T(8,128)(2,1)}, bf16[2,2,64,2048]{3,2,1,0:T(8,128)(2,1)S(1)}, u32[]{:S(2)}, u32[]{:S(2)}) %collective-permute-start.2) | collective-permute-done | bytes 1048608 | tf_op jit(solution)/shard_map/ppermute | solution.py:1107
  103.7 3.6 pile.5.refs_1_.refs_2_.refs_5_
  107.3 2.3 collective-permute-start.4
  109.6 26.3 %all-gather.7.cloned.1.call-done = bf16[6400,1024]{1,0:T(8,128)(2,1)} async-done(((bf16[200,1024]{1,0:T(8,128)(2,1)}), bf16[6400,1024]{1,0:T(8,128)(2,1)}) %all-gather.7.cloned.1.call-update) | async-done | bytes 13107216 | tf_op jit(solution)/shard_map/all_gather | solution.py:1181
  138.6 9.8 %merge_forward.1.refs_0_ = f32[1104,1024]{1,0:T(8,128)} custom-call(s32[5]{0:T(128)} %stack.23.where_ref, bf16[1104,1024]{1,0:T(8,128)(2,1)} %refs_0_.5, bf16[1104,1024]{1,0:T(8,128)(2,1)} %refs_1_.3, bf16[2,2,2,2,2,200,1024]{6,5,4,3,2,1,0:T(8,128)(2,1)} %gate.3.refs_2_.refs_3_.refs_1_), custom_call_target="tpu_custom_call" | custom-call | tf_op jit(solution)/shard_map/merge_forward/pallas_call | solution.py:449
  148.4 16.1 %project_forward.1 = (f32[1104,1024]{1,0:T(8,128)}, bf16[1104,1024]{1,0:T(8,128)(2,1)}, bf16[1104,3072]{1,0:T(8,128)(2,1)}) custom-call(s32[5]{0:T(128)} %stack.23.where_ref, f32[1104,1024]{1,0:T(8,128)} %merge_forward.1.refs_0_, f32[8,1024]{1,0:T(8,128)} %pad.9.refs_1_.refs_2_.refs_4_, bf16[2,2,2,2,2,200,1024]{6,5,4,3,2,1,0:T(8,128)(2,1)} %gate.3.refs_2_.refs_3_.refs_1_), custom_call_target="tpu_custom_call" | custom-call | tf_op jit(solution)/shard_map/project_forward/pallas_call | solution.py:449
  164.5 1.3 copy-done.2
  168.8 31.6 %attention_forward.1 = (bf16[1104,1024]{1,0:T(8,128)(2,1)}, f32[1104,1024]{1,0:T(8,128)}) custom-call(s32[5]{0:T(128)} %stack.23.where_ref, bf16[1104,3072]{1,0:T(8,128)(2,1)} %get-tuple-element.111.refs_0_.refs_1_.refs_2_, bf16[1104,3072]{1,0:T(8,128)(2,1)} %get-tuple-element.111.refs_0_.refs_1_.refs_2_, ...), custom_call_target="tpu_custom_call" | custom-call | tf_op jit(solution)/shard_map/attention_forward/pallas_call | solution.py:449
  200.4 1.4 copy-done.3
  202.4 10.4 %result_forward.1 = (f32[1104,1024]{1,0:T(8,128)}, bf16[1104,1024]{1,0:T(8,128)(2,1)}) custom-call(s32[5]{0:T(128)} %stack.23.where_ref, bf16[1104,1024]{1,0:T(8,128)(2,1)} %get-tuple-element.114.refs_0_.refs_1_.refs_3_, f32[1104,1024]{1,0:T(8,128)} %get-tuple-element.115.refs_1_.refs_0_, f32[8,1024]{1,0:T(8,128)} %pad.9.refs_1_.refs_2_.refs_4_, ...), custom_call_target="tpu_custom_call" | custom-call | tf_op jit(solution)/shard_map/result_forward/pallas_call | solution.py:449
  212.8 30.0 %expand_forward.1 = (bf16[2,1104,2048]{2,1,0:T(8,128)(2,1)}, bf16[2,1104,2048]{2,1,0:T(8,128)(2,1)}) custom-call(s32[5]{0:T(128)} %stack.23.where_ref, bf16[1104,1024]{1,0:T(8,128)(2,1)} %get-tuple-element.116.refs_0_.refs_1_, f32[2,1,2048]{2,1,0:T(1,128)} %bitcast.51, bf16[2,2,2,64,2048]{4,3,2,1,0:T(8,128)(2,1)} %pile.5.refs_1_.refs_2_.refs_5_, ...), custom_call_target="tpu_custom_call" | custom-call | tf_op jit(solution)/shard_map/expand_forward/pallas_call | solution.py:449
  242.7 18.9 %contract_forward.1 = (bf16[1104,1024]{1,0:T(8,128)(2,1)}, bf16[1104,1024]{1,0:T(8,128)(2,1)}, f32[8,1024]{1,0:T(8,128)}, f32[8,128]{1,0:T(8,128)}) custom-call(s32[5]{0:T(128)} %stack.23.where_ref, f32[1]{0:T(128)S(6)} %convert_element_type.16.refs_0_.refs_7_, bf16[2,1104,2048]{2,1,0:T(8,128)(2,1)} %get-tuple-element.119.refs_1_.refs_2_, ...), custom_call_target="tpu_custom_call" | custom-call | tf_op jit(solution)/shard_map/contract_forward/pallas_call | solution.py:449
  261.7 29.9 %feed_backward.2 = (bf16[1104,1024]{1,0:T(8,128)(2,1)}, bf16[2,2,2,64,2048]{4,3,2,1,0:T(8,128)(2,1)}, bf16[2,2,2,64,2048]{4,3,2,1,0:T(8,128)(2,1)}, bf16[2,2,2,6...) custom-call(s32[5]{0:T(128)} %stack.23.where_ref, ...), custom_call_target="tpu_custom_call" | custom-call | tf_op jit(solution)/shard_map/feed_backward/pallas_call | solution.py:449
  292.1 29.5 %feed_backward.3 = (bf16[1104,1024]{1,0:T(8,128)(2,1)}, bf16[2,2,2,64,2048]{4,3,2,1,0:T(8,128)(2,1)}, bf16[2,2,2,64,2048]{4,3,2,1,0:T(8,128)(2,1)}, bf16[2,2,2,6...) custom-call(s32[5]{0:T(128)} %stack.23.where_ref, ...), custom_call_target="tpu_custom_call" | custom-call | tf_op jit(solution)/shard_map/feed_backward/pallas_call | solution.py:449
  321.6 1.4 copy-done.7
  323.0 5.6 fold.11
  329.2 10.9 %norm_backward.2 = (f32[1104,1024]{1,0:T(8,128)}, bf16[1104,1024]{1,0:T(8,128)(2,1)}, f32[16,1024]{1,0:T(8,128)}) custom-call(s32[5]{0:T(128)} %stack.23.where_ref, f32[1104,1024]{1,0:T(8,128)} %get-tuple-element.120.refs_2_.refs_0_, bf16[1104,1024]{1,0:T(8,128)(2,1)} %get-tuple-element.122.refs_0_.refs_1_, f32[8,1024]{1,0:T(8,128)} %pad.9.refs_1_.refs_2_.refs_4_, ...), custom_call_target="tpu_custom_call" | custom-call | tf_op jit(solution)/shard_map/norm_backward/pallas_call | solution.py:449
  340.1 1.5 collective-permute-start.9
  341.6 1.7 collective-permute-start.10
  343.3 1.3 copy-done.4
  344.6 3.4 fold.12
  348.3 9.5 %result_backward.1 = (bf16[1104,1024]{1,0:T(8,128)(2,1)}, bf16[2,2,2,2,2,64,512]{6,5,4,3,2,1,0:T(8,128)(2,1)}, bf16[2,2,2,2,2,64,512]{6,5,4,3,2,1,0:T(8,128)(2,1)}) custom-call(s32[5]{0:T(128)} %stack.23.where_ref, bf16[1104,1024]{1,0:T(8,128)(2,1)} %get-tuple-element.147.refs_0_, bf16[1104,1024]{1,0:T(8,128)(2,1)} %get-tuple-element.114.refs_0_.refs_1_.refs_3_, ...), custom_call_target="tpu_custom_call" | custom-call | tf_op jit(solution)/shard_map/result_backward/pallas_call | solution.py:449
  357.8 34.5 %attention_backward.2.refs_6_ = bf16[3,1104,1024]{2,1,0:T(8,128)(2,1)} custom-call(s32[5]{0:T(128)} %stack.23.where_ref, bf16[1104,3072]{1,0:T(8,128)(2,1)} %get-tuple-element.111.refs_0_.refs_1_.refs_2_, bf16[1104,3072]{1,0:T(8,128)(2,1)} %get-tuple-element.111.refs_0_.refs_1_.refs_2_, bf16[1104,3072]{1,0:T(8,128)(2,1)} %get-tuple-element.111.refs_0_.refs_1_.refs_2_, ...), custom_call_target="tpu_custom_call" | custom-call | tf_op jit(solution)/shard_map/attention_backward/pallas_call | solution.py:449
  394.8 5.2 fold.13
  400.0 2.4 collective-permute-start.13
  402.9 34.4 %attention_backward.3.refs_8_ = bf16[3,1104,1024]{2,1,0:T(8,128)(2,1)} custom-call(s32[5]{0:T(128)} %stack.23.where_ref, bf16[1104,3072]{1,0:T(8,128)(2,1)} %get-tuple-element.111.refs_0_.refs_1_.refs_2_, bf16[1104,3072]{1,0:T(8,128)(2,1)} %get-tuple-element.111.refs_0_.refs_1_.refs_2_, ...), custom_call_target="tpu_custom_call", output_to_operand_aliasing={{}: (7, {})} | custom-call | tf_op jit(solution)/shard_map/attention_backward/pallas_call | solution.py:449
  438.7 6.7 %fold.14 = (f32[2,64,4096]{2,1,0:T(8,128)}, bf16[2,64,4096]{2,1,0:T(8,128)(2,1)}, bf16[3,1104,1024]{2,1,0:T(8,128)(2,1)}) custom-call(s32[5]{0:T(128)} %stack.23.where_ref, bf16[2,2,2,64,2048]{4,3,2,1,0:T(8,128)(2,1)} %get-tuple-element.139.refs_0_, bf16[2,2,2,64,2048]{4,3,2,1,0:T(8,128)(2,1)} %copy-done.4, ...), custom_call_target="tpu_custom_call", output_to_operand_aliasing={{2}: (9, {})} | custom-call | tf_op jit(solution)/shard_map/fold/pallas_call | solution.py:449
  445.4 5.7 collective-permute-start.17
  451.0 14.4 %project_backward.1.refs_2_ = bf16[1104,1024]{1,0:T(8,128)(2,1)} custom-call(s32[5]{0:T(128)} %stack.23.where_ref, bf16[3,1104,1024]{2,1,0:T(8,128)(2,1)} %get-tuple-element.153.refs_1_.refs_0_, bf16[2,2,2,2,2,200,1024]{6,5,4,3,2,1,0:T(8,128)(2,1)} %gate.3.refs_2_.refs_3_.refs_1_), custom_call_target="tpu_custom_call" | custom-call | tf_op jit(solution)/shard_map/project_backward/pallas_call | solution.py:449
  465.5 14.4 %project_weight.1 = (bf16[2,2,2,2,2,64,512]{6,5,4,3,2,1,0:T(8,128)(2,1)}, bf16[2,2,2,2,2,64,512]{6,5,4,3,2,1,0:T(8,128)(2,1)}, bf16[2,2,2,2,2,64,512]{6,5,4,3,2,...) custom-call(s32[5]{0:T(128)} %stack.23.where_ref, ...), custom_call_target="tpu_custom_call", output_to_operand_aliasing={{2}: (3, {}), {3}: (4, {})} | custom-call | tf_op jit(solution)/shard_map/project_weight/pallas_call | solution.py:449
  481.4 3.8 fold.15
  485.2 1.9 collective-permute-done.15.refs_1_.refs_3_.refs_5_
  488.5 4.6 fold.16
  495.1 8.9 %norm_backward.3 = (bf16[1104,1024]{1,0:T(8,128)(2,1)}, f32[8,1024]{1,0:T(8,128)}) custom-call(s32[5]{0:T(128)} %stack.23.where_ref, f32[1104,1024]{1,0:T(8,128)} %get-tuple-element.115.refs_1_.refs_0_, f32[1104,1024]{1,0:T(8,128)} %get-tuple-element.167.refs_1_, f32[8,1024]{1,0:T(8,128)} %pad.9.refs_1_.refs_2_.refs_4_, ...), custom_call_target="tpu_custom_call" | custom-call | tf_op jit(solution)/shard_map/norm_backward/pallas_call | solution.py:449
  504.0 10.7 %merge_weight.1 = (bf16[2,2,2,2,2,64,512]{6,5,4,3,2,1,0:T(8,128)(2,1)}, bf16[2,2,2,2,2,64,512]{6,5,4,3,2,1,0:T(8,128)(2,1)}) custom-call(s32[5]{0:T(128)} %stack.23.where_ref, bf16[1104,1024]{1,0:T(8,128)(2,1)} %refs_0_.5, bf16[1104,1024]{1,0:T(8,128)(2,1)} %refs_1_.3, bf16[1104,1024]{1,0:T(8,128)(2,1)} %get-tuple-element.170.refs_2_.refs_10_), custom_call_target="tpu_custom_call" | custom-call | tf_op jit(solution)/shard_map/merge_weight/pallas_call | solution.py:449
  514.7 4.8 collective-permute-done.19.refs_1_
  521.0 4.6 fold.17
  525.6 1.8 collective-permute-start.22
  528.7 9.5 %merge_backward.1 = (f32[1104,1024]{1,0:T(8,128)}, f32[1104,1024]{1,0:T(8,128)}) custom-call(s32[5]{0:T(128)} %stack.23.where_ref, bf16[1104,1024]{1,0:T(8,128)(2,1)} %get-tuple-element.177.refs_0_, bf16[2,2,2,2,2,200,1024]{6,5,4,3,2,1,0:T(8,128)(2,1)} %gate.3.refs_2_.refs_3_.refs_1_), custom_call_target="tpu_custom_call" | custom-call | tf_op jit(solution)/shard_map/merge_backward/pallas_call | solution.py:449
  538.2 1.9 collective-permute-done.22.refs_3_.refs_7_
  540.1 1.4 collective-permute-done.23.refs_11_.refs_15_
  543.1 5.2 fold.18
  548.3 1.3 collective-permute-start.26
  550.1 1.7 reduce_sum.9
  551.9 2.7 collective-permute-start.28
  554.6 7.1 %collective-permute-done.28.refs_7_ = f32[8,1024]{1,0:T(8,128)S(1)} collective-permute-done((f32[8,1024]{1,0:T(8,128)S(1)}, f32[8,1024]{1,0:T(8,128)S(1)}, u32[]{:S(2)}, u32[]{:S(2)}) %collective-permute-start.28) | collective-permute-done | bytes 32800 | tf_op jit(solution)/shard_map/ppermute | solution.py:1111
  564.8 3.7 fold.19
  574.7 1.5 collective-permute-start.34
  578.1 3.2 fold.20
  584.5 2.3 collective-permute-done.34.refs_3_
  586.8 4.2 collective-permute-done.33.refs_1_
  591.7 3.0 fold.21
  596.0 1.9 slice_bitcast_fusion.1
  598.4 4.9 collective-permute-done.36
  603.3 1.7 convert_add_fusion
  (149 shorter events, 40.5 us)
Async XLA Ops:
  7.2 128.7 %all-gather.7.cloned.1.call-start = ((), (), s32[]{:S(2)}) async-start(), calls=%async_computation | async-start | bytes 13516800 | tf_op jit(solution)/shard_map/all_gather | solution.py:1181
  14.6 228.2 %all-gather.9.cloned.1.call-start = ((), (), s32[]{:S(2)}) async-start(), calls=%async_computation.1 | async-start | bytes 8650752 | tf_op jit(solution)/shard_map/all_gather | solution.py:1184
  15.3 422.0 %all-gather.11.cloned.1.call-start = ((), (), s32[]{:S(2)}) async-start(), calls=%async_computation.2 | async-start | bytes 2162688 | tf_op jit(solution)/shard_map/all_gather | solution.py:1237
  15.4 21.0 %collective-permute-start = (bf16[64,2048]{1,0:T(8,128)(2,1)}, bf16[64,2048]{1,0:T(8,128)(2,1)S(1)}, u32[]{:S(2)}, u32[]{:S(2)}) collective-permute-start(bf16[64,2048]{1,0:T(8,128)(2,1)} %refs_0_.3), channel_id=1, source_target_pairs={{0,16},{8,24},{16,0},{24,8},{1,17},{9,25},{17,1},{25,9},{2,18},{10... | collective-permute-start | bytes 786440 | tf_op jit(solution)/shard_map/ppermute | solution.py:1111
  39.6 26.4 %collective-permute-start.1 = (bf16[2,64,2048]{2,1,0:T(8,128)(2,1)}, bf16[2,64,2048]{2,1,0:T(8,128)(2,1)S(1)}, u32[]{:S(2)}, u32[]{:S(2)}) collective-permute-start(bf16[2,64,2048]{2,1,0:T(8,128)(2,1)} %pile.3.refs_0_), channel_id=1, source_target_pairs={{0,8},{8,0},{16,24},{24,16},{1,9},{9,1},{17,25},{25,17},{2,10},{10... | collective-permute-start | bytes 1572872 | tf_op jit(solution)/shard_map/ppermute | solution.py:1111
  69.6 33.0 %collective-permute-start.2 = (bf16[2,2,64,2048]{3,2,1,0:T(8,128)(2,1)}, bf16[2,2,64,2048]{3,2,1,0:T(8,128)(2,1)S(1)}, u32[]{:S(2)}, u32[]{:S(2)}) collective-permute-start(bf16[2,2,64,2048]{3,2,1,0:T(8,128)(2,1)} %pile.4.refs_0_), channel_id=1, source_target_pairs={{0,4},{4,0},{1,5},{5,1},{2,6},{6,2},{3,7},{7,3},{8,12},{12,8},{9,1... | collective-permute-start | bytes 3145736 | tf_op jit(solution)/shard_map/ppermute | solution.py:1107
  107.3 57.2 %collective-permute-start.4 = (bf16[2,2,2,64,2048]{4,3,2,1,0:T(8,128)(2,1)}, bf16[2,2,2,64,2048]{4,3,2,1,0:T(8,128)(2,1)S(1)}, u32[]{:S(2)}, u32[]{:S(2)}) collective-permute-start(bf16[2,2,2,64,2048]{4,3,2,1,0:T(8,128)(2,1)} %pile.5.refs_1_.refs_2_.refs_5_), channel_id=1, source_target_pairs={{0,1},{1,0},{2,3},{3,2},{4,5},{5,4},{6,7},{7,6},{8,9},{9,8},{10,11... | collective-permute-start | bytes 6291464 | tf_op jit(solution)/shard_map/ppermute | solution.py:1107
  109.6 90.7 %collective-permute-start.3 = (bf16[2,2,2,64,2048]{4,3,2,1,0:T(8,128)(2,1)}, bf16[2,2,2,64,2048]{4,3,2,1,0:T(8,128)(2,1)}, u32[]{:S(2)}, u32[]{:S(2)}) collective-permute-start(bf16[2,2,2,64,2048]{4,3,2,1,0:T(8,128)(2,1)} %pile.5.refs_1_.refs_2_.refs_5_), channel_id=1, source_target_pairs={{0,2},{2,0},{1,3},{3,1},{4,6},{6,4},{5,7},{7,5},{8,10},{10,8},{9,1... | collective-permute-start | bytes 6291464 | tf_op jit(solution)/shard_map/ppermute | solution.py:1107
  164.5 1.3 copy-start.2
  165.8 1.1 copy-start.34
  166.6 33.8 %collective-permute-start.5 = (bf16[2,2,2,64,2048]{4,3,2,1,0:T(8,128)(2,1)}, bf16[2,2,2,64,2048]{4,3,2,1,0:T(8,128)(2,1)S(1)}, u32[]{:S(2)}, u32[]{:S(2)}) collective-permute-start(bf16[2,2,2,64,2048]{4,3,2,1,0:T(8,128)(2,1)} %get-tuple-element.110.refs_4_.refs_5_), channel_id=1, source_target_pairs={{0,2},{2,0},{1,3},{3,1},{4,6},{6,4},{5,7},{7,5},{8,10},{10,8},{9,1... | collective-permute-start | bytes 6291464 | tf_op jit(solution)/shard_map/ppermute | solution.py:1107
  200.4 1.4 copy-start.3
  291.6 30.0 %collective-permute-start.6 = (bf16[2,2,2,64,2048]{4,3,2,1,0:T(8,128)(2,1)}, bf16[2,2,2,64,2048]{4,3,2,1,0:T(8,128)(2,1)}, u32[]{:S(2)}, u32[]{:S(2)}) collective-permute-start(bf16[2,2,2,64,2048]{4,3,2,1,0:T(8,128)(2,1)} %get-tuple-element.125), channel_id=1, source_target_pairs={{0,2},{2,0},{1,3},{3,1},{4,6},{6,4},{5,7},{7,5},{8,10},{10,8},{9,1... | collective-permute-start | bytes 6291464 | tf_op jit(solution)/shard_map/ppermute | solution.py:1107
  291.9 29.7 %collective-permute-start.7 = (bf16[2,2,2,64,2048]{4,3,2,1,0:T(8,128)(2,1)}, bf16[2,2,2,64,2048]{4,3,2,1,0:T(8,128)(2,1)S(1)}, u32[]{:S(2)}, u32[]{:S(2)}) collective-permute-start(bf16[2,2,2,64,2048]{4,3,2,1,0:T(8,128)(2,1)} %get-tuple-element.127), channel_id=1, source_target_pairs={{0,2},{2,0},{1,3},{3,1},{4,6},{6,4},{5,7},{7,5},{8,10},{10,8},{9,1... | collective-permute-start | bytes 6291464 | tf_op jit(solution)/shard_map/ppermute | solution.py:1107
  321.6 1.4 copy-start.7
  328.7 14.6 %collective-permute-start.8 = (bf16[2,2,2,64,2048]{4,3,2,1,0:T(8,128)(2,1)}, bf16[2,2,2,64,2048]{4,3,2,1,0:T(8,128)(2,1)S(1)}, u32[]{:S(2)}, u32[]{:S(2)}) collective-permute-start(bf16[2,2,2,64,2048]{4,3,2,1,0:T(8,128)(2,1)} %get-tuple-element.140), channel_id=1, source_target_pairs={{0,2},{2,0},{1,3},{3,1},{4,6},{6,4},{5,7},{7,5},{8,10},{10,8},{9,1... | collective-permute-start | bytes 6291464 | tf_op jit(solution)/shard_map/ppermute | solution.py:1107
  329.0 14.3 %collective-permute-start.11 = (bf16[2,2,2,64,2048]{4,3,2,1,0:T(8,128)(2,1)}, bf16[2,2,2,64,2048]{4,3,2,1,0:T(8,128)(2,1)}, u32[]{:S(2)}, u32[]{:S(2)}) collective-permute-start(bf16[2,2,2,64,2048]{4,3,2,1,0:T(8,128)(2,1)} %get-tuple-element.145), channel_id=1, source_target_pairs={{0,2},{2,0},{1,3},{3,1},{4,6},{6,4},{5,7},{7,5},{8,10},{10,8},{9,1... | collective-permute-start | bytes 6291464 | tf_op jit(solution)/shard_map/ppermute | solution.py:1107
  340.1 52.5 %collective-permute-start.9 = (bf16[2,2,2,64,2048]{4,3,2,1,0:T(8,128)(2,1)}, bf16[2,2,2,64,2048]{4,3,2,1,0:T(8,128)(2,1)}, u32[]{:S(2)}, u32[]{:S(2)}) collective-permute-start(bf16[2,2,2,64,2048]{4,3,2,1,0:T(8,128)(2,1)} %get-tuple-element.141), channel_id=1, source_target_pairs={{0,1},{1,0},{2,3},{3,2},{4,5},{5,4},{6,7},{7,6},{8,9},{9,8},{10,11... | collective-permute-start | bytes 6291464 | tf_op jit(solution)/shard_map/ppermute | solution.py:1107
  341.6 50.8 %collective-permute-start.10 = (bf16[2,2,64,2048]{3,2,1,0:T(8,128)(2,1)}, bf16[2,2,64,2048]{3,2,1,0:T(8,128)(2,1)S(1)}, u32[]{:S(2)}, u32[]{:S(2)}) collective-permute-start(bf16[2,2,64,2048]{3,2,1,0:T(8,128)(2,1)} %get-tuple-element.142), channel_id=1, source_target_pairs={{0,4},{4,0},{1,5},{5,1},{2,6},{6,2},{3,7},{7,3},{8,12},{12,8},{9,1... | collective-permute-start | bytes 3145736 | tf_op jit(solution)/shard_map/ppermute | solution.py:1107
  343.3 1.3 copy-start.4
  348.0 45.8 %collective-permute-start.12 = (bf16[2,2,64,2048]{3,2,1,0:T(8,128)(2,1)}, bf16[2,2,64,2048]{3,2,1,0:T(8,128)(2,1)S(1)}, u32[]{:S(2)}, u32[]{:S(2)}) collective-permute-start(bf16[2,2,64,2048]{3,2,1,0:T(8,128)(2,1)} %get-tuple-element.149), channel_id=1, source_target_pairs={{0,4},{4,0},{1,5},{5,1},{2,6},{6,2},{3,7},{7,3},{8,12},{12,8},{9,1... | collective-permute-start | bytes 3145736 | tf_op jit(solution)/shard_map/ppermute | solution.py:1107
  392.4 1.4 copy-start.13
  393.8 1.0 copy-start.8
  400.0 37.3 %collective-permute-start.13 = (bf16[2,2,64,2048]{3,2,1,0:T(8,128)(2,1)}, bf16[2,2,64,2048]{3,2,1,0:T(8,128)(2,1)S(1)}, u32[]{:S(2)}, u32[]{:S(2)}) collective-permute-start(bf16[2,2,64,2048]{3,2,1,0:T(8,128)(2,1)} %get-tuple-element.150), channel_id=1, source_target_pairs={{0,4},{4,0},{1,5},{5,1},{2,6},{6,2},{3,7},{7,3},{8,12},{12,8},{9,1... | collective-permute-start | bytes 3145736 | tf_op jit(solution)/shard_map/ppermute | solution.py:1107
  402.4 35.0 %collective-permute-start.14 = (bf16[2,2,64,2048]{3,2,1,0:T(8,128)(2,1)}, bf16[2,2,64,2048]{3,2,1,0:T(8,128)(2,1)S(1)}, u32[]{:S(2)}, u32[]{:S(2)}) collective-permute-start(bf16[2,2,64,2048]{3,2,1,0:T(8,128)(2,1)} %get-tuple-element.151), channel_id=1, source_target_pairs={{0,1},{1,0},{2,3},{3,2},{4,5},{5,4},{6,7},{7,6},{8,9},{9,8},{10,11... | collective-permute-start | bytes 3145736 | tf_op jit(solution)/shard_map/ppermute | solution.py:1107
  437.3 1.0 copy-start.14
  437.4 1.3 copy-start.15
  445.4 35.0 %collective-permute-start.17 = (bf16[2,64,4096]{2,1,0:T(8,128)(2,1)}, bf16[2,64,4096]{2,1,0:T(8,128)(2,1)S(1)}, u32[]{:S(2)}, u32[]{:S(2)}) collective-permute-start(bf16[2,64,4096]{2,1,0:T(8,128)(2,1)} %get-tuple-element.161), channel_id=1, source_target_pairs={{0,8},{8,0},{16,24},{24,16},{1,9},{9,1},{17,25},{25,17},{2,10},{10... | collective-permute-start | bytes 3145736 | tf_op jit(solution)/shard_map/ppermute | solution.py:1111
  479.9 7.2 %collective-permute-start.15 = (bf16[2,2,2,2,2,64,512]{6,5,4,3,2,1,0:T(8,128)(2,1)}, bf16[2,2,2,2,2,64,512]{6,5,4,3,2,1,0:T(8,128)(2,1)S(1)}, u32[]{:S(2)}, u32[]{:S(2)}) collective-permute-start(bf16[2,2,2,2,2,64,512]{6,5,4,3,2,1,0:T(8,128)(2,1)} %get-tuple-element.157), channel_id=1, source_target_pairs={{0,2},{2,0},{1,3},{3,1},{4,6},{6,4},{5,7},{7,5},{8,10},{10,8},{9,1... | collective-permute-start | bytes 6291464 | tf_op jit(solution)/shard_map/ppermute | solution.py:1107
  479.9 7.5 %collective-permute-start.16 = (bf16[2,2,2,2,2,64,512]{6,5,4,3,2,1,0:T(8,128)(2,1)}, bf16[2,2,2,2,2,64,512]{6,5,4,3,2,1,0:T(8,128)(2,1)}, u32[]{:S(2)}, u32[]{:S(2)}) collective-permute-start(bf16[2,2,2,2,2,64,512]{6,5,4,3,2,1,0:T(8,128)(2,1)} %get-tuple-element.159), channel_id=1, source_target_pairs={{0,2},{2,0},{1,3},{3,1},{4,6},{6,4},{5,7},{7,5},{8,10},{10,8},{9,1... | collective-permute-start | bytes 6291464 | tf_op jit(solution)/shard_map/ppermute | solution.py:1107
  480.4 1.0 copy-start.32
  487.1 1.4 copy-start.1
  488.5 5.6 copy-start.33
  493.1 26.4 %collective-permute-start.18 = (bf16[2,2,2,2,64,512]{5,4,3,2,1,0:T(8,128)(2,1)}, bf16[2,2,2,2,64,512]{5,4,3,2,1,0:T(8,128)(2,1)S(1)}, u32[]{:S(2)}, u32[]{:S(2)}) collective-permute-start(bf16[2,2,2,2,64,512]{5,4,3,2,1,0:T(8,128)(2,1)} %get-tuple-element.163), channel_id=1, source_target_pairs={{0,1},{1,0},{2,3},{3,2},{4,5},{5,4},{6,7},{7,6},{8,9},{9,8},{10,11... | collective-permute-start | bytes 3145736 | tf_op jit(solution)/shard_map/ppermute | solution.py:1107
  493.8 25.7 %collective-permute-start.20 = (bf16[2,2,2,2,64,512]{5,4,3,2,1,0:T(8,128)(2,1)}, bf16[2,2,2,2,64,512]{5,4,3,2,1,0:T(8,128)(2,1)S(1)}, u32[]{:S(2)}, u32[]{:S(2)}) collective-permute-start(bf16[2,2,2,2,64,512]{5,4,3,2,1,0:T(8,128)(2,1)} %get-tuple-element.166), channel_id=1, source_target_pairs={{0,4},{4,0},{1,5},{5,1},{2,6},{6,2},{3,7},{7,3},{8,12},{12,8},{9,1... | collective-permute-start | bytes 3145736 | tf_op jit(solution)/shard_map/ppermute | solution.py:1107
  494.1 25.3 %collective-permute-start.19 = (bf16[64,4096]{1,0:T(8,128)(2,1)S(1)}, bf16[64,4096]{1,0:T(8,128)(2,1)S(1)}, u32[]{:S(2)}, u32[]{:S(2)}) collective-permute-start(bf16[64,4096]{1,0:T(8,128)(2,1)S(1)} %copy-done.33), channel_id=1, source_target_pairs={{0,16},{8,24},{16,0},{24,8},{1,17},{9,25},{17,1},{25,9},{2,18},{10... | collective-permute-start | bytes 1572872 | tf_op jit(solution)/shard_map/ppermute | solution.py:1111
  504.0 15.5 %collective-permute-start.21 = (f32[8,1024]{1,0:T(8,128)}, f32[8,1024]{1,0:T(8,128)S(1)}, u32[]{:S(2)}, u32[]{:S(2)}) collective-permute-start(f32[8,1024]{1,0:T(8,128)} %get-tuple-element.169.refs_8_), channel_id=1, source_target_pairs={{0,2},{2,0},{1,3},{3,1},{4,6},{6,4},{5,7},{7,5},{8,10},{10,8},{9,1... | collective-permute-start | bytes 98312 | tf_op jit(solution)/shard_map/ppermute | solution.py:1107
  519.5 1.2 copy-start.5
  519.5 1.5 copy-start.6
  525.6 16.0 %collective-permute-start.24 = (bf16[2,2,2,2,2,64,512]{6,5,4,3,2,1,0:T(8,128)(2,1)}, bf16[2,2,2,2,2,64,512]{6,5,4,3,2,1,0:T(8,128)(2,1)S(1)}, u32[]{:S(2)}, u32[]{:S(2)}) collective-permute-start(bf16[2,2,2,2,2,64,512]{6,5,4,3,2,1,0:T(8,128)(2,1)} %get-tuple-element.175), channel_id=1, source_target_pairs={{0,2},{2,0},{1,3},{3,1},{4,6},{6,4},{5,7},{7,5},{8,10},{10,8},{9,1... | collective-permute-start | bytes 6291464 | tf_op jit(solution)/shard_map/ppermute | solution.py:1107
  525.6 14.5 %collective-permute-start.22 = (bf16[2,2,2,64,512]{4,3,2,1,0:T(8,128)(2,1)}, bf16[2,2,2,64,512]{4,3,2,1,0:T(8,128)(2,1)S(1)}, u32[]{:S(2)}, u32[]{:S(2)}) collective-permute-start(bf16[2,2,2,64,512]{4,3,2,1,0:T(8,128)(2,1)} %get-tuple-element.172), channel_id=1, source_target_pairs={{0,4},{4,0},{1,5},{5,1},{2,6},{6,2},{3,7},{7,3},{8,12},{12,8},{9,1... | collective-permute-start | bytes 1572872 | tf_op jit(solution)/shard_map/ppermute | solution.py:1107
  527.4 14.2 %collective-permute-start.23 = (bf16[2,2,2,64,512]{4,3,2,1,0:T(8,128)(2,1)}, bf16[2,2,2,64,512]{4,3,2,1,0:T(8,128)(2,1)S(1)}, u32[]{:S(2)}, u32[]{:S(2)}) collective-permute-start(bf16[2,2,2,64,512]{4,3,2,1,0:T(8,128)(2,1)} %get-tuple-element.173), channel_id=1, source_target_pairs={{0,1},{1,0},{2,3},{3,2},{4,5},{5,4},{6,7},{7,6},{8,9},{9,8},{10,11... | collective-permute-start | bytes 1572872 | tf_op jit(solution)/shard_map/ppermute | solution.py:1107
  528.7 9.6 %collective-permute-start.25 = (f32[8,1024]{1,0:T(8,128)}, f32[8,1024]{1,0:T(8,128)S(1)}, u32[]{:S(2)}, u32[]{:S(2)}) collective-permute-start(f32[8,1024]{1,0:T(8,128)} %get-tuple-element.176.refs_20_), channel_id=1, source_target_pairs={{0,8},{8,0},{16,24},{24,16},{1,9},{9,1},{17,25},{25,17},{2,10},{10... | collective-permute-start | bytes 98312 | tf_op jit(solution)/shard_map/ppermute | solution.py:1111
  538.2 3.4 copy-start.28
  540.1 1.5 copy-start.9
  541.6 1.5 copy-start
  548.3 3.5 copy-start.26
  548.3 13.4 %collective-permute-start.26 = (bf16[2,2,2,64,512]{4,3,2,1,0:T(8,128)(2,1)}, bf16[2,2,2,64,512]{4,3,2,1,0:T(8,128)(2,1)S(1)}, u32[]{:S(2)}, u32[]{:S(2)}) collective-permute-start(bf16[2,2,2,64,512]{4,3,2,1,0:T(8,128)(2,1)} %get-tuple-element.181), channel_id=1, source_target_pairs={{0,1},{1,0},{2,3},{3,2},{4,5},{5,4},{6,7},{7,6},{8,9},{9,8},{10,11... | collective-permute-start | bytes 1572872 | tf_op jit(solution)/shard_map/ppermute | solution.py:1107
  549.7 13.1 %collective-permute-start.27 = (bf16[2,2,2,64,512]{4,3,2,1,0:T(8,128)(2,1)}, bf16[2,2,2,64,512]{4,3,2,1,0:T(8,128)(2,1)S(1)}, u32[]{:S(2)}, u32[]{:S(2)}) collective-permute-start(bf16[2,2,2,64,512]{4,3,2,1,0:T(8,128)(2,1)} %get-tuple-element.182), channel_id=1, source_target_pairs={{0,4},{4,0},{1,5},{5,1},{2,6},{6,2},{3,7},{7,3},{8,12},{12,8},{9,1... | collective-permute-start | bytes 1572872 | tf_op jit(solution)/shard_map/ppermute | solution.py:1107
  550.1 13.8 %collective-permute-start.29 = (bf16[2,64,2048]{2,1,0:T(8,128)(2,1)}, bf16[2,64,2048]{2,1,0:T(8,128)(2,1)S(1)}, u32[]{:S(2)}, u32[]{:S(2)}) collective-permute-start(bf16[2,64,2048]{2,1,0:T(8,128)(2,1)} %get-tuple-element.185), channel_id=1, source_target_pairs={{0,8},{8,0},{16,24},{24,16},{1,9},{9,1},{17,25},{25,17},{2,10},{10... | collective-permute-start | bytes 1572872 | tf_op jit(solution)/shard_map/ppermute | solution.py:1111
  551.9 9.9 %collective-permute-start.28 = (f32[8,1024]{1,0:T(8,128)S(1)}, f32[8,1024]{1,0:T(8,128)S(1)}, u32[]{:S(2)}, u32[]{:S(2)}) collective-permute-start(f32[8,1024]{1,0:T(8,128)S(1)} %copy-done.26), channel_id=1, source_target_pairs={{0,16},{8,24},{16,0},{24,8},{1,17},{9,25},{17,1},{25,9},{2,18},{10... | collective-permute-start | bytes 98312 | tf_op jit(solution)/shard_map/ppermute | solution.py:1111
  561.8 2.2 copy-start.30
  561.8 2.2 copy-start.11
  562.8 1.2 copy-start.12
  568.5 8.2 %collective-permute-start.30 = (bf16[2,2,64,512]{3,2,1,0:T(8,128)(2,1)}, bf16[2,2,64,512]{3,2,1,0:T(8,128)(2,1)S(1)}, u32[]{:S(2)}, u32[]{:S(2)}) collective-permute-start(bf16[2,2,64,512]{3,2,1,0:T(8,128)(2,1)} %get-tuple-element.186), channel_id=1, source_target_pairs={{0,4},{4,0},{1,5},{5,1},{2,6},{6,2},{3,7},{7,3},{8,12},{12,8},{9,1... | collective-permute-start | bytes 786440 | tf_op jit(solution)/shard_map/ppermute | solution.py:1107
  569.7 6.9 %collective-permute-start.31 = (bf16[2,2,64,512]{3,2,1,0:T(8,128)(2,1)}, bf16[2,2,64,512]{3,2,1,0:T(8,128)(2,1)S(1)}, u32[]{:S(2)}, u32[]{:S(2)}) collective-permute-start(bf16[2,2,64,512]{3,2,1,0:T(8,128)(2,1)} %get-tuple-element.187), channel_id=1, source_target_pairs={{0,1},{1,0},{2,3},{3,2},{4,5},{5,4},{6,7},{7,6},{8,9},{9,8},{10,11... | collective-permute-start | bytes 786440 | tf_op jit(solution)/shard_map/ppermute | solution.py:1107
  571.0 5.7 collective-permute-start.32
  574.7 8.7 %copy-start.17 = (f32[64,4096]{1,0:T(8,128)S(1)}, f32[64,4096]{1,0:T(8,128)}, u32[]{:S(2)}) copy-start(f32[64,4096]{1,0:T(8,128)} %get-tuple-element.198) | copy-start | bytes 3145732
  574.7 12.1 %collective-permute-start.34 = (bf16[64,2048]{1,0:T(8,128)(2,1)}, bf16[64,2048]{1,0:T(8,128)(2,1)S(1)}, u32[]{:S(2)}, u32[]{:S(2)}) collective-permute-start(bf16[64,2048]{1,0:T(8,128)(2,1)} %get-tuple-element.192), channel_id=1, source_target_pairs={{0,16},{8,24},{16,0},{24,8},{1,17},{9,25},{17,1},{25,9},{2,18},{10... | collective-permute-start | bytes 786440 | tf_op jit(solution)/shard_map/ppermute | solution.py:1111
  581.3 5.4 collective-permute-start.35
  582.2 8.8 %collective-permute-start.33 = (bf16[2,64,1024]{2,1,0:T(8,128)(2,1)}, bf16[2,64,1024]{2,1,0:T(8,128)(2,1)S(1)}, u32[]{:S(2)}, u32[]{:S(2)}) collective-permute-start(bf16[2,64,1024]{2,1,0:T(8,128)(2,1)} %get-tuple-element.190), channel_id=1, source_target_pairs={{0,8},{8,0},{16,24},{24,16},{1,9},{9,1},{17,25},{25,17},{2,10},{10... | collective-permute-start | bytes 786440 | tf_op jit(solution)/shard_map/ppermute | solution.py:1111
  586.8 4.2 copy-start.24
  586.8 4.2 copy-start.31
  595.4 7.9 %collective-permute-start.36 = (bf16[64,1024]{1,0:T(8,128)(2,1)}, bf16[64,1024]{1,0:T(8,128)(2,1)S(1)}, u32[]{:S(2)}, u32[]{:S(2)}) collective-permute-start(bf16[64,1024]{1,0:T(8,128)(2,1)} %get-tuple-element.195), channel_id=1, source_target_pairs={{0,16},{8,24},{16,0},{24,8},{1,17},{9,25},{17,1},{25,9},{2,18},{10... | collective-permute-start | bytes 393224 | tf_op jit(solution)/shard_map/ppermute | solution.py:1111
  (11 other events, 8.4 us)
Sparse Core Ops, SparseCore 0:
  14.7 121.1 all-gather.6
  138.9 81.8 all-gather.8
  340.2 63.6 all-gather.10
where the time goes:
time: 623 us; the launch traced here: 613 us
  Pallas kernels  384 us (62%)
  waiting for transfers between devices  131 us (21%)
  starting transfers between devices  42.5 us (7%)
  local copies, waits for them, and re-layouts  33.3 us (5%)
  between operations  17.6 us (3%)
    pallas_call x34, Pallas kernels, call(): pl.pallas_call(ordered_kernel, grid_spec=pltpu.PrefetchScalarGridSpec(num...  384 us
    ppermute x10, waiting for transfers between devices, swap_line(): return lax.ppermute(value, 'z', [(i, i ^ bit) for i in range(4)])  63.7 us
    ppermute x27, waiting for transfers between devices, swap(): return lax.ppermute(value, axis, [(0, 1), (1, 0)])  40 us
    all_gather x1, waiting for transfers between devices, one_sequence_plan(): pack = lax.all_gather(pack, everyone, axis=0, tiled=False)  26.3 us
    ppermute x27, starting transfers between devices, swap(): return lax.ppermute(value, axis, [(0, 1), (1, 0)])  22.2 us
    ppermute x10, starting transfers between devices, swap_line(): return lax.ppermute(value, 'z', [(i, i ^ bit) for i in range(4)])  20.3 us
    unnamed x72, local copies, waits for them, and re-layouts  18.1 us
  transfers between devices with their start and end apart: 40, of which 18 were waited for; matrix products, arithmetic and copies ran while one was open for 2% of the time, Pallas kernels for 49%

commit v1 on v0

--- a/solution.py
+++ b/solution.py
@@ -622,26 +622,6 @@
     return made if parts > 1 else made[0]
 
 
-def merge_kernel(where, ent, byp, full, out):
-    half = ent.shape[1]
-    weight = full[...].reshape(2 * half, half)
-    out[...] = nn(ent[...], weight[:half, :]) + nn(byp[...], weight[half:, :])
-
-
-def merge_forward(where, ent, byp, gathered, r):
-    rows, d = ent.shape
-    part = pl.BlockSpec((CHUNK, d), lambda i, w: (i, 0))
-    return call(
-        merge_kernel,
-        (rows // CHUNK,),
-        where,
-        [(ent, part), (byp, part), (gathered, resident((2, 2, 2, 2, 2, r, d)))],
-        [((rows, d), jnp.float32, part)],
-        [],
-        "merge_forward",
-    )[0]
-
-
 def weight_block(r, col, number):
     def index(*args):
         which, x_rel = number(*args[:-1])
@@ -650,12 +630,14 @@
     return pl.BlockSpec((2, 2, 2, 2, pl.squeezed, r, col), index)
 
 
-def project_kernel(where, raw, vec, weight, merged, first, out):
+def project_kernel(where, ent, byp, full, vec, weight, merged, first, out):
     @pl.when((pl.program_id(0) == 0) & (pl.program_id(1) == 0))
     def _():
-        for start in range(0, raw.shape[0], CHUNK):
+        d = ent.shape[1]
+        merge = full[...].reshape(2 * d, d)
+        for start in range(0, ent.shape[0], CHUNK):
             part = slice(start, start + CHUNK)
-            total = raw[part, :] + vec[0:1, :]
+            total = nn(ent[part, :], merge[:d, :]) + nn(byp[part, :], merge[d:, :]) + vec[0:1, :]
             merged[part, :] = total
             norm, _ = normalized(total)
             first[part, :] = (norm * vec[1:2, :] + vec[2:3, :]).astype(jnp.bfloat16)
@@ -663,15 +645,17 @@
     out[...] = nn(first[...], weight[...].reshape(first.shape[1], -1)).astype(jnp.bfloat16)
 
 
-def project_forward(where, raw, vec, gathered, r, col):
-    rows, d = raw.shape
+def project_forward(where, ent, byp, vec, gathered, r, col):
+    rows, d = ent.shape
     f32, bf16 = jnp.float32, jnp.bfloat16
     return call(
         project_kernel,
         (3, 2),
         where,
         [
-            (raw, resident((rows, d))),
+            (ent, resident((rows, d))),
+            (byp, resident((rows, d))),
+            (gathered, resident((2, 2, 2, 2, 2, r, d))),
             (vec, resident(vec.shape)),
             (gathered, weight_block(r, col, lambda w, x: (w, x))),
         ],
@@ -685,42 +669,36 @@
     )
 
 
-def result_kernel(where, attended, merged, vec, weight, after, second, total):
-    step = pl.program_id(0)
-    natural = weight[...].reshape(after.shape[1], -1)
-
-    @pl.when(step == 0)
-    def _():
-        total[...] = nt(attended[...], natural)
-
-    @pl.when(step == 1)
-    def _():
-        for start in range(0, after.shape[0], CHUNK):
-            here = slice(start, start + CHUNK)
-            part = nt(attended[here, :], natural)
-            value = merged[here, :] + vec[3:4, :] + (total[here, :] + part)
-            after[here, :] = value
-            norm, _ = normalized(value)
-            second[here, :] = (norm * vec[4:5, :] + vec[5:6, :]).astype(jnp.bfloat16)
+def result_kernel(where, attended, merged, vec, weight, after, second):
+    d, col = after.shape[1], weight.shape[-1]
+    own = weight[:, :, :, :, where[2]].reshape(d, col)
+    other = weight[:, :, :, :, 1 - where[2]].reshape(d, col)
+    for start in range(0, after.shape[0], CHUNK):
+        here = slice(start, start + CHUNK)
+        part = nt(attended[here, :col], own) + nt(attended[here, col:], other)
+        value = merged[here, :] + vec[3:4, :] + part
+        after[here, :] = value
+        norm, _ = normalized(value)
+        second[here, :] = (norm * vec[4:5, :] + vec[5:6, :]).astype(jnp.bfloat16)
 
 
 def result_forward(where, attended, merged, vec, gathered, r, col):
     rows, d = merged.shape
     return call(
         result_kernel,
-        (2,),
-        where,
-        [
-            (attended, pl.BlockSpec((rows, col), lambda x, s: (0, x))),
+        (1,),
+        where,
+        [
+            (attended, resident((rows, d))),
             (merged, resident((rows, d))),
             (vec, resident(vec.shape)),
-            (gathered, weight_block(r, col, lambda x: (3, x))),
+            (gathered, once((2, 2, 2, 2, 2, r, col), lambda i, s: (0, 0, 0, 0, 0, 2, 1))),
         ],
         [
             ((rows, d), jnp.float32, resident((rows, d))),
             ((rows, d), jnp.bfloat16, resident((rows, d))),
         ],
-        [pltpu.VMEM((rows, d), jnp.float32)],
+        [],
         "result_forward",
     )
 
@@ -1168,8 +1146,10 @@
         contract_layer_offset,
         expand_layer_offset,
     )
-    flat = jnp.concatenate(small)
-    flat = jnp.pad(flat, (0, 8 * d - flat.shape[0])).reshape(8, d)
+    share = d // (2**5)
+    rows_of_vectors = jnp.concatenate([v.reshape(1, -1) for v in small[:7]], axis=0)
+    flat = jnp.pad(rows_of_vectors, ((0, 1), (0, d - share)))
+    flat = flat + jnp.pad(expand_layer_offset.reshape(1, -1), ((7, 0), (0, d - expand_layer_offset.shape[0])))
     pack = jnp.concatenate(
         [
             bypass_merge_matrix,
@@ -1189,22 +1169,23 @@
     up = pile(where, 4, up, swap_line(up, 1), 1)
     up_block = pile(where, None, up, swap(up, "y"), 0)
     (gathered,) = gate(where, [gathered], (up_block,))
-    raw = merge_forward(where, entering_states, bypass_states, gathered, r)
-
-    rest = pack[:, 3 * r].astype(f32)
+
+    rest = pack[:, 3 * r : 3 * r + 8].astype(f32)
     count = pack.shape[0]
-    vec = rest[:, : 7 * d // count].reshape(count, 7, d // count).transpose(1, 0, 2).reshape(7, d)
+    vec = rest[:, :7, : d // count].transpose(1, 0, 2).reshape(7, d)
     vec = jnp.pad(vec, ((0, 1), (0, 0)))
-    hidden_add = rest[:, 7 * d // count : 7 * d // count + 2 * half // count].reshape(2, 1, half)
+    hidden_add = rest[:, 7, : 2 * half // count].reshape(2, 1, half)
     alive = lax.dynamic_index_in_dim(occupancy_mask, x, keepdims=True).astype(f32)
 
-    merged, first, projected = project_forward(where, raw, vec, gathered, r, col)
+    merged, first, projected = project_forward(
+        where, entering_states, bypass_states, vec, gathered, r, col
+    )
     up_other, projected = gate(where, [swap(up_block, "x"), projected], ())
     up_away = [swap(up_block, "c"), swap(up_other, "c")]
     attended, logs = attention_forward(where, projected)
-    *up_away, attended, logs = gate(where, up_away + [attended, logs], ())
+    after_attn, second = result_forward(where, attended, merged, vec, gathered, r, col)
+    *up_away, second = gate(where, up_away + [second], ())
     expand_pieces = ((up_block, up_away[0]), (up_other, up_away[1]))
-    after_attn, second = result_forward(where, attended, merged, vec, gathered, r, col)
     active, slope = expand_forward(where, second, hidden_add, expand_pieces)
     block_out, upstream, down_bias, energy = contract_forward(
         where, alive, active, after_attn, mentor_states, vec, down

time: 623 us -> 609 us (0.978)
  starting transfers between devices: 42.5 us -> 36.2 us
    pallas_call x34 -> x33, Pallas kernels: 384 us -> 379 us  [call(): pl.pallas_call(ordered_kernel, grid_spec=pltpu.PrefetchScalarGridSpec(num...]
    unnamed x72 -> x70, local copies, waits for them, and re-layouts: 18.1 us -> 16.8 us
  transfers between devices with their start and end apart: 40 -> 40, of which waited for: 18 -> 19; matrix products, arithmetic and copies ran while one was open for 2% -> 2% of each run, Pallas kernels for 49% -> 50%
where the time goes in v1:
time: 609 us; the launch traced here: 598 us
  Pallas kernels  379 us (62%)
  waiting for transfers between devices  132 us (22%)
  starting transfers between devices  36.2 us (6%)
  local copies, waits for them, and re-layouts  27.1 us (4%)
  between operations  17.6 us (3%)
  other arithmetic  6.19 us (1%)
    pallas_call x33, Pallas kernels, call(): pl.pallas_call(ordered_kernel, grid_spec=pltpu.PrefetchScalarGridSpec(num...  379 us
    ppermute x10, waiting for transfers between devices, swap_line(): return lax.ppermute(value, 'z', [(i, i ^ bit) for i in range(4)])  60.4 us
    ppermute x27, waiting for transfers between devices, swap(): return lax.ppermute(value, axis, [(0, 1), (1, 0)])  40.6 us
    all_gather x1, waiting for transfers between devices, one_sequence_plan(): pack = lax.all_gather(pack, everyone, axis=0, tiled=False)  30.8 us
    ppermute x27, starting transfers between devices, swap(): return lax.ppermute(value, axis, [(0, 1), (1, 0)])  19.2 us
    ppermute x10, starting transfers between devices, swap_line(): return lax.ppermute(value, 'z', [(i, i ^ bit) for i in range(4)])  16.9 us
    unnamed x70, local copies, waits for them, and re-layouts  16.8 us
  transfers between devices with their start and end apart: 40, of which 19 were waited for; matrix products, arithmetic and copies ran while one was open for 2% of the time, Pallas kernels for 50%

profile of v1, /device:TPU:0, one launch (start us, length us, event | category | flops | bytes accessed | tf_op | source)
XLA Modules:
  0.0 598.1 jit_solution(17615947190071661362)
XLA Ops:
  8.7 1.8 pad_maximum_fusion
  11.3 4.1 collective-permute-start
  16.0 14.5 %collective-permute-done.refs_1_ = bf16[64,2048]{1,0:T(8,128)(2,1)S(1)} collective-permute-done((bf16[64,2048]{1,0:T(8,128)(2,1)}, bf16[64,2048]{1,0:T(8,128)(2,1)S(1)}, u32[]{:S(2)}, u32[]{:S(2)}) %collective-permute-start) | collective-permute-done | bytes 262176 | tf_op jit(solution)/shard_map/ppermute | solution.py:1089
  31.3 2.5 pile.3.refs_0_
  33.8 3.6 collective-permute-start.1
  37.4 21.4 %collective-permute-done.1.refs_1_ = bf16[2,64,2048]{2,1,0:T(8,128)(2,1)S(1)} collective-permute-done((bf16[2,64,2048]{2,1,0:T(8,128)(2,1)}, bf16[2,64,2048]{2,1,0:T(8,128)(2,1)S(1)}, u32[]{:S(2)}, u32[]{:S(2)}) %collective-permute-start.1) | collective-permute-done | bytes 524320 | tf_op jit(solution)/shard_map/ppermute | solution.py:1089
  59.6 2.9 pile.4.refs_0_
  63.1 31.3 %collective-permute-done.2.refs_1_ = bf16[2,2,64,2048]{3,2,1,0:T(8,128)(2,1)S(1)} collective-permute-done((bf16[2,2,64,2048]{3,2,1,0:T(8,128)(2,1)}, bf16[2,2,64,2048]{3,2,1,0:T(8,128)(2,1)S(1)}, u32[]{:S(2)}, u32[]{:S(2)}) %collective-permute-start.2) | collective-permute-done | bytes 1048608 | tf_op jit(solution)/shard_map/ppermute | solution.py:1085
  95.4 3.7 pile.5.refs_1_.refs_2_.refs_5_
  99.1 30.8 %all-gather.7.cloned.1.call-done = bf16[6400,1024]{1,0:T(8,128)(2,1)} async-done(((bf16[200,1024]{1,0:T(8,128)(2,1)}), bf16[6400,1024]{1,0:T(8,128)(2,1)}) %all-gather.7.cloned.1.call-update) | async-done | bytes 13107216 | tf_op jit(solution)/shard_map/all_gather | solution.py:1161
  132.7 21.4 %project_forward.1 = (f32[1104,1024]{1,0:T(8,128)}, bf16[1104,1024]{1,0:T(8,128)(2,1)}, bf16[1104,3072]{1,0:T(8,128)(2,1)}) custom-call(s32[5]{0:T(128)} %stack.23.where_ref, bf16[1104,1024]{1,0:T(8,128)(2,1)} %refs_0_.5, bf16[1104,1024]{1,0:T(8,128)(2,1)} %refs_1_.3, bf16[2,2,2,2,2,200,1024]{6,5,4,3,2,1,0:T(8,128)(2,1)} %gate.3.refs_2_.refs_4_.refs_3_.refs_1_, ...), custom_call_target="tpu_custom_call" | custom-call | tf_op jit(solution)/shard_map/project_forward/pallas_call | solution.py:449
  157.1 31.5 %attention_forward.1 = (bf16[1104,1024]{1,0:T(8,128)(2,1)}, f32[1104,1024]{1,0:T(8,128)}) custom-call(s32[5]{0:T(128)} %stack.23.where_ref, bf16[1104,3072]{1,0:T(8,128)(2,1)} %get-tuple-element.110.refs_0_.refs_1_.refs_2_, bf16[1104,3072]{1,0:T(8,128)(2,1)} %get-tuple-element.110.refs_0_.refs_1_.refs_2_, ...), custom_call_target="tpu_custom_call" | custom-call | tf_op jit(solution)/shard_map/attention_forward/pallas_call | solution.py:449
  188.6 10.0 %result_forward.1 = (f32[1104,1024]{1,0:T(8,128)}, bf16[1104,1024]{1,0:T(8,128)(2,1)}) custom-call(s32[5]{0:T(128)} %stack.23.where_ref, bf16[1104,1024]{1,0:T(8,128)(2,1)} %get-tuple-element.111.refs_0_.refs_1_.refs_3_, f32[1104,1024]{1,0:T(8,128)} %get-tuple-element.112.refs_1_.refs_0_, f32[8,1024]{1,0:T(8,128)} %pad.14.refs_3_.refs_2_.refs_4_, ...), custom_call_target="tpu_custom_call" | custom-call | tf_op jit(solution)/shard_map/result_forward/pallas_call | solution.py:449
  198.6 1.3 copy-done.2
  200.6 29.8 %expand_forward.1 = (bf16[2,1104,2048]{2,1,0:T(8,128)(2,1)}, bf16[2,1104,2048]{2,1,0:T(8,128)(2,1)}) custom-call(s32[5]{0:T(128)} %stack.23.where_ref, bf16[1104,1024]{1,0:T(8,128)(2,1)} %get-tuple-element.114.refs_0_.refs_1_, f32[2,1,2048]{2,1,0:T(1,128)} %bitcast.54, bf16[2,2,2,64,2048]{4,3,2,1,0:T(8,128)(2,1)} %pile.5.refs_1_.refs_2_.refs_5_, ...), custom_call_target="tpu_custom_call" | custom-call | tf_op jit(solution)/shard_map/expand_forward/pallas_call | solution.py:449
  230.4 19.0 %contract_forward.1 = (bf16[1104,1024]{1,0:T(8,128)(2,1)}, bf16[1104,1024]{1,0:T(8,128)(2,1)}, f32[8,1024]{1,0:T(8,128)}, f32[8,128]{1,0:T(8,128)}) custom-call(s32[5]{0:T(128)} %stack.23.where_ref, f32[1]{0:T(128)S(6)} %convert_element_type.15.refs_0_.refs_7_, bf16[2,1104,2048]{2,1,0:T(8,128)(2,1)} %get-tuple-element.117.refs_1_.refs_2_, ...), custom_call_target="tpu_custom_call" | custom-call | tf_op jit(solution)/shard_map/contract_forward/pallas_call | solution.py:449
  249.4 29.8 %feed_backward.2 = (bf16[1104,1024]{1,0:T(8,128)(2,1)}, bf16[2,2,2,64,2048]{4,3,2,1,0:T(8,128)(2,1)}, bf16[2,2,2,64,2048]{4,3,2,1,0:T(8,128)(2,1)}, bf16[2,2,2,6...) custom-call(s32[5]{0:T(128)} %stack.23.where_ref, ...), custom_call_target="tpu_custom_call" | custom-call | tf_op jit(solution)/shard_map/feed_backward/pallas_call | solution.py:449
  279.8 29.4 %feed_backward.3 = (bf16[1104,1024]{1,0:T(8,128)(2,1)}, bf16[2,2,2,64,2048]{4,3,2,1,0:T(8,128)(2,1)}, bf16[2,2,2,64,2048]{4,3,2,1,0:T(8,128)(2,1)}, bf16[2,2,2,6...) custom-call(s32[5]{0:T(128)} %stack.23.where_ref, ...), custom_call_target="tpu_custom_call" | custom-call | tf_op jit(solution)/shard_map/feed_backward/pallas_call | solution.py:449
  309.2 1.3 copy-done.6
  310.5 5.6 fold.11
  316.7 10.9 %norm_backward.2 = (f32[1104,1024]{1,0:T(8,128)}, bf16[1104,1024]{1,0:T(8,128)(2,1)}, f32[16,1024]{1,0:T(8,128)}) custom-call(s32[5]{0:T(128)} %stack.23.where_ref, f32[1104,1024]{1,0:T(8,128)} %get-tuple-element.118.refs_2_.refs_0_, bf16[1104,1024]{1,0:T(8,128)(2,1)} %get-tuple-element.120.refs_0_.refs_1_, f32[8,1024]{1,0:T(8,128)} %pad.14.refs_3_.refs_2_.refs_4_, ...), custom_call_target="tpu_custom_call" | custom-call | tf_op jit(solution)/shard_map/norm_backward/pallas_call | solution.py:449
  327.6 1.5 collective-permute-start.9
  329.1 1.9 collective-permute-start.10
  330.9 1.4 copy-done.3
  332.4 3.4 fold.12
  336.0 9.6 %result_backward.1 = (bf16[1104,1024]{1,0:T(8,128)(2,1)}, bf16[2,2,2,2,2,64,512]{6,5,4,3,2,1,0:T(8,128)(2,1)}, bf16[2,2,2,2,2,64,512]{6,5,4,3,2,1,0:T(8,128)(2,1)}) custom-call(s32[5]{0:T(128)} %stack.23.where_ref, bf16[1104,1024]{1,0:T(8,128)(2,1)} %get-tuple-element.145.refs_0_, bf16[1104,1024]{1,0:T(8,128)(2,1)} %get-tuple-element.111.refs_0_.refs_1_.refs_3_, ...), custom_call_target="tpu_custom_call" | custom-call | tf_op jit(solution)/shard_map/result_backward/pallas_call | solution.py:449
  345.5 34.5 %attention_backward.2.refs_6_ = bf16[3,1104,1024]{2,1,0:T(8,128)(2,1)} custom-call(s32[5]{0:T(128)} %stack.23.where_ref, bf16[1104,3072]{1,0:T(8,128)(2,1)} %get-tuple-element.110.refs_0_.refs_1_.refs_2_, bf16[1104,3072]{1,0:T(8,128)(2,1)} %get-tuple-element.110.refs_0_.refs_1_.refs_2_, bf16[1104,3072]{1,0:T(8,128)(2,1)} %get-tuple-element.110.refs_0_.refs_1_.refs_2_, ...), custom_call_target="tpu_custom_call" | custom-call | tf_op jit(solution)/shard_map/attention_backward/pallas_call | solution.py:449
  380.1 1.7 collective-permute-done.9.refs_2_
  383.2 5.2 fold.13
  388.4 2.6 collective-permute-start.13
  391.8 34.4 %attention_backward.3.refs_8_ = bf16[3,1104,1024]{2,1,0:T(8,128)(2,1)} custom-call(s32[5]{0:T(128)} %stack.23.where_ref, bf16[1104,3072]{1,0:T(8,128)(2,1)} %get-tuple-element.110.refs_0_.refs_1_.refs_2_, bf16[1104,3072]{1,0:T(8,128)(2,1)} %get-tuple-element.110.refs_0_.refs_1_.refs_2_, ...), custom_call_target="tpu_custom_call", output_to_operand_aliasing={{}: (7, {})} | custom-call | tf_op jit(solution)/shard_map/attention_backward/pallas_call | solution.py:449
  427.5 6.6 %fold.14 = (f32[2,64,4096]{2,1,0:T(8,128)}, bf16[2,64,4096]{2,1,0:T(8,128)(2,1)}, bf16[3,1104,1024]{2,1,0:T(8,128)(2,1)}) custom-call(s32[5]{0:T(128)} %stack.23.where_ref, bf16[2,2,2,64,2048]{4,3,2,1,0:T(8,128)(2,1)} %get-tuple-element.137.refs_0_, bf16[2,2,2,64,2048]{4,3,2,1,0:T(8,128)(2,1)} %copy-done.3, ...), custom_call_target="tpu_custom_call", output_to_operand_aliasing={{2}: (9, {})} | custom-call | tf_op jit(solution)/shard_map/fold/pallas_call | solution.py:449
  434.1 2.0 collective-permute-start.17
  436.1 14.4 %project_backward.1.refs_2_ = bf16[1104,1024]{1,0:T(8,128)(2,1)} custom-call(s32[5]{0:T(128)} %stack.23.where_ref, bf16[3,1104,1024]{2,1,0:T(8,128)(2,1)} %get-tuple-element.151.refs_1_.refs_0_, bf16[2,2,2,2,2,200,1024]{6,5,4,3,2,1,0:T(8,128)(2,1)} %gate.3.refs_2_.refs_4_.refs_3_.refs_1_), custom_call_target="tpu_custom_call" | custom-call | tf_op jit(solution)/shard_map/project_backward/pallas_call | solution.py:449
  450.6 14.5 %project_weight.1 = (bf16[2,2,2,2,2,64,512]{6,5,4,3,2,1,0:T(8,128)(2,1)}, bf16[2,2,2,2,2,64,512]{6,5,4,3,2,1,0:T(8,128)(2,1)}, bf16[2,2,2,2,2,64,512]{6,5,4,3,2,...) custom-call(s32[5]{0:T(128)} %stack.23.where_ref, ...), custom_call_target="tpu_custom_call", output_to_operand_aliasing={{2}: (3, {}), {3}: (4, {})} | custom-call | tf_op jit(solution)/shard_map/project_weight/pallas_call | solution.py:449
  466.5 3.8 fold.15
  470.3 2.0 collective-permute-done.15.refs_1_.refs_3_.refs_5_
  473.7 4.6 fold.16
  480.4 8.9 %norm_backward.3 = (bf16[1104,1024]{1,0:T(8,128)(2,1)}, f32[8,1024]{1,0:T(8,128)}) custom-call(s32[5]{0:T(128)} %stack.23.where_ref, f32[1104,1024]{1,0:T(8,128)} %get-tuple-element.112.refs_1_.refs_0_, f32[1104,1024]{1,0:T(8,128)} %get-tuple-element.165.refs_1_, f32[8,1024]{1,0:T(8,128)} %pad.14.refs_3_.refs_2_.refs_4_, ...), custom_call_target="tpu_custom_call" | custom-call | tf_op jit(solution)/shard_map/norm_backward/pallas_call | solution.py:449
  489.3 10.7 %merge_weight.1 = (bf16[2,2,2,2,2,64,512]{6,5,4,3,2,1,0:T(8,128)(2,1)}, bf16[2,2,2,2,2,64,512]{6,5,4,3,2,1,0:T(8,128)(2,1)}) custom-call(s32[5]{0:T(128)} %stack.23.where_ref, bf16[1104,1024]{1,0:T(8,128)(2,1)} %refs_0_.5, bf16[1104,1024]{1,0:T(8,128)(2,1)} %refs_1_.3, bf16[1104,1024]{1,0:T(8,128)(2,1)} %get-tuple-element.168.refs_2_.refs_10_), custom_call_target="tpu_custom_call" | custom-call | tf_op jit(solution)/shard_map/merge_weight/pallas_call | solution.py:449
  500.0 4.8 collective-permute-done.19.refs_1_
  506.3 4.5 fold.17
  510.8 1.7 collective-permute-start.22
  512.6 1.2 collective-permute-start.23
  513.8 9.5 %merge_backward.1 = (f32[1104,1024]{1,0:T(8,128)}, f32[1104,1024]{1,0:T(8,128)}) custom-call(s32[5]{0:T(128)} %stack.23.where_ref, bf16[1104,1024]{1,0:T(8,128)(2,1)} %get-tuple-element.175.refs_0_, bf16[2,2,2,2,2,200,1024]{6,5,4,3,2,1,0:T(8,128)(2,1)} %gate.3.refs_2_.refs_4_.refs_3_.refs_1_), custom_call_target="tpu_custom_call" | custom-call | tf_op jit(solution)/shard_map/merge_backward/pallas_call | solution.py:449
  523.3 2.1 collective-permute-done.22.refs_3_.refs_7_
  525.4 1.4 collective-permute-done.23.refs_11_.refs_15_
  528.3 5.2 fold.18
  533.5 1.2 collective-permute-start.26
  535.2 1.7 reduce_sum.9
  536.9 2.7 collective-permute-start.28
  539.7 7.1 %collective-permute-done.28.refs_7_ = f32[8,1024]{1,0:T(8,128)S(1)} collective-permute-done((f32[8,1024]{1,0:T(8,128)S(1)}, f32[8,1024]{1,0:T(8,128)S(1)}, u32[]{:S(2)}, u32[]{:S(2)}) %collective-permute-start.28) | collective-permute-done | bytes 32800 | tf_op jit(solution)/shard_map/ppermute | solution.py:1089
  547.8 1.2 collective-permute-done.29.refs_9_
  549.8 3.7 fold.19
  553.5 1.3 collective-permute-start.30
  559.7 1.5 collective-permute-start.34
  563.1 3.2 fold.20
  567.2 1.2 collective-permute-start.33
  569.5 2.3 collective-permute-done.34.refs_3_
  571.8 4.2 collective-permute-done.33.refs_1_
  576.7 3.0 fold.21
  581.0 1.9 slice_bitcast_fusion.1
  583.4 4.9 collective-permute-done.36
  588.4 1.7 convert_add_fusion
  (143 shorter events, 36.7 us)
Async XLA Ops:
  7.2 122.7 %all-gather.7.cloned.1.call-start = ((), (), s32[]{:S(2)}) async-start(), calls=%async_computation | async-start | bytes 13516800 | tf_op jit(solution)/shard_map/all_gather | solution.py:1161
  10.5 219.9 %all-gather.9.cloned.1.call-start = ((), (), s32[]{:S(2)}) async-start(), calls=%async_computation.1 | async-start | bytes 8650752 | tf_op jit(solution)/shard_map/all_gather | solution.py:1164
  11.3 414.9 %all-gather.11.cloned.1.call-start = ((), (), s32[]{:S(2)}) async-start(), calls=%async_computation.2 | async-start | bytes 2162688 | tf_op jit(solution)/shard_map/all_gather | solution.py:1218
  11.3 19.2 %collective-permute-start = (bf16[64,2048]{1,0:T(8,128)(2,1)}, bf16[64,2048]{1,0:T(8,128)(2,1)S(1)}, u32[]{:S(2)}, u32[]{:S(2)}) collective-permute-start(bf16[64,2048]{1,0:T(8,128)(2,1)} %refs_0_.3), channel_id=1, source_target_pairs={{0,16},{8,24},{16,0},{24,8},{1,17},{9,25},{17,1},{25,9},{2,18},{10... | collective-permute-start | bytes 786440 | tf_op jit(solution)/shard_map/ppermute | solution.py:1089
  33.8 25.0 %collective-permute-start.1 = (bf16[2,64,2048]{2,1,0:T(8,128)(2,1)}, bf16[2,64,2048]{2,1,0:T(8,128)(2,1)S(1)}, u32[]{:S(2)}, u32[]{:S(2)}) collective-permute-start(bf16[2,64,2048]{2,1,0:T(8,128)(2,1)} %pile.3.refs_0_), channel_id=1, source_target_pairs={{0,8},{8,0},{16,24},{24,16},{1,9},{9,1},{17,25},{25,17},{2,10},{10... | collective-permute-start | bytes 1572872 | tf_op jit(solution)/shard_map/ppermute | solution.py:1089
  62.5 32.0 %collective-permute-start.2 = (bf16[2,2,64,2048]{3,2,1,0:T(8,128)(2,1)}, bf16[2,2,64,2048]{3,2,1,0:T(8,128)(2,1)S(1)}, u32[]{:S(2)}, u32[]{:S(2)}) collective-permute-start(bf16[2,2,64,2048]{3,2,1,0:T(8,128)(2,1)} %pile.4.refs_0_), channel_id=1, source_target_pairs={{0,4},{4,0},{1,5},{5,1},{2,6},{6,2},{3,7},{7,3},{8,12},{12,8},{9,1... | collective-permute-start | bytes 3145736 | tf_op jit(solution)/shard_map/ppermute | solution.py:1085
  94.5 1.0 copy-start.15
  99.1 55.0 %collective-permute-start.4 = (bf16[2,2,2,64,2048]{4,3,2,1,0:T(8,128)(2,1)}, bf16[2,2,2,64,2048]{4,3,2,1,0:T(8,128)(2,1)}, u32[]{:S(2)}, u32[]{:S(2)}) collective-permute-start(bf16[2,2,2,64,2048]{4,3,2,1,0:T(8,128)(2,1)} %pile.5.refs_1_.refs_2_.refs_5_), channel_id=1, source_target_pairs={{0,1},{1,0},{2,3},{3,2},{4,5},{5,4},{6,7},{7,6},{8,9},{9,8},{10,11... | collective-permute-start | bytes 6291464 | tf_op jit(solution)/shard_map/ppermute | solution.py:1085
  99.1 99.5 %collective-permute-start.3 = (bf16[2,2,2,64,2048]{4,3,2,1,0:T(8,128)(2,1)}, bf16[2,2,2,64,2048]{4,3,2,1,0:T(8,128)(2,1)S(1)}, u32[]{:S(2)}, u32[]{:S(2)}) collective-permute-start(bf16[2,2,2,64,2048]{4,3,2,1,0:T(8,128)(2,1)} %pile.5.refs_1_.refs_2_.refs_5_), channel_id=1, source_target_pairs={{0,2},{2,0},{1,3},{3,1},{4,6},{6,4},{5,7},{7,5},{8,10},{10,8},{9,1... | collective-permute-start | bytes 6291464 | tf_op jit(solution)/shard_map/ppermute | solution.py:1085
  154.1 1.1 copy-start.33
  154.9 43.7 %collective-permute-start.5 = (bf16[2,2,2,64,2048]{4,3,2,1,0:T(8,128)(2,1)}, bf16[2,2,2,64,2048]{4,3,2,1,0:T(8,128)(2,1)}, u32[]{:S(2)}, u32[]{:S(2)}) collective-permute-start(bf16[2,2,2,64,2048]{4,3,2,1,0:T(8,128)(2,1)} %get-tuple-element.109.refs_4_.refs_5_), channel_id=1, source_target_pairs={{0,2},{2,0},{1,3},{3,1},{4,6},{6,4},{5,7},{7,5},{8,10},{10,8},{9,1... | collective-permute-start | bytes 6291464 | tf_op jit(solution)/shard_map/ppermute | solution.py:1085
  198.6 1.4 copy-start.2
  279.2 30.0 %collective-permute-start.6 = (bf16[2,2,2,64,2048]{4,3,2,1,0:T(8,128)(2,1)}, bf16[2,2,2,64,2048]{4,3,2,1,0:T(8,128)(2,1)}, u32[]{:S(2)}, u32[]{:S(2)}) collective-permute-start(bf16[2,2,2,64,2048]{4,3,2,1,0:T(8,128)(2,1)} %get-tuple-element.123), channel_id=1, source_target_pairs={{0,2},{2,0},{1,3},{3,1},{4,6},{6,4},{5,7},{7,5},{8,10},{10,8},{9,1... | collective-permute-start | bytes 6291464 | tf_op jit(solution)/shard_map/ppermute | solution.py:1085
  279.5 29.7 %collective-permute-start.7 = (bf16[2,2,2,64,2048]{4,3,2,1,0:T(8,128)(2,1)}, bf16[2,2,2,64,2048]{4,3,2,1,0:T(8,128)(2,1)S(1)}, u32[]{:S(2)}, u32[]{:S(2)}) collective-permute-start(bf16[2,2,2,64,2048]{4,3,2,1,0:T(8,128)(2,1)} %get-tuple-element.125), channel_id=1, source_target_pairs={{0,2},{2,0},{1,3},{3,1},{4,6},{6,4},{5,7},{7,5},{8,10},{10,8},{9,1... | collective-permute-start | bytes 6291464 | tf_op jit(solution)/shard_map/ppermute | solution.py:1085
  309.2 1.3 copy-start.6
  316.1 14.8 %collective-permute-start.8 = (bf16[2,2,2,64,2048]{4,3,2,1,0:T(8,128)(2,1)}, bf16[2,2,2,64,2048]{4,3,2,1,0:T(8,128)(2,1)S(1)}, u32[]{:S(2)}, u32[]{:S(2)}) collective-permute-start(bf16[2,2,2,64,2048]{4,3,2,1,0:T(8,128)(2,1)} %get-tuple-element.138), channel_id=1, source_target_pairs={{0,2},{2,0},{1,3},{3,1},{4,6},{6,4},{5,7},{7,5},{8,10},{10,8},{9,1... | collective-permute-start | bytes 6291464 | tf_op jit(solution)/shard_map/ppermute | solution.py:1085
  316.4 14.5 %collective-permute-start.11 = (bf16[2,2,2,64,2048]{4,3,2,1,0:T(8,128)(2,1)}, bf16[2,2,2,64,2048]{4,3,2,1,0:T(8,128)(2,1)}, u32[]{:S(2)}, u32[]{:S(2)}) collective-permute-start(bf16[2,2,2,64,2048]{4,3,2,1,0:T(8,128)(2,1)} %get-tuple-element.143), channel_id=1, source_target_pairs={{0,2},{2,0},{1,3},{3,1},{4,6},{6,4},{5,7},{7,5},{8,10},{10,8},{9,1... | collective-permute-start | bytes 6291464 | tf_op jit(solution)/shard_map/ppermute | solution.py:1085
  327.6 54.2 %collective-permute-start.9 = (bf16[2,2,2,64,2048]{4,3,2,1,0:T(8,128)(2,1)}, bf16[2,2,2,64,2048]{4,3,2,1,0:T(8,128)(2,1)}, u32[]{:S(2)}, u32[]{:S(2)}) collective-permute-start(bf16[2,2,2,64,2048]{4,3,2,1,0:T(8,128)(2,1)} %get-tuple-element.139), channel_id=1, source_target_pairs={{0,1},{1,0},{2,3},{3,2},{4,5},{5,4},{6,7},{7,6},{8,9},{9,8},{10,11... | collective-permute-start | bytes 6291464 | tf_op jit(solution)/shard_map/ppermute | solution.py:1085
  329.1 51.0 %collective-permute-start.10 = (bf16[2,2,64,2048]{3,2,1,0:T(8,128)(2,1)}, bf16[2,2,64,2048]{3,2,1,0:T(8,128)(2,1)S(1)}, u32[]{:S(2)}, u32[]{:S(2)}) collective-permute-start(bf16[2,2,64,2048]{3,2,1,0:T(8,128)(2,1)} %get-tuple-element.140), channel_id=1, source_target_pairs={{0,4},{4,0},{1,5},{5,1},{2,6},{6,2},{3,7},{7,3},{8,12},{12,8},{9,1... | collective-permute-start | bytes 3145736 | tf_op jit(solution)/shard_map/ppermute | solution.py:1085
  330.9 1.4 copy-start.3
  335.8 46.4 %collective-permute-start.12 = (bf16[2,2,64,2048]{3,2,1,0:T(8,128)(2,1)}, bf16[2,2,64,2048]{3,2,1,0:T(8,128)(2,1)S(1)}, u32[]{:S(2)}, u32[]{:S(2)}) collective-permute-start(bf16[2,2,64,2048]{3,2,1,0:T(8,128)(2,1)} %get-tuple-element.147), channel_id=1, source_target_pairs={{0,4},{4,0},{1,5},{5,1},{2,6},{6,2},{3,7},{7,3},{8,12},{12,8},{9,1... | collective-permute-start | bytes 3145736 | tf_op jit(solution)/shard_map/ppermute | solution.py:1085
  380.1 2.1 copy-start.12
  382.2 1.0 copy-start.7
  388.4 37.8 %collective-permute-start.13 = (bf16[2,2,64,2048]{3,2,1,0:T(8,128)(2,1)}, bf16[2,2,64,2048]{3,2,1,0:T(8,128)(2,1)S(1)}, u32[]{:S(2)}, u32[]{:S(2)}) collective-permute-start(bf16[2,2,64,2048]{3,2,1,0:T(8,128)(2,1)} %get-tuple-element.148), channel_id=1, source_target_pairs={{0,4},{4,0},{1,5},{5,1},{2,6},{6,2},{3,7},{7,3},{8,12},{12,8},{9,1... | collective-permute-start | bytes 3145736 | tf_op jit(solution)/shard_map/ppermute | solution.py:1085
  391.0 35.1 %collective-permute-start.14 = (bf16[2,2,64,2048]{3,2,1,0:T(8,128)(2,1)}, bf16[2,2,64,2048]{3,2,1,0:T(8,128)(2,1)S(1)}, u32[]{:S(2)}, u32[]{:S(2)}) collective-permute-start(bf16[2,2,64,2048]{3,2,1,0:T(8,128)(2,1)} %get-tuple-element.149), channel_id=1, source_target_pairs={{0,1},{1,0},{2,3},{3,2},{4,5},{5,4},{6,7},{7,6},{8,9},{9,8},{10,11... | collective-permute-start | bytes 3145736 | tf_op jit(solution)/shard_map/ppermute | solution.py:1085
  426.2 1.0 copy-start.13
  426.2 1.3 copy-start.14
  434.1 31.4 %collective-permute-start.17 = (bf16[2,64,4096]{2,1,0:T(8,128)(2,1)}, bf16[2,64,4096]{2,1,0:T(8,128)(2,1)S(1)}, u32[]{:S(2)}, u32[]{:S(2)}) collective-permute-start(bf16[2,64,4096]{2,1,0:T(8,128)(2,1)} %get-tuple-element.159), channel_id=1, source_target_pairs={{0,8},{8,0},{16,24},{24,16},{1,9},{9,1},{17,25},{25,17},{2,10},{10... | collective-permute-start | bytes 3145736 | tf_op jit(solution)/shard_map/ppermute | solution.py:1089
  465.0 7.3 %collective-permute-start.15 = (bf16[2,2,2,2,2,64,512]{6,5,4,3,2,1,0:T(8,128)(2,1)}, bf16[2,2,2,2,2,64,512]{6,5,4,3,2,1,0:T(8,128)(2,1)S(1)}, u32[]{:S(2)}, u32[]{:S(2)}) collective-permute-start(bf16[2,2,2,2,2,64,512]{6,5,4,3,2,1,0:T(8,128)(2,1)} %get-tuple-element.155), channel_id=1, source_target_pairs={{0,2},{2,0},{1,3},{3,1},{4,6},{6,4},{5,7},{7,5},{8,10},{10,8},{9,1... | collective-permute-start | bytes 6291464 | tf_op jit(solution)/shard_map/ppermute | solution.py:1085
  465.0 7.5 %collective-permute-start.16 = (bf16[2,2,2,2,2,64,512]{6,5,4,3,2,1,0:T(8,128)(2,1)}, bf16[2,2,2,2,2,64,512]{6,5,4,3,2,1,0:T(8,128)(2,1)}, u32[]{:S(2)}, u32[]{:S(2)}) collective-permute-start(bf16[2,2,2,2,2,64,512]{6,5,4,3,2,1,0:T(8,128)(2,1)} %get-tuple-element.157), channel_id=1, source_target_pairs={{0,2},{2,0},{1,3},{3,1},{4,6},{6,4},{5,7},{7,5},{8,10},{10,8},{9,1... | collective-permute-start | bytes 6291464 | tf_op jit(solution)/shard_map/ppermute | solution.py:1085
  465.5 1.0 copy-start.31
  472.3 1.4 copy-start.1
  473.7 5.6 copy-start.32
  478.3 26.6 %collective-permute-start.18 = (bf16[2,2,2,2,64,512]{5,4,3,2,1,0:T(8,128)(2,1)}, bf16[2,2,2,2,64,512]{5,4,3,2,1,0:T(8,128)(2,1)S(1)}, u32[]{:S(2)}, u32[]{:S(2)}) collective-permute-start(bf16[2,2,2,2,64,512]{5,4,3,2,1,0:T(8,128)(2,1)} %get-tuple-element.161), channel_id=1, source_target_pairs={{0,1},{1,0},{2,3},{3,2},{4,5},{5,4},{6,7},{7,6},{8,9},{9,8},{10,11... | collective-permute-start | bytes 3145736 | tf_op jit(solution)/shard_map/ppermute | solution.py:1085
  479.0 25.9 %collective-permute-start.20 = (bf16[2,2,2,2,64,512]{5,4,3,2,1,0:T(8,128)(2,1)}, bf16[2,2,2,2,64,512]{5,4,3,2,1,0:T(8,128)(2,1)S(1)}, u32[]{:S(2)}, u32[]{:S(2)}) collective-permute-start(bf16[2,2,2,2,64,512]{5,4,3,2,1,0:T(8,128)(2,1)} %get-tuple-element.164), channel_id=1, source_target_pairs={{0,4},{4,0},{1,5},{5,1},{2,6},{6,2},{3,7},{7,3},{8,12},{12,8},{9,1... | collective-permute-start | bytes 3145736 | tf_op jit(solution)/shard_map/ppermute | solution.py:1085
  479.3 25.5 %collective-permute-start.19 = (bf16[64,4096]{1,0:T(8,128)(2,1)S(1)}, bf16[64,4096]{1,0:T(8,128)(2,1)S(1)}, u32[]{:S(2)}, u32[]{:S(2)}) collective-permute-start(bf16[64,4096]{1,0:T(8,128)(2,1)S(1)} %copy-done.32), channel_id=1, source_target_pairs={{0,16},{8,24},{16,0},{24,8},{1,17},{9,25},{17,1},{25,9},{2,18},{10... | collective-permute-start | bytes 1572872 | tf_op jit(solution)/shard_map/ppermute | solution.py:1089
  489.3 15.5 %collective-permute-start.21 = (f32[8,1024]{1,0:T(8,128)}, f32[8,1024]{1,0:T(8,128)S(1)}, u32[]{:S(2)}, u32[]{:S(2)}) collective-permute-start(f32[8,1024]{1,0:T(8,128)} %get-tuple-element.167.refs_8_), channel_id=1, source_target_pairs={{0,2},{2,0},{1,3},{3,1},{4,6},{6,4},{5,7},{7,5},{8,10},{10,8},{9,1... | collective-permute-start | bytes 98312 | tf_op jit(solution)/shard_map/ppermute | solution.py:1085
  504.9 1.2 copy-start.4
  504.9 1.5 copy-start.5
  510.8 16.0 %collective-permute-start.24 = (bf16[2,2,2,2,2,64,512]{6,5,4,3,2,1,0:T(8,128)(2,1)}, bf16[2,2,2,2,2,64,512]{6,5,4,3,2,1,0:T(8,128)(2,1)S(1)}, u32[]{:S(2)}, u32[]{:S(2)}) collective-permute-start(bf16[2,2,2,2,2,64,512]{6,5,4,3,2,1,0:T(8,128)(2,1)} %get-tuple-element.173), channel_id=1, source_target_pairs={{0,2},{2,0},{1,3},{3,1},{4,6},{6,4},{5,7},{7,5},{8,10},{10,8},{9,1... | collective-permute-start | bytes 6291464 | tf_op jit(solution)/shard_map/ppermute | solution.py:1085
  510.8 14.5 %collective-permute-start.22 = (bf16[2,2,2,64,512]{4,3,2,1,0:T(8,128)(2,1)}, bf16[2,2,2,64,512]{4,3,2,1,0:T(8,128)(2,1)S(1)}, u32[]{:S(2)}, u32[]{:S(2)}) collective-permute-start(bf16[2,2,2,64,512]{4,3,2,1,0:T(8,128)(2,1)} %get-tuple-element.170), channel_id=1, source_target_pairs={{0,4},{4,0},{1,5},{5,1},{2,6},{6,2},{3,7},{7,3},{8,12},{12,8},{9,1... | collective-permute-start | bytes 1572872 | tf_op jit(solution)/shard_map/ppermute | solution.py:1085
  512.6 14.2 %collective-permute-start.23 = (bf16[2,2,2,64,512]{4,3,2,1,0:T(8,128)(2,1)}, bf16[2,2,2,64,512]{4,3,2,1,0:T(8,128)(2,1)S(1)}, u32[]{:S(2)}, u32[]{:S(2)}) collective-permute-start(bf16[2,2,2,64,512]{4,3,2,1,0:T(8,128)(2,1)} %get-tuple-element.171), channel_id=1, source_target_pairs={{0,1},{1,0},{2,3},{3,2},{4,5},{5,4},{6,7},{7,6},{8,9},{9,8},{10,11... | collective-permute-start | bytes 1572872 | tf_op jit(solution)/shard_map/ppermute | solution.py:1085
  513.8 9.6 %collective-permute-start.25 = (f32[8,1024]{1,0:T(8,128)}, f32[8,1024]{1,0:T(8,128)S(1)}, u32[]{:S(2)}, u32[]{:S(2)}) collective-permute-start(f32[8,1024]{1,0:T(8,128)} %get-tuple-element.174.refs_20_), channel_id=1, source_target_pairs={{0,8},{8,0},{16,24},{24,16},{1,9},{9,1},{17,25},{25,17},{2,10},{10... | collective-permute-start | bytes 98312 | tf_op jit(solution)/shard_map/ppermute | solution.py:1089
  523.3 3.5 copy-start.27
  525.4 1.4 copy-start.8
  526.8 1.5 copy-start
  533.5 3.4 copy-start.25
  533.5 13.4 %collective-permute-start.26 = (bf16[2,2,2,64,512]{4,3,2,1,0:T(8,128)(2,1)}, bf16[2,2,2,64,512]{4,3,2,1,0:T(8,128)(2,1)S(1)}, u32[]{:S(2)}, u32[]{:S(2)}) collective-permute-start(bf16[2,2,2,64,512]{4,3,2,1,0:T(8,128)(2,1)} %get-tuple-element.179), channel_id=1, source_target_pairs={{0,1},{1,0},{2,3},{3,2},{4,5},{5,4},{6,7},{7,6},{8,9},{9,8},{10,11... | collective-permute-start | bytes 1572872 | tf_op jit(solution)/shard_map/ppermute | solution.py:1085
  534.7 13.1 %collective-permute-start.27 = (bf16[2,2,2,64,512]{4,3,2,1,0:T(8,128)(2,1)}, bf16[2,2,2,64,512]{4,3,2,1,0:T(8,128)(2,1)S(1)}, u32[]{:S(2)}, u32[]{:S(2)}) collective-permute-start(bf16[2,2,2,64,512]{4,3,2,1,0:T(8,128)(2,1)} %get-tuple-element.180), channel_id=1, source_target_pairs={{0,4},{4,0},{1,5},{5,1},{2,6},{6,2},{3,7},{7,3},{8,12},{12,8},{9,1... | collective-permute-start | bytes 1572872 | tf_op jit(solution)/shard_map/ppermute | solution.py:1085
  535.2 13.8 %collective-permute-start.29 = (bf16[2,64,2048]{2,1,0:T(8,128)(2,1)}, bf16[2,64,2048]{2,1,0:T(8,128)(2,1)S(1)}, u32[]{:S(2)}, u32[]{:S(2)}) collective-permute-start(bf16[2,64,2048]{2,1,0:T(8,128)(2,1)} %get-tuple-element.183), channel_id=1, source_target_pairs={{0,8},{8,0},{16,24},{24,16},{1,9},{9,1},{17,25},{25,17},{2,10},{10... | collective-permute-start | bytes 1572872 | tf_op jit(solution)/shard_map/ppermute | solution.py:1089
  536.9 9.9 %collective-permute-start.28 = (f32[8,1024]{1,0:T(8,128)S(1)}, f32[8,1024]{1,0:T(8,128)S(1)}, u32[]{:S(2)}, u32[]{:S(2)}) collective-permute-start(f32[8,1024]{1,0:T(8,128)S(1)} %copy-done.25), channel_id=1, source_target_pairs={{0,16},{8,24},{16,0},{24,8},{1,17},{9,25},{17,1},{25,9},{2,18},{10... | collective-permute-start | bytes 98312 | tf_op jit(solution)/shard_map/ppermute | solution.py:1089
  546.8 2.2 copy-start.29
  546.9 2.1 copy-start.10
  547.8 1.2 copy-start.11
  553.5 8.2 %collective-permute-start.30 = (bf16[2,2,64,512]{3,2,1,0:T(8,128)(2,1)}, bf16[2,2,64,512]{3,2,1,0:T(8,128)(2,1)S(1)}, u32[]{:S(2)}, u32[]{:S(2)}) collective-permute-start(bf16[2,2,64,512]{3,2,1,0:T(8,128)(2,1)} %get-tuple-element.184), channel_id=1, source_target_pairs={{0,4},{4,0},{1,5},{5,1},{2,6},{6,2},{3,7},{7,3},{8,12},{12,8},{9,1... | collective-permute-start | bytes 786440 | tf_op jit(solution)/shard_map/ppermute | solution.py:1085
  554.8 6.9 %collective-permute-start.31 = (bf16[2,2,64,512]{3,2,1,0:T(8,128)(2,1)}, bf16[2,2,64,512]{3,2,1,0:T(8,128)(2,1)S(1)}, u32[]{:S(2)}, u32[]{:S(2)}) collective-permute-start(bf16[2,2,64,512]{3,2,1,0:T(8,128)(2,1)} %get-tuple-element.185), channel_id=1, source_target_pairs={{0,1},{1,0},{2,3},{3,2},{4,5},{5,4},{6,7},{7,6},{8,9},{9,8},{10,11... | collective-permute-start | bytes 786440 | tf_op jit(solution)/shard_map/ppermute | solution.py:1085
  556.1 5.6 collective-permute-start.32
  559.7 8.7 %copy-start.16 = (f32[64,4096]{1,0:T(8,128)S(1)}, f32[64,4096]{1,0:T(8,128)}, u32[]{:S(2)}) copy-start(f32[64,4096]{1,0:T(8,128)} %get-tuple-element.196) | copy-start | bytes 3145732
  559.7 12.1 %collective-permute-start.34 = (bf16[64,2048]{1,0:T(8,128)(2,1)}, bf16[64,2048]{1,0:T(8,128)(2,1)S(1)}, u32[]{:S(2)}, u32[]{:S(2)}) collective-permute-start(bf16[64,2048]{1,0:T(8,128)(2,1)} %get-tuple-element.190), channel_id=1, source_target_pairs={{0,16},{8,24},{16,0},{24,8},{1,17},{9,25},{17,1},{25,9},{2,18},{10... | collective-permute-start | bytes 786440 | tf_op jit(solution)/shard_map/ppermute | solution.py:1089
  566.4 5.5 collective-permute-start.35
  567.2 8.8 %collective-permute-start.33 = (bf16[2,64,1024]{2,1,0:T(8,128)(2,1)}, bf16[2,64,1024]{2,1,0:T(8,128)(2,1)S(1)}, u32[]{:S(2)}, u32[]{:S(2)}) collective-permute-start(bf16[2,64,1024]{2,1,0:T(8,128)(2,1)} %get-tuple-element.188), channel_id=1, source_target_pairs={{0,8},{8,0},{16,24},{24,16},{1,9},{9,1},{17,25},{25,17},{2,10},{10... | collective-permute-start | bytes 786440 | tf_op jit(solution)/shard_map/ppermute | solution.py:1089
  571.8 4.2 copy-start.23
  571.8 4.2 copy-start.30
  580.4 7.9 %collective-permute-start.36 = (bf16[64,1024]{1,0:T(8,128)(2,1)}, bf16[64,1024]{1,0:T(8,128)(2,1)S(1)}, u32[]{:S(2)}, u32[]{:S(2)}) collective-permute-start(bf16[64,1024]{1,0:T(8,128)(2,1)} %get-tuple-element.193), channel_id=1, source_target_pairs={{0,16},{8,24},{16,0},{24,8},{1,17},{9,25},{17,1},{25,9},{2,18},{10... | collective-permute-start | bytes 393224 | tf_op jit(solution)/shard_map/ppermute | solution.py:1089
  (10 other events, 7.4 us)
Sparse Core Ops, SparseCore 0:
  11.4 118.3 all-gather.6
  132.8 78.7 all-gather.8
  327.7 61.6 all-gather.10

commit v2 on v1

--- a/solution.py
+++ b/solution.py
@@ -1212,8 +1212,8 @@
         (gs0, e0s, d0s),
     )
     e1x, d1y, e0c, d0c = swap(e1x, "x"), swap(d1y, "y"), swap(e0s, "c"), swap(d0s, "c")
-    grad_after, branch, sums_two = norm_backward(
-        where, after_attn, upstream, vec, 4, [gs0, gs1], (down_bias, energy, alive, hb0, hb1)
+    branch, sums_two = norm_backward(
+        where, after_attn, upstream, vec, 4, [gs0, gs1], (down_bias, energy, alive, hb0, hb1), True
     )
     parcel = lax.all_gather(sums_two, everyone, axis=0, tiled=False)
     d0y, branch = fold(
@@ -1268,7 +1268,7 @@
         (grad_first,),
     )
     qk_x, vo_y, ends_z = swap(qk_x, "x"), swap(vo_y, "y"), swap_line(ends_z, 2)
-    merge_grad, three = norm_backward(where, merged, grad_after, vec, 1, [grad_first], last=True)
+    merge_grad, three = norm_backward(where, merged, branch, vec, 1, [grad_first], last=True)
     m0, m1 = merge_weight(where, entering_states, bypass_states, merge_grad, r)
     three_c = swap(three, "c")
     ends, qk_y, vo_x, three, merge_grad, m1 = fold(

time: 609 us -> 607 us (level)
  transfers between devices with their start and end apart: 40 -> 40, of which waited for: 19 -> 18; matrix products, arithmetic and copies ran while one was open for 2% -> 2% of each run, Pallas kernels for 50% -> 49%
where the time goes in v2:
time: 607 us; the launch traced here: 596 us
  Pallas kernels  376 us (62%)
  waiting for transfers between devices  133 us (22%)
  starting transfers between devices  36.6 us (6%)
  local copies, waits for them, and re-layouts  27 us (4%)
  between operations  17.6 us (3%)
  other arithmetic  6.19 us (1%)
    pallas_call x33, Pallas kernels, call(): pl.pallas_call(ordered_kernel, grid_spec=pltpu.PrefetchScalarGridSpec(num...  376 us
    ppermute x10, waiting for transfers between devices, swap_line(): return lax.ppermute(value, 'z', [(i, i ^ bit) for i in range(4)])  61.3 us
    ppermute x27, waiting for transfers between devices, swap(): return lax.ppermute(value, axis, [(0, 1), (1, 0)])  40.7 us
    all_gather x1, waiting for transfers between devices, one_sequence_plan(): pack = lax.all_gather(pack, everyone, axis=0, tiled=False)  30.5 us
    ppermute x27, starting transfers between devices, swap(): return lax.ppermute(value, axis, [(0, 1), (1, 0)])  19.2 us
    ppermute x10, starting transfers between devices, swap_line(): return lax.ppermute(value, 'z', [(i, i ^ bit) for i in range(4)])  17.2 us
    unnamed x70, local copies, waits for them, and re-layouts  16.7 us
  transfers between devices with their start and end apart: 40, of which 18 were waited for; matrix products, arithmetic and copies ran while one was open for 2% of the time, Pallas kernels for 49%

profile of v2, /device:TPU:0, one launch (start us, length us, event | category | flops | bytes accessed | tf_op | source)
XLA Modules:
  0.0 596.3 jit_solution(2825728149121694812)
XLA Ops:
  8.7 1.8 pad_maximum_fusion
  11.3 4.1 collective-permute-start
  16.0 14.5 %collective-permute-done.refs_1_ = bf16[64,2048]{1,0:T(8,128)(2,1)S(1)} collective-permute-done((bf16[64,2048]{1,0:T(8,128)(2,1)}, bf16[64,2048]{1,0:T(8,128)(2,1)S(1)}, u32[]{:S(2)}, u32[]{:S(2)}) %collective-permute-start) | collective-permute-done | bytes 262176 | tf_op jit(solution)/shard_map/ppermute | solution.py:1089
  31.3 2.5 pile.3.refs_0_
  33.8 3.6 collective-permute-start.1
  37.4 21.4 %collective-permute-done.1.refs_1_ = bf16[2,64,2048]{2,1,0:T(8,128)(2,1)S(1)} collective-permute-done((bf16[2,64,2048]{2,1,0:T(8,128)(2,1)}, bf16[2,64,2048]{2,1,0:T(8,128)(2,1)S(1)}, u32[]{:S(2)}, u32[]{:S(2)}) %collective-permute-start.1) | collective-permute-done | bytes 524320 | tf_op jit(solution)/shard_map/ppermute | solution.py:1089
  59.6 2.9 pile.4.refs_0_
  63.1 31.4 %collective-permute-done.2.refs_1_ = bf16[2,2,64,2048]{3,2,1,0:T(8,128)(2,1)S(1)} collective-permute-done((bf16[2,2,64,2048]{3,2,1,0:T(8,128)(2,1)}, bf16[2,2,64,2048]{3,2,1,0:T(8,128)(2,1)S(1)}, u32[]{:S(2)}, u32[]{:S(2)}) %collective-permute-start.2) | collective-permute-done | bytes 1048608 | tf_op jit(solution)/shard_map/ppermute | solution.py:1085
  95.4 3.7 pile.5.refs_1_.refs_2_.refs_5_
  99.1 30.5 %all-gather.7.cloned.1.call-done = bf16[6400,1024]{1,0:T(8,128)(2,1)} async-done(((bf16[200,1024]{1,0:T(8,128)(2,1)}), bf16[6400,1024]{1,0:T(8,128)(2,1)}) %all-gather.7.cloned.1.call-update) | async-done | bytes 13107216 | tf_op jit(solution)/shard_map/all_gather | solution.py:1161
  132.4 21.4 %project_forward.1 = (f32[1104,1024]{1,0:T(8,128)}, bf16[1104,1024]{1,0:T(8,128)(2,1)}, bf16[1104,3072]{1,0:T(8,128)(2,1)}) custom-call(s32[5]{0:T(128)} %stack.23.where_ref, bf16[1104,1024]{1,0:T(8,128)(2,1)} %refs_0_.5, bf16[1104,1024]{1,0:T(8,128)(2,1)} %refs_1_.3, bf16[2,2,2,2,2,200,1024]{6,5,4,3,2,1,0:T(8,128)(2,1)} %gate.3.refs_2_.refs_4_.refs_3_.refs_1_, ...), custom_call_target="tpu_custom_call" | custom-call | tf_op jit(solution)/shard_map/project_forward/pallas_call | solution.py:449
  156.8 31.5 %attention_forward.1 = (bf16[1104,1024]{1,0:T(8,128)(2,1)}, f32[1104,1024]{1,0:T(8,128)}) custom-call(s32[5]{0:T(128)} %stack.23.where_ref, bf16[1104,3072]{1,0:T(8,128)(2,1)} %get-tuple-element.109.refs_0_.refs_1_.refs_2_, bf16[1104,3072]{1,0:T(8,128)(2,1)} %get-tuple-element.109.refs_0_.refs_1_.refs_2_, ...), custom_call_target="tpu_custom_call" | custom-call | tf_op jit(solution)/shard_map/attention_forward/pallas_call | solution.py:449
  188.3 10.0 %result_forward.1 = (f32[1104,1024]{1,0:T(8,128)}, bf16[1104,1024]{1,0:T(8,128)(2,1)}) custom-call(s32[5]{0:T(128)} %stack.23.where_ref, bf16[1104,1024]{1,0:T(8,128)(2,1)} %get-tuple-element.110.refs_0_.refs_1_.refs_3_, f32[1104,1024]{1,0:T(8,128)} %get-tuple-element.111.refs_1_.refs_0_, f32[8,1024]{1,0:T(8,128)} %pad.14.refs_3_.refs_2_.refs_4_, ...), custom_call_target="tpu_custom_call" | custom-call | tf_op jit(solution)/shard_map/result_forward/pallas_call | solution.py:449
  198.4 1.3 copy-done.2
  200.4 29.8 %expand_forward.1 = (bf16[2,1104,2048]{2,1,0:T(8,128)(2,1)}, bf16[2,1104,2048]{2,1,0:T(8,128)(2,1)}) custom-call(s32[5]{0:T(128)} %stack.23.where_ref, bf16[1104,1024]{1,0:T(8,128)(2,1)} %get-tuple-element.113.refs_0_.refs_1_, f32[2,1,2048]{2,1,0:T(1,128)} %bitcast.54, bf16[2,2,2,64,2048]{4,3,2,1,0:T(8,128)(2,1)} %pile.5.refs_1_.refs_2_.refs_5_, ...), custom_call_target="tpu_custom_call" | custom-call | tf_op jit(solution)/shard_map/expand_forward/pallas_call | solution.py:449
  230.2 19.0 %contract_forward.1 = (bf16[1104,1024]{1,0:T(8,128)(2,1)}, bf16[1104,1024]{1,0:T(8,128)(2,1)}, f32[8,1024]{1,0:T(8,128)}, f32[8,128]{1,0:T(8,128)}) custom-call(s32[5]{0:T(128)} %stack.23.where_ref, f32[1]{0:T(128)S(6)} %convert_element_type.15.refs_0_.refs_7_, bf16[2,1104,2048]{2,1,0:T(8,128)(2,1)} %get-tuple-element.116.refs_1_.refs_2_, ...), custom_call_target="tpu_custom_call" | custom-call | tf_op jit(solution)/shard_map/contract_forward/pallas_call | solution.py:449
  249.2 29.8 %feed_backward.2 = (bf16[1104,1024]{1,0:T(8,128)(2,1)}, bf16[2,2,2,64,2048]{4,3,2,1,0:T(8,128)(2,1)}, bf16[2,2,2,64,2048]{4,3,2,1,0:T(8,128)(2,1)}, bf16[2,2,2,6...) custom-call(s32[5]{0:T(128)} %stack.23.where_ref, ...), custom_call_target="tpu_custom_call" | custom-call | tf_op jit(solution)/shard_map/feed_backward/pallas_call | solution.py:449
  279.6 29.4 %feed_backward.3 = (bf16[1104,1024]{1,0:T(8,128)(2,1)}, bf16[2,2,2,64,2048]{4,3,2,1,0:T(8,128)(2,1)}, bf16[2,2,2,64,2048]{4,3,2,1,0:T(8,128)(2,1)}, bf16[2,2,2,6...) custom-call(s32[5]{0:T(128)} %stack.23.where_ref, ...), custom_call_target="tpu_custom_call" | custom-call | tf_op jit(solution)/shard_map/feed_backward/pallas_call | solution.py:449
  309.0 1.4 copy-done.6
  310.4 5.7 fold.11
  316.6 9.1 %norm_backward.2 = (bf16[1104,1024]{1,0:T(8,128)(2,1)}, f32[16,1024]{1,0:T(8,128)}) custom-call(s32[5]{0:T(128)} %stack.23.where_ref, f32[1104,1024]{1,0:T(8,128)} %get-tuple-element.117.refs_2_.refs_0_, bf16[1104,1024]{1,0:T(8,128)(2,1)} %get-tuple-element.119.refs_0_.refs_1_, f32[8,1024]{1,0:T(8,128)} %pad.14.refs_3_.refs_2_.refs_4_, ...), custom_call_target="tpu_custom_call" | custom-call | tf_op jit(solution)/shard_map/norm_backward/pallas_call | solution.py:449
  325.7 1.7 collective-permute-start.9
  327.5 1.9 collective-permute-start.10
  329.3 1.3 copy-done.3
  330.7 3.4 fold.12
  334.2 9.6 %result_backward.1 = (bf16[1104,1024]{1,0:T(8,128)(2,1)}, bf16[2,2,2,2,2,64,512]{6,5,4,3,2,1,0:T(8,128)(2,1)}, bf16[2,2,2,2,2,64,512]{6,5,4,3,2,1,0:T(8,128)(2,1)}) custom-call(s32[5]{0:T(128)} %stack.23.where_ref, bf16[1104,1024]{1,0:T(8,128)(2,1)} %get-tuple-element.144.refs_0_.refs_1_, bf16[1104,1024]{1,0:T(8,128)(2,1)} %get-tuple-element.110.refs_0_.refs_1_.refs_3_, ...), custom_call_target="tpu_custom_call" | custom-call | tf_op jit(solution)/shard_map/result_backward/pallas_call | solution.py:449
  343.8 34.6 %attention_backward.2.refs_6_ = bf16[3,1104,1024]{2,1,0:T(8,128)(2,1)} custom-call(s32[5]{0:T(128)} %stack.23.where_ref, bf16[1104,3072]{1,0:T(8,128)(2,1)} %get-tuple-element.109.refs_0_.refs_1_.refs_2_, bf16[1104,3072]{1,0:T(8,128)(2,1)} %get-tuple-element.109.refs_0_.refs_1_.refs_2_, bf16[1104,3072]{1,0:T(8,128)(2,1)} %get-tuple-element.109.refs_0_.refs_1_.refs_2_, ...), custom_call_target="tpu_custom_call" | custom-call | tf_op jit(solution)/shard_map/attention_backward/pallas_call | solution.py:449
  378.4 1.5 collective-permute-done.9.refs_2_
  381.6 5.2 fold.13
  386.8 2.3 collective-permute-start.13
  389.8 34.4 %attention_backward.3.refs_8_ = bf16[3,1104,1024]{2,1,0:T(8,128)(2,1)} custom-call(s32[5]{0:T(128)} %stack.23.where_ref, bf16[1104,3072]{1,0:T(8,128)(2,1)} %get-tuple-element.109.refs_0_.refs_1_.refs_2_, bf16[1104,3072]{1,0:T(8,128)(2,1)} %get-tuple-element.109.refs_0_.refs_1_.refs_2_, ...), custom_call_target="tpu_custom_call", output_to_operand_aliasing={{}: (7, {})} | custom-call | tf_op jit(solution)/shard_map/attention_backward/pallas_call | solution.py:449
  425.5 6.7 %fold.14 = (f32[2,64,4096]{2,1,0:T(8,128)}, bf16[2,64,4096]{2,1,0:T(8,128)(2,1)}, bf16[3,1104,1024]{2,1,0:T(8,128)(2,1)}) custom-call(s32[5]{0:T(128)} %stack.23.where_ref, bf16[2,2,2,64,2048]{4,3,2,1,0:T(8,128)(2,1)} %get-tuple-element.136.refs_0_, bf16[2,2,2,64,2048]{4,3,2,1,0:T(8,128)(2,1)} %copy-done.3, ...), custom_call_target="tpu_custom_call", output_to_operand_aliasing={{2}: (9, {})} | custom-call | tf_op jit(solution)/shard_map/fold/pallas_call | solution.py:449
  432.2 2.3 collective-permute-start.17
  434.5 14.4 %project_backward.1.refs_2_ = bf16[1104,1024]{1,0:T(8,128)(2,1)} custom-call(s32[5]{0:T(128)} %stack.23.where_ref, bf16[3,1104,1024]{2,1,0:T(8,128)(2,1)} %get-tuple-element.150.refs_1_.refs_0_, bf16[2,2,2,2,2,200,1024]{6,5,4,3,2,1,0:T(8,128)(2,1)} %gate.3.refs_2_.refs_4_.refs_3_.refs_1_), custom_call_target="tpu_custom_call" | custom-call | tf_op jit(solution)/shard_map/project_backward/pallas_call | solution.py:449
  448.9 14.4 %project_weight.1 = (bf16[2,2,2,2,2,64,512]{6,5,4,3,2,1,0:T(8,128)(2,1)}, bf16[2,2,2,2,2,64,512]{6,5,4,3,2,1,0:T(8,128)(2,1)}, bf16[2,2,2,2,2,64,512]{6,5,4,3,2,...) custom-call(s32[5]{0:T(128)} %stack.23.where_ref, ...), custom_call_target="tpu_custom_call", output_to_operand_aliasing={{2}: (3, {}), {3}: (4, {})} | custom-call | tf_op jit(solution)/shard_map/project_weight/pallas_call | solution.py:449
  464.8 3.8 fold.15
  468.6 1.9 collective-permute-done.15.refs_1_.refs_3_.refs_5_
  471.9 4.5 fold.16
  478.5 8.0 %norm_backward.3 = (bf16[1104,1024]{1,0:T(8,128)(2,1)}, f32[8,1024]{1,0:T(8,128)}) custom-call(s32[5]{0:T(128)} %stack.23.where_ref, f32[1104,1024]{1,0:T(8,128)} %get-tuple-element.111.refs_1_.refs_0_, bf16[1104,1024]{1,0:T(8,128)(2,1)} %get-tuple-element.144.refs_0_.refs_1_, f32[8,1024]{1,0:T(8,128)} %pad.14.refs_3_.refs_2_.refs_4_, ...), custom_call_target="tpu_custom_call" | custom-call | tf_op jit(solution)/shard_map/norm_backward/pallas_call | solution.py:449
  486.5 10.7 %merge_weight.1 = (bf16[2,2,2,2,2,64,512]{6,5,4,3,2,1,0:T(8,128)(2,1)}, bf16[2,2,2,2,2,64,512]{6,5,4,3,2,1,0:T(8,128)(2,1)}) custom-call(s32[5]{0:T(128)} %stack.23.where_ref, bf16[1104,1024]{1,0:T(8,128)(2,1)} %refs_0_.5, bf16[1104,1024]{1,0:T(8,128)(2,1)} %refs_1_.3, bf16[1104,1024]{1,0:T(8,128)(2,1)} %get-tuple-element.166.refs_2_.refs_10_), custom_call_target="tpu_custom_call" | custom-call | tf_op jit(solution)/shard_map/merge_weight/pallas_call | solution.py:449
  497.2 5.7 collective-permute-done.19.refs_1_
  504.4 4.5 fold.17
  508.9 1.7 collective-permute-start.22
  510.6 1.3 collective-permute-start.23
  511.9 9.5 %merge_backward.1 = (f32[1104,1024]{1,0:T(8,128)}, f32[1104,1024]{1,0:T(8,128)}) custom-call(s32[5]{0:T(128)} %stack.23.where_ref, bf16[1104,1024]{1,0:T(8,128)(2,1)} %get-tuple-element.173.refs_0_, bf16[2,2,2,2,2,200,1024]{6,5,4,3,2,1,0:T(8,128)(2,1)} %gate.3.refs_2_.refs_4_.refs_3_.refs_1_), custom_call_target="tpu_custom_call" | custom-call | tf_op jit(solution)/shard_map/merge_backward/pallas_call | solution.py:449
  521.5 2.0 collective-permute-done.22.refs_3_.refs_7_
  523.4 1.4 collective-permute-done.23.refs_11_.refs_15_
  526.3 5.2 fold.18
  531.6 1.4 collective-permute-start.26
  533.4 1.7 reduce_sum.9
  535.1 2.7 collective-permute-start.28
  537.9 7.1 %collective-permute-done.28.refs_7_ = f32[8,1024]{1,0:T(8,128)S(1)} collective-permute-done((f32[8,1024]{1,0:T(8,128)S(1)}, f32[8,1024]{1,0:T(8,128)S(1)}, u32[]{:S(2)}, u32[]{:S(2)}) %collective-permute-start.28) | collective-permute-done | bytes 32800 | tf_op jit(solution)/shard_map/ppermute | solution.py:1089
  548.0 3.7 fold.19
  551.7 1.3 collective-permute-start.30
  554.2 1.3 collective-permute-start.32
  557.9 1.5 collective-permute-start.34
  561.3 3.2 fold.20
  565.4 1.2 collective-permute-start.33
  567.7 2.3 collective-permute-done.34.refs_3_
  570.0 4.2 collective-permute-done.33.refs_1_
  574.9 3.0 fold.21
  579.2 1.9 slice_bitcast_fusion.1
  581.6 4.9 collective-permute-done.36
  586.6 1.7 convert_add_fusion
  (143 shorter events, 36.8 us)
Async XLA Ops:
  7.2 122.4 %all-gather.7.cloned.1.call-start = ((), (), s32[]{:S(2)}) async-start(), calls=%async_computation | async-start | bytes 13516800 | tf_op jit(solution)/shard_map/all_gather | solution.py:1161
  10.5 219.7 %all-gather.9.cloned.1.call-start = ((), (), s32[]{:S(2)}) async-start(), calls=%async_computation.1 | async-start | bytes 8650752 | tf_op jit(solution)/shard_map/all_gather | solution.py:1164
  11.3 412.9 %all-gather.11.cloned.1.call-start = ((), (), s32[]{:S(2)}) async-start(), calls=%async_computation.2 | async-start | bytes 2162688 | tf_op jit(solution)/shard_map/all_gather | solution.py:1218
  11.3 19.2 %collective-permute-start = (bf16[64,2048]{1,0:T(8,128)(2,1)}, bf16[64,2048]{1,0:T(8,128)(2,1)S(1)}, u32[]{:S(2)}, u32[]{:S(2)}) collective-permute-start(bf16[64,2048]{1,0:T(8,128)(2,1)} %refs_0_.3), channel_id=1, source_target_pairs={{0,16},{8,24},{16,0},{24,8},{1,17},{9,25},{17,1},{25,9},{2,18},{10... | collective-permute-start | bytes 786440 | tf_op jit(solution)/shard_map/ppermute | solution.py:1089
  33.8 25.0 %collective-permute-start.1 = (bf16[2,64,2048]{2,1,0:T(8,128)(2,1)}, bf16[2,64,2048]{2,1,0:T(8,128)(2,1)S(1)}, u32[]{:S(2)}, u32[]{:S(2)}) collective-permute-start(bf16[2,64,2048]{2,1,0:T(8,128)(2,1)} %pile.3.refs_0_), channel_id=1, source_target_pairs={{0,8},{8,0},{16,24},{24,16},{1,9},{9,1},{17,25},{25,17},{2,10},{10... | collective-permute-start | bytes 1572872 | tf_op jit(solution)/shard_map/ppermute | solution.py:1089
  62.5 32.0 %collective-permute-start.2 = (bf16[2,2,64,2048]{3,2,1,0:T(8,128)(2,1)}, bf16[2,2,64,2048]{3,2,1,0:T(8,128)(2,1)S(1)}, u32[]{:S(2)}, u32[]{:S(2)}) collective-permute-start(bf16[2,2,64,2048]{3,2,1,0:T(8,128)(2,1)} %pile.4.refs_0_), channel_id=1, source_target_pairs={{0,4},{4,0},{1,5},{5,1},{2,6},{6,2},{3,7},{7,3},{8,12},{12,8},{9,1... | collective-permute-start | bytes 3145736 | tf_op jit(solution)/shard_map/ppermute | solution.py:1085
  94.5 1.0 copy-start.15
  99.1 54.7 %collective-permute-start.4 = (bf16[2,2,2,64,2048]{4,3,2,1,0:T(8,128)(2,1)}, bf16[2,2,2,64,2048]{4,3,2,1,0:T(8,128)(2,1)}, u32[]{:S(2)}, u32[]{:S(2)}) collective-permute-start(bf16[2,2,2,64,2048]{4,3,2,1,0:T(8,128)(2,1)} %pile.5.refs_1_.refs_2_.refs_5_), channel_id=1, source_target_pairs={{0,1},{1,0},{2,3},{3,2},{4,5},{5,4},{6,7},{7,6},{8,9},{9,8},{10,11... | collective-permute-start | bytes 6291464 | tf_op jit(solution)/shard_map/ppermute | solution.py:1085
  99.1 99.2 %collective-permute-start.3 = (bf16[2,2,2,64,2048]{4,3,2,1,0:T(8,128)(2,1)}, bf16[2,2,2,64,2048]{4,3,2,1,0:T(8,128)(2,1)S(1)}, u32[]{:S(2)}, u32[]{:S(2)}) collective-permute-start(bf16[2,2,2,64,2048]{4,3,2,1,0:T(8,128)(2,1)} %pile.5.refs_1_.refs_2_.refs_5_), channel_id=1, source_target_pairs={{0,2},{2,0},{1,3},{3,1},{4,6},{6,4},{5,7},{7,5},{8,10},{10,8},{9,1... | collective-permute-start | bytes 6291464 | tf_op jit(solution)/shard_map/ppermute | solution.py:1085
  153.8 1.1 copy-start.33
  154.6 43.7 %collective-permute-start.5 = (bf16[2,2,2,64,2048]{4,3,2,1,0:T(8,128)(2,1)}, bf16[2,2,2,64,2048]{4,3,2,1,0:T(8,128)(2,1)}, u32[]{:S(2)}, u32[]{:S(2)}) collective-permute-start(bf16[2,2,2,64,2048]{4,3,2,1,0:T(8,128)(2,1)} %get-tuple-element.108.refs_4_.refs_5_), channel_id=1, source_target_pairs={{0,2},{2,0},{1,3},{3,1},{4,6},{6,4},{5,7},{7,5},{8,10},{10,8},{9,1... | collective-permute-start | bytes 6291464 | tf_op jit(solution)/shard_map/ppermute | solution.py:1085
  198.3 1.4 copy-start.2
  279.0 30.0 %collective-permute-start.6 = (bf16[2,2,2,64,2048]{4,3,2,1,0:T(8,128)(2,1)}, bf16[2,2,2,64,2048]{4,3,2,1,0:T(8,128)(2,1)}, u32[]{:S(2)}, u32[]{:S(2)}) collective-permute-start(bf16[2,2,2,64,2048]{4,3,2,1,0:T(8,128)(2,1)} %get-tuple-element.122), channel_id=1, source_target_pairs={{0,2},{2,0},{1,3},{3,1},{4,6},{6,4},{5,7},{7,5},{8,10},{10,8},{9,1... | collective-permute-start | bytes 6291464 | tf_op jit(solution)/shard_map/ppermute | solution.py:1085
  279.3 29.7 %collective-permute-start.7 = (bf16[2,2,2,64,2048]{4,3,2,1,0:T(8,128)(2,1)}, bf16[2,2,2,64,2048]{4,3,2,1,0:T(8,128)(2,1)S(1)}, u32[]{:S(2)}, u32[]{:S(2)}) collective-permute-start(bf16[2,2,2,64,2048]{4,3,2,1,0:T(8,128)(2,1)} %get-tuple-element.124), channel_id=1, source_target_pairs={{0,2},{2,0},{1,3},{3,1},{4,6},{6,4},{5,7},{7,5},{8,10},{10,8},{9,1... | collective-permute-start | bytes 6291464 | tf_op jit(solution)/shard_map/ppermute | solution.py:1085
  309.0 1.4 copy-start.6
  316.1 13.2 %collective-permute-start.8 = (bf16[2,2,2,64,2048]{4,3,2,1,0:T(8,128)(2,1)}, bf16[2,2,2,64,2048]{4,3,2,1,0:T(8,128)(2,1)S(1)}, u32[]{:S(2)}, u32[]{:S(2)}) collective-permute-start(bf16[2,2,2,64,2048]{4,3,2,1,0:T(8,128)(2,1)} %get-tuple-element.137), channel_id=1, source_target_pairs={{0,2},{2,0},{1,3},{3,1},{4,6},{6,4},{5,7},{7,5},{8,10},{10,8},{9,1... | collective-permute-start | bytes 6291464 | tf_op jit(solution)/shard_map/ppermute | solution.py:1085
  316.3 13.0 %collective-permute-start.11 = (bf16[2,2,2,64,2048]{4,3,2,1,0:T(8,128)(2,1)}, bf16[2,2,2,64,2048]{4,3,2,1,0:T(8,128)(2,1)}, u32[]{:S(2)}, u32[]{:S(2)}) collective-permute-start(bf16[2,2,2,64,2048]{4,3,2,1,0:T(8,128)(2,1)} %get-tuple-element.142), channel_id=1, source_target_pairs={{0,2},{2,0},{1,3},{3,1},{4,6},{6,4},{5,7},{7,5},{8,10},{10,8},{9,1... | collective-permute-start | bytes 6291464 | tf_op jit(solution)/shard_map/ppermute | solution.py:1085
  325.7 54.1 %collective-permute-start.9 = (bf16[2,2,2,64,2048]{4,3,2,1,0:T(8,128)(2,1)}, bf16[2,2,2,64,2048]{4,3,2,1,0:T(8,128)(2,1)}, u32[]{:S(2)}, u32[]{:S(2)}) collective-permute-start(bf16[2,2,2,64,2048]{4,3,2,1,0:T(8,128)(2,1)} %get-tuple-element.138), channel_id=1, source_target_pairs={{0,1},{1,0},{2,3},{3,2},{4,5},{5,4},{6,7},{7,6},{8,9},{9,8},{10,11... | collective-permute-start | bytes 6291464 | tf_op jit(solution)/shard_map/ppermute | solution.py:1085
  327.5 50.9 %collective-permute-start.10 = (bf16[2,2,64,2048]{3,2,1,0:T(8,128)(2,1)}, bf16[2,2,64,2048]{3,2,1,0:T(8,128)(2,1)S(1)}, u32[]{:S(2)}, u32[]{:S(2)}) collective-permute-start(bf16[2,2,64,2048]{3,2,1,0:T(8,128)(2,1)} %get-tuple-element.139), channel_id=1, source_target_pairs={{0,4},{4,0},{1,5},{5,1},{2,6},{6,2},{3,7},{7,3},{8,12},{12,8},{9,1... | collective-permute-start | bytes 3145736 | tf_op jit(solution)/shard_map/ppermute | solution.py:1085
  329.3 1.3 copy-start.3
  334.1 46.5 %collective-permute-start.12 = (bf16[2,2,64,2048]{3,2,1,0:T(8,128)(2,1)}, bf16[2,2,64,2048]{3,2,1,0:T(8,128)(2,1)S(1)}, u32[]{:S(2)}, u32[]{:S(2)}) collective-permute-start(bf16[2,2,64,2048]{3,2,1,0:T(8,128)(2,1)} %get-tuple-element.146), channel_id=1, source_target_pairs={{0,4},{4,0},{1,5},{5,1},{2,6},{6,2},{3,7},{7,3},{8,12},{12,8},{9,1... | collective-permute-start | bytes 3145736 | tf_op jit(solution)/shard_map/ppermute | solution.py:1085
  378.4 2.3 copy-start.12
  380.6 1.0 copy-start.7
  386.8 37.4 %collective-permute-start.13 = (bf16[2,2,64,2048]{3,2,1,0:T(8,128)(2,1)}, bf16[2,2,64,2048]{3,2,1,0:T(8,128)(2,1)S(1)}, u32[]{:S(2)}, u32[]{:S(2)}) collective-permute-start(bf16[2,2,64,2048]{3,2,1,0:T(8,128)(2,1)} %get-tuple-element.147), channel_id=1, source_target_pairs={{0,4},{4,0},{1,5},{5,1},{2,6},{6,2},{3,7},{7,3},{8,12},{12,8},{9,1... | collective-permute-start | bytes 3145736 | tf_op jit(solution)/shard_map/ppermute | solution.py:1085
  389.1 35.2 %collective-permute-start.14 = (bf16[2,2,64,2048]{3,2,1,0:T(8,128)(2,1)}, bf16[2,2,64,2048]{3,2,1,0:T(8,128)(2,1)S(1)}, u32[]{:S(2)}, u32[]{:S(2)}) collective-permute-start(bf16[2,2,64,2048]{3,2,1,0:T(8,128)(2,1)} %get-tuple-element.148), channel_id=1, source_target_pairs={{0,1},{1,0},{2,3},{3,2},{4,5},{5,4},{6,7},{7,6},{8,9},{9,8},{10,11... | collective-permute-start | bytes 3145736 | tf_op jit(solution)/shard_map/ppermute | solution.py:1085
  424.2 1.0 copy-start.13
  424.2 1.3 copy-start.14
  432.2 31.7 %collective-permute-start.17 = (bf16[2,64,4096]{2,1,0:T(8,128)(2,1)}, bf16[2,64,4096]{2,1,0:T(8,128)(2,1)S(1)}, u32[]{:S(2)}, u32[]{:S(2)}) collective-permute-start(bf16[2,64,4096]{2,1,0:T(8,128)(2,1)} %get-tuple-element.158), channel_id=1, source_target_pairs={{0,8},{8,0},{16,24},{24,16},{1,9},{9,1},{17,25},{25,17},{2,10},{10... | collective-permute-start | bytes 3145736 | tf_op jit(solution)/shard_map/ppermute | solution.py:1089
  463.3 7.2 %collective-permute-start.15 = (bf16[2,2,2,2,2,64,512]{6,5,4,3,2,1,0:T(8,128)(2,1)}, bf16[2,2,2,2,2,64,512]{6,5,4,3,2,1,0:T(8,128)(2,1)S(1)}, u32[]{:S(2)}, u32[]{:S(2)}) collective-permute-start(bf16[2,2,2,2,2,64,512]{6,5,4,3,2,1,0:T(8,128)(2,1)} %get-tuple-element.154), channel_id=1, source_target_pairs={{0,2},{2,0},{1,3},{3,1},{4,6},{6,4},{5,7},{7,5},{8,10},{10,8},{9,1... | collective-permute-start | bytes 6291464 | tf_op jit(solution)/shard_map/ppermute | solution.py:1085
  463.3 7.5 %collective-permute-start.16 = (bf16[2,2,2,2,2,64,512]{6,5,4,3,2,1,0:T(8,128)(2,1)}, bf16[2,2,2,2,2,64,512]{6,5,4,3,2,1,0:T(8,128)(2,1)}, u32[]{:S(2)}, u32[]{:S(2)}) collective-permute-start(bf16[2,2,2,2,2,64,512]{6,5,4,3,2,1,0:T(8,128)(2,1)} %get-tuple-element.156), channel_id=1, source_target_pairs={{0,2},{2,0},{1,3},{3,1},{4,6},{6,4},{5,7},{7,5},{8,10},{10,8},{9,1... | collective-permute-start | bytes 6291464 | tf_op jit(solution)/shard_map/ppermute | solution.py:1085
  463.9 1.0 copy-start.31
  470.5 1.4 copy-start.1
  471.9 5.6 copy-start.32
  476.4 26.5 %collective-permute-start.18 = (bf16[2,2,2,2,64,512]{5,4,3,2,1,0:T(8,128)(2,1)}, bf16[2,2,2,2,64,512]{5,4,3,2,1,0:T(8,128)(2,1)S(1)}, u32[]{:S(2)}, u32[]{:S(2)}) collective-permute-start(bf16[2,2,2,2,64,512]{5,4,3,2,1,0:T(8,128)(2,1)} %get-tuple-element.160), channel_id=1, source_target_pairs={{0,1},{1,0},{2,3},{3,2},{4,5},{5,4},{6,7},{7,6},{8,9},{9,8},{10,11... | collective-permute-start | bytes 3145736 | tf_op jit(solution)/shard_map/ppermute | solution.py:1085
  477.1 25.8 %collective-permute-start.20 = (bf16[2,2,2,2,64,512]{5,4,3,2,1,0:T(8,128)(2,1)}, bf16[2,2,2,2,64,512]{5,4,3,2,1,0:T(8,128)(2,1)S(1)}, u32[]{:S(2)}, u32[]{:S(2)}) collective-permute-start(bf16[2,2,2,2,64,512]{5,4,3,2,1,0:T(8,128)(2,1)} %get-tuple-element.163), channel_id=1, source_target_pairs={{0,4},{4,0},{1,5},{5,1},{2,6},{6,2},{3,7},{7,3},{8,12},{12,8},{9,1... | collective-permute-start | bytes 3145736 | tf_op jit(solution)/shard_map/ppermute | solution.py:1085
  477.5 25.4 %collective-permute-start.19 = (bf16[64,4096]{1,0:T(8,128)(2,1)S(1)}, bf16[64,4096]{1,0:T(8,128)(2,1)S(1)}, u32[]{:S(2)}, u32[]{:S(2)}) collective-permute-start(bf16[64,4096]{1,0:T(8,128)(2,1)S(1)} %copy-done.32), channel_id=1, source_target_pairs={{0,16},{8,24},{16,0},{24,8},{1,17},{9,25},{17,1},{25,9},{2,18},{10... | collective-permute-start | bytes 1572872 | tf_op jit(solution)/shard_map/ppermute | solution.py:1089
  486.5 16.4 %collective-permute-start.21 = (f32[8,1024]{1,0:T(8,128)}, f32[8,1024]{1,0:T(8,128)S(1)}, u32[]{:S(2)}, u32[]{:S(2)}) collective-permute-start(f32[8,1024]{1,0:T(8,128)} %get-tuple-element.165.refs_8_), channel_id=1, source_target_pairs={{0,2},{2,0},{1,3},{3,1},{4,6},{6,4},{5,7},{7,5},{8,10},{10,8},{9,1... | collective-permute-start | bytes 98312 | tf_op jit(solution)/shard_map/ppermute | solution.py:1085
  502.9 1.1 copy-start.4
  502.9 1.5 copy-start.5
  508.9 15.9 %collective-permute-start.24 = (bf16[2,2,2,2,2,64,512]{6,5,4,3,2,1,0:T(8,128)(2,1)}, bf16[2,2,2,2,2,64,512]{6,5,4,3,2,1,0:T(8,128)(2,1)S(1)}, u32[]{:S(2)}, u32[]{:S(2)}) collective-permute-start(bf16[2,2,2,2,2,64,512]{6,5,4,3,2,1,0:T(8,128)(2,1)} %get-tuple-element.171), channel_id=1, source_target_pairs={{0,2},{2,0},{1,3},{3,1},{4,6},{6,4},{5,7},{7,5},{8,10},{10,8},{9,1... | collective-permute-start | bytes 6291464 | tf_op jit(solution)/shard_map/ppermute | solution.py:1085
  508.9 14.5 %collective-permute-start.22 = (bf16[2,2,2,64,512]{4,3,2,1,0:T(8,128)(2,1)}, bf16[2,2,2,64,512]{4,3,2,1,0:T(8,128)(2,1)S(1)}, u32[]{:S(2)}, u32[]{:S(2)}) collective-permute-start(bf16[2,2,2,64,512]{4,3,2,1,0:T(8,128)(2,1)} %get-tuple-element.168), channel_id=1, source_target_pairs={{0,4},{4,0},{1,5},{5,1},{2,6},{6,2},{3,7},{7,3},{8,12},{12,8},{9,1... | collective-permute-start | bytes 1572872 | tf_op jit(solution)/shard_map/ppermute | solution.py:1085
  510.6 14.2 %collective-permute-start.23 = (bf16[2,2,2,64,512]{4,3,2,1,0:T(8,128)(2,1)}, bf16[2,2,2,64,512]{4,3,2,1,0:T(8,128)(2,1)S(1)}, u32[]{:S(2)}, u32[]{:S(2)}) collective-permute-start(bf16[2,2,2,64,512]{4,3,2,1,0:T(8,128)(2,1)} %get-tuple-element.169), channel_id=1, source_target_pairs={{0,1},{1,0},{2,3},{3,2},{4,5},{5,4},{6,7},{7,6},{8,9},{9,8},{10,11... | collective-permute-start | bytes 1572872 | tf_op jit(solution)/shard_map/ppermute | solution.py:1085
  511.9 9.6 %collective-permute-start.25 = (f32[8,1024]{1,0:T(8,128)}, f32[8,1024]{1,0:T(8,128)S(1)}, u32[]{:S(2)}, u32[]{:S(2)}) collective-permute-start(f32[8,1024]{1,0:T(8,128)} %get-tuple-element.172.refs_20_), channel_id=1, source_target_pairs={{0,8},{8,0},{16,24},{24,16},{1,9},{9,1},{17,25},{25,17},{2,10},{10... | collective-permute-start | bytes 98312 | tf_op jit(solution)/shard_map/ppermute | solution.py:1089
  521.5 3.4 copy-start.27
  523.4 1.4 copy-start.8
  524.8 1.5 copy-start
  531.6 3.5 copy-start.25
  531.6 13.4 %collective-permute-start.26 = (bf16[2,2,2,64,512]{4,3,2,1,0:T(8,128)(2,1)}, bf16[2,2,2,64,512]{4,3,2,1,0:T(8,128)(2,1)S(1)}, u32[]{:S(2)}, u32[]{:S(2)}) collective-permute-start(bf16[2,2,2,64,512]{4,3,2,1,0:T(8,128)(2,1)} %get-tuple-element.177), channel_id=1, source_target_pairs={{0,1},{1,0},{2,3},{3,2},{4,5},{5,4},{6,7},{7,6},{8,9},{9,8},{10,11... | collective-permute-start | bytes 1572872 | tf_op jit(solution)/shard_map/ppermute | solution.py:1085
  532.9 13.1 %collective-permute-start.27 = (bf16[2,2,2,64,512]{4,3,2,1,0:T(8,128)(2,1)}, bf16[2,2,2,64,512]{4,3,2,1,0:T(8,128)(2,1)S(1)}, u32[]{:S(2)}, u32[]{:S(2)}) collective-permute-start(bf16[2,2,2,64,512]{4,3,2,1,0:T(8,128)(2,1)} %get-tuple-element.178), channel_id=1, source_target_pairs={{0,4},{4,0},{1,5},{5,1},{2,6},{6,2},{3,7},{7,3},{8,12},{12,8},{9,1... | collective-permute-start | bytes 1572872 | tf_op jit(solution)/shard_map/ppermute | solution.py:1085
  533.4 13.8 %collective-permute-start.29 = (bf16[2,64,2048]{2,1,0:T(8,128)(2,1)}, bf16[2,64,2048]{2,1,0:T(8,128)(2,1)S(1)}, u32[]{:S(2)}, u32[]{:S(2)}) collective-permute-start(bf16[2,64,2048]{2,1,0:T(8,128)(2,1)} %get-tuple-element.181), channel_id=1, source_target_pairs={{0,8},{8,0},{16,24},{24,16},{1,9},{9,1},{17,25},{25,17},{2,10},{10... | collective-permute-start | bytes 1572872 | tf_op jit(solution)/shard_map/ppermute | solution.py:1089
  535.1 9.9 %collective-permute-start.28 = (f32[8,1024]{1,0:T(8,128)S(1)}, f32[8,1024]{1,0:T(8,128)S(1)}, u32[]{:S(2)}, u32[]{:S(2)}) collective-permute-start(f32[8,1024]{1,0:T(8,128)S(1)} %copy-done.25), channel_id=1, source_target_pairs={{0,16},{8,24},{16,0},{24,8},{1,17},{9,25},{17,1},{25,9},{2,18},{10... | collective-permute-start | bytes 98312 | tf_op jit(solution)/shard_map/ppermute | solution.py:1089
  545.0 2.2 copy-start.29
  545.0 2.2 copy-start.10
  546.0 1.2 copy-start.11
  551.7 8.2 %collective-permute-start.30 = (bf16[2,2,64,512]{3,2,1,0:T(8,128)(2,1)}, bf16[2,2,64,512]{3,2,1,0:T(8,128)(2,1)S(1)}, u32[]{:S(2)}, u32[]{:S(2)}) collective-permute-start(bf16[2,2,64,512]{3,2,1,0:T(8,128)(2,1)} %get-tuple-element.182), channel_id=1, source_target_pairs={{0,4},{4,0},{1,5},{5,1},{2,6},{6,2},{3,7},{7,3},{8,12},{12,8},{9,1... | collective-permute-start | bytes 786440 | tf_op jit(solution)/shard_map/ppermute | solution.py:1085
  553.0 6.9 %collective-permute-start.31 = (bf16[2,2,64,512]{3,2,1,0:T(8,128)(2,1)}, bf16[2,2,64,512]{3,2,1,0:T(8,128)(2,1)S(1)}, u32[]{:S(2)}, u32[]{:S(2)}) collective-permute-start(bf16[2,2,64,512]{3,2,1,0:T(8,128)(2,1)} %get-tuple-element.183), channel_id=1, source_target_pairs={{0,1},{1,0},{2,3},{3,2},{4,5},{5,4},{6,7},{7,6},{8,9},{9,8},{10,11... | collective-permute-start | bytes 786440 | tf_op jit(solution)/shard_map/ppermute | solution.py:1085
  554.2 5.7 collective-permute-start.32
  557.9 8.7 %copy-start.16 = (f32[64,4096]{1,0:T(8,128)S(1)}, f32[64,4096]{1,0:T(8,128)}, u32[]{:S(2)}) copy-start(f32[64,4096]{1,0:T(8,128)} %get-tuple-element.194) | copy-start | bytes 3145732
  557.9 12.1 %collective-permute-start.34 = (bf16[64,2048]{1,0:T(8,128)(2,1)}, bf16[64,2048]{1,0:T(8,128)(2,1)S(1)}, u32[]{:S(2)}, u32[]{:S(2)}) collective-permute-start(bf16[64,2048]{1,0:T(8,128)(2,1)} %get-tuple-element.188), channel_id=1, source_target_pairs={{0,16},{8,24},{16,0},{24,8},{1,17},{9,25},{17,1},{25,9},{2,18},{10... | collective-permute-start | bytes 786440 | tf_op jit(solution)/shard_map/ppermute | solution.py:1089
  564.5 5.5 collective-permute-start.35
  565.4 8.8 %collective-permute-start.33 = (bf16[2,64,1024]{2,1,0:T(8,128)(2,1)}, bf16[2,64,1024]{2,1,0:T(8,128)(2,1)S(1)}, u32[]{:S(2)}, u32[]{:S(2)}) collective-permute-start(bf16[2,64,1024]{2,1,0:T(8,128)(2,1)} %get-tuple-element.186), channel_id=1, source_target_pairs={{0,8},{8,0},{16,24},{24,16},{1,9},{9,1},{17,25},{25,17},{2,10},{10... | collective-permute-start | bytes 786440 | tf_op jit(solution)/shard_map/ppermute | solution.py:1089
  570.0 4.2 copy-start.23
  570.0 4.2 copy-start.30
  578.6 7.9 %collective-permute-start.36 = (bf16[64,1024]{1,0:T(8,128)(2,1)}, bf16[64,1024]{1,0:T(8,128)(2,1)S(1)}, u32[]{:S(2)}, u32[]{:S(2)}) collective-permute-start(bf16[64,1024]{1,0:T(8,128)(2,1)} %get-tuple-element.191), channel_id=1, source_target_pairs={{0,16},{8,24},{16,0},{24,8},{1,17},{9,25},{17,1},{25,9},{2,18},{10... | collective-permute-start | bytes 393224 | tf_op jit(solution)/shard_map/ppermute | solution.py:1089
  (10 other events, 7.4 us)
Sparse Core Ops, SparseCore 0:
  11.4 118.1 all-gather.6
  132.6 79.0 all-gather.8
  325.9 61.8 all-gather.10
